TPU v7x, 256 devices: a whole 4x4x8 slice. The times are simulated.
256 devices in a mesh: gx: 32 (over x, y, core), gy: 8 (over z).
Axes of the slice: x: 4, y: 4, z: 8, core: 2. Of those that a mesh axis runs over, the one named last changes fastest.
Arguments:
- sens_temp: float32 [48, 512, 1024], P(None, 'gx', 'gy'), may hold values from -8.5 to 8.5
- sens_salt: float32 [48, 512, 1024], P(None, 'gx', 'gy'), may hold values from -8.5 to 8.5
- sens_surface: float32 [512, 1024], P('gx', 'gy'), may hold values from -8.5 to 8.5
- flow_east: float32 [48, 512, 1024], P(None, 'gx', 'gy'), may hold values from -4 to 4
- flow_north: float32 [48, 512, 1024], P(None, 'gx', 'gy'), may hold values from -4 to 4
- mix_profile: float32 [48], replicated, may hold values from 0.2 to 5
- thermal_weight: float32 [48], replicated, may hold values from 0.1 to 0.5
- haline_weight: float32 [48], replicated, may hold values from 0.1 to 0.5
- surface_diag: float32 [512, 1024], P('gx', 'gy'), may hold values from 0.05 to 1
- land_mask: int32 [48, 512, 1024], P(None, 'gx', 'gy'), may hold values 0 or 1
- bottom_level: int32 [512, 1024], P('gx', 'gy'), may hold values from 24 to 48
Outputs:
- start_temp: float32 [48, 512, 1024], P(None, 'gx', 'gy')
- start_salt: float32 [48, 512, 1024], P(None, 'gx', 'gy')
- start_surface: float32 [512, 1024], P('gx', 'gy')
All inputs are finite; a program needn't handle non-finite values. No bound on the sum of `land_mask` on one device may be relied on, other than what follows from the above.
Results may differ from a plain program's by a relative error of at most 0.0001.
Values sent between devices are 32-bit elements; how exact they have to be, the bound alone decides.
No kernel may reach another device: no remote copies, remote signals or barrier semaphores. Data moves between devices by JAX's collectives and lax.ppermute only.
A program may use at most 128 MiB of HBM per device.

v0:
```python
import jax
import jax.numpy as jnp
from jax import lax
from jax.sharding import PartitionSpec as P

CG_ITERS = 4
STEPS = 2


diffusion_coef = 0.5
hyper_coef = 0.1
step_scale = 0.1


def with_halo(cells, sides, width):
    for axis, dim in sides:
        count = lax.axis_size(axis)
        head = lax.slice_in_dim(cells, 0, width, axis=dim)
        tail = lax.slice_in_dim(cells, cells.shape[dim] - width, cells.shape[dim], axis=dim)
        cells = jnp.concatenate(
            [
                lax.ppermute(tail, axis, [(i, (i + 1) % count) for i in range(count)]),
                cells,
                lax.ppermute(head, axis, [((i + 1) % count, i) for i in range(count)]),
            ],
            axis=dim,
        )
    return cells


def passed_along(x, axis, by):
    length = lax.axis_size(axis)
    return lax.ppermute(x, axis, [(i, (i + by) % length) for i in range(length)])


def passed_along_2(x, axis, by):
    length = lax.axis_size(axis)
    pairs = [(i, i + by) for i in range(length) if 0 <= i + by < length]
    return lax.ppermute(x, axis, pairs)


def pad_cells(array_in, margin):
    widths = [(0, 0)] * (array_in.ndim - 2) + [(margin, margin), (margin, margin)]
    return jnp.pad(array_in, widths)


def displace(array_in, axis_index, offset):
    extent = array_in.shape[axis_index]
    widths = [(0, 0)] * array_in.ndim
    widths[axis_index] = (1, 1)
    padded = jnp.pad(array_in, widths)
    return lax.slice_in_dim(padded, 1 - offset, 1 - offset + extent, axis=axis_index)


def laplacian(padded, wet_padded):
    center = padded[..., 1:-1, 1:-1]
    summed = wet_padded[..., 2:, 1:-1] * (padded[..., 2:, 1:-1] - center)
    summed = summed + wet_padded[..., :-2, 1:-1] * (padded[..., :-2, 1:-1] - center)
    summed = summed + wet_padded[..., 1:-1, 2:] * (padded[..., 1:-1, 2:] - center)
    summed = summed + wet_padded[..., 1:-1, :-2] * (padded[..., 1:-1, :-2] - center)
    return wet_padded[..., 1:-1, 1:-1] * summed


def vertical_solve(right_side, couple):
    levels = right_side.shape[-3]
    no_coupling = jnp.zeros_like(couple[0])
    ratios = []
    partial_values = []
    for level_index in range(levels):
        coupling_up = couple[level_index - 1] if level_index > 0 else no_coupling
        coupling_down = couple[level_index] if level_index < levels - 1 else no_coupling
        pivot_value = 1.0 + coupling_up + coupling_down
        source = right_side[..., level_index, :, :]
        if level_index > 0:
            pivot_value = pivot_value - coupling_up * ratios[-1]
            source = source + coupling_up * partial_values[-1]
        ratios.append(coupling_down / pivot_value)
        partial_values.append(source / pivot_value)
    solved = [partial_values[-1]]
    for level_index in range(levels - 2, -1, -1):
        solved.append(partial_values[level_index] + ratios[level_index] * solved[-1])
    return jnp.stack(solved[::-1], axis=-3)


def squares(residual):
    return lax.psum(jnp.sum(residual * residual), ("gx", "gy"))


def per_device(
    sens_temp,
    sens_salt,
    sens_surface,
    flow_east,
    flow_north,
    mix_profile,
    thermal_weight,
    haline_weight,
    surface_diag,
    land_mask,
    bottom_level,
):
    levels, cells_lon, cells_lat = sens_temp.shape
    level_ids = lax.broadcasted_iota(jnp.int32, sens_temp.shape, 0)
    wet_cells = land_mask.astype(jnp.float32) * (level_ids < bottom_level[None, :, :]).astype(
        jnp.float32
    )
    column_depth = jnp.sum(wet_cells, axis=0) / levels
    lat_position = lax.broadcasted_iota(jnp.int32, (cells_lat + 4,), 0)
    row_index = lax.axis_index("gy")
    last_index = lax.axis_size("gy") - 1
    dropped = (lat_position < 2) & (row_index == 0) | (lat_position >= cells_lat + 2) & (
        row_index == last_index
    )
    keep_rows = jnp.where(dropped, 0.0, 1.0).astype(jnp.float32)
    stacked = jnp.concatenate([wet_cells, column_depth[None]], axis=0)
    padded_fields = with_halo(stacked, (("gx", 1), ("gy", 2)), 2) * keep_rows
    wet_padded = padded_fields[:levels]
    depth_padded = padded_fields[levels]
    depth_cycle = depth_padded[1:-1, 1:-1]
    face_east = jnp.minimum(depth_cycle[1:-1, 1:-1], depth_cycle[2:, 1:-1])
    face_west = jnp.minimum(depth_cycle[:-2, 1:-1], depth_cycle[1:-1, 1:-1])
    face_north = jnp.minimum(depth_cycle[1:-1, 1:-1], depth_cycle[1:-1, 2:])
    face_south = jnp.minimum(depth_cycle[1:-1, :-2], depth_cycle[1:-1, 1:-1])
    wet_cycle = wet_padded[:, 1:-1, 1:-1]
    diagonal = wet_cells * (
        wet_cycle[:, 2:, 1:-1] * (diffusion_coef - 0.5 * flow_east)
        + wet_cycle[:, :-2, 1:-1] * (diffusion_coef + 0.5 * flow_east)
        + wet_cycle[:, 1:-1, 2:] * (diffusion_coef - 0.5 * flow_north)
        + wet_cycle[:, 1:-1, :-2] * (diffusion_coef + 0.5 * flow_north)
    )
    couple = mix_profile[:-1, None, None] * wet_cells[:-1] * wet_cells[1:]
    tracers = jnp.stack([sens_temp, sens_salt])
    surface = sens_surface
    for repeat in range(STEPS):
        combined = surface + jnp.sum(
            wet_cells
            * (
                thermal_weight[:, None, None] * tracers[0]
                - haline_weight[:, None, None] * tracers[1]
            ),
            axis=0,
        )
        solution = jnp.zeros_like(combined)
        residual = combined
        surface_direction = combined
        norm_now = squares(residual)
        for iteration in range(CG_ITERS):
            padded = with_halo(surface_direction, (("gx", 0), ("gy", 1)), 1)
            applied = (
                surface_diag * surface_direction
                + face_east * (surface_direction - padded[2:, 1:-1])
                + face_west * (surface_direction - padded[:-2, 1:-1])
                + face_north * (surface_direction - padded[1:-1, 2:])
                + face_south * (surface_direction - padded[1:-1, :-2])
            )
            step_length = norm_now / lax.psum(jnp.sum(surface_direction * applied), ("gx", "gy"))
            solution = solution + step_length * surface_direction
            if iteration + 1 < CG_ITERS:
                residual = residual - step_length * applied
                norm_next = squares(residual)
                surface_direction = residual + norm_next / norm_now * surface_direction
                norm_now = norm_next
        surface = surface_diag * solution
        adjusted = jnp.stack(
            [
                tracers[0] + thermal_weight[:, None, None] * wet_cells * solution[None, :, :],
                tracers[1] - haline_weight[:, None, None] * wet_cells * solution[None, :, :],
            ]
        )
        mixed_tracers = vertical_solve(adjusted, couple)
        widened = pad_cells(mixed_tracers, 2)
        wet_wide = pad_cells(wet_padded, 1)
        first_lap = laplacian(pad_cells(widened, 1), wet_wide)
        second_lap = laplacian(pad_cells(first_lap, 1), wet_wide)
        east_flux = wet_cells * flow_east
        north_flux = wet_cells * flow_north
        east_out = pad_cells((diffusion_coef * wet_cells - 0.5 * east_flux) * mixed_tracers, 2)
        west_out = pad_cells((diffusion_coef * wet_cells + 0.5 * east_flux) * mixed_tracers, 2)
        north_out = pad_cells((diffusion_coef * wet_cells - 0.5 * north_flux) * mixed_tracers, 2)
        south_out = pad_cells((diffusion_coef * wet_cells + 0.5 * north_flux) * mixed_tracers, 2)
        lon_axis = east_out.ndim - 2
        lat_axis = east_out.ndim - 1
        incoming = (
            displace(east_out, lon_axis, 1)
            + displace(west_out, lon_axis, -1)
            + displace(north_out, lat_axis, 1)
            + displace(south_out, lat_axis, -1)
        )
        scattered = (
            wet_padded * incoming - pad_cells(diagonal * mixed_tracers, 2) - hyper_coef * second_lap
        )
        from_east = passed_along(scattered[..., :2, :], "gx", -1)
        from_west = passed_along(scattered[..., -2:, :], "gx", 1)
        middle = scattered[..., 2:-2, :]
        middle = middle.at[..., :2, :].add(from_west).at[..., -2:, :].add(from_east)
        from_north = passed_along_2(middle[..., :2], "gy", -1)
        from_south = passed_along_2(middle[..., -2:], "gy", 1)
        interior = middle[..., 2:-2]
        tracers = mixed_tracers + step_scale * interior.at[..., :2].add(from_south).at[
            ..., -2:
        ].add(from_north)
    return (tracers[0], tracers[1], surface)


def solution(mesh):
    in_specs = (
        P(None, "gx", "gy"),
        P(None, "gx", "gy"),
        P("gx", "gy"),
        P(None, "gx", "gy"),
        P(None, "gx", "gy"),
        P(),
        P(),
        P(),
        P("gx", "gy"),
        P(None, "gx", "gy"),
        P("gx", "gy"),
    )
    out_specs = (P(None, "gx", "gy"), P(None, "gx", "gy"), P("gx", "gy"))
    return jax.shard_map(
        per_device, mesh=mesh, in_specs=in_specs, out_specs=out_specs, check_vma=False
    )
```

profile of v0, /device:TPU:1, one launch (start us, length us, event | category | flops | bytes accessed | tf_op | source)
XLA Modules:
  0.0 1347.6 jit_solution(12942970393530767192)
XLA Ops:
  0.7 2.0 multiply_subtract_fusion.1
  4.0 2.8 collective-permute-start.5
  8.6 4.0 collective-permute-start.1
  28.6 3.9 collective-permute-start.3
  32.6 2.7 collective-permute-start.6
  37.1 1.6 maximum_multiply_fusion
  40.5 77.5 %all-reduce.26 = (f32[]{:T(128)}, f32[]{:T(128)}) all-reduce(f32[]{:T(128)} %get-tuple-element.104, f32[]{:T(128)} %get-tuple-element.103), channel_id=1, replica_groups=mesh['gx'=32,'gy'=8] {'gx','gy'}, use_global_device_ids=true, to_apply=%region_2.3 | all-reduce | flops 2 | bytes 16 | tf_op jit(solution)/shard_map/psum | solution.py:86
  120.6 74.5 %psum.114 = f32[]{:T(128)} all-reduce(f32[]{:T(128)} %multiply_reduce_fusion.13), channel_id=1, replica_groups=mesh['gx'=32,'gy'=8] {'gx','gy'}, use_global_device_ids=true, to_apply=%region_7.8 | all-reduce | flops 1 | bytes 8 | tf_op jit(solution)/shard_map/psum | solution.py:86
  196.5 2.2 collective-permute-start.9
  199.6 2.0 collective-permute-done.8
  204.2 2.1 collective-permute-done.11
  207.1 77.9 %psum.115 = f32[]{:T(128)} all-reduce(f32[]{:T(128)} %get-tuple-element.330), channel_id=1, replica_groups=mesh['gx'=32,'gy'=8] {'gx','gy'}, use_global_device_ids=true, to_apply=%region_9.10 | all-reduce | flops 1 | bytes 8 | tf_op jit(solution)/shard_map/psum | solution.py:156
  287.0 73.4 %psum.116 = f32[]{:T(128)} all-reduce(f32[]{:T(128)} %get-tuple-element.328), channel_id=1, replica_groups=mesh['gx'=32,'gy'=8] {'gx','gy'}, use_global_device_ids=true, to_apply=%region_11.12 | all-reduce | flops 1 | bytes 8 | tf_op jit(solution)/shard_map/psum | solution.py:86
  363.5 2.2 collective-permute-done.12
  368.3 2.2 collective-permute-done.15
  371.2 78.5 %psum.117 = f32[]{:T(128)} all-reduce(f32[]{:T(128)} %get-tuple-element.326), channel_id=1, replica_groups=mesh['gx'=32,'gy'=8] {'gx','gy'}, use_global_device_ids=true, to_apply=%region_13.14 | all-reduce | flops 1 | bytes 8 | tf_op jit(solution)/shard_map/psum | solution.py:156
  452.3 73.4 %psum.118 = f32[]{:T(128)} all-reduce(f32[]{:T(128)} %multiply_reduce_fusion.9), channel_id=1, replica_groups=mesh['gx'=32,'gy'=8] {'gx','gy'}, use_global_device_ids=true, to_apply=%region_15.16 | all-reduce | flops 1 | bytes 8 | tf_op jit(solution)/shard_map/psum | solution.py:86
  533.6 2.3 collective-permute-done.19
  536.8 2.5 pad_slice_fusion.203
  539.3 78.5 %psum.119 = f32[]{:T(128)} all-reduce(f32[]{:T(128)} %fusion.520), channel_id=1, replica_groups=mesh['gx'=32,'gy'=8] {'gx','gy'}, use_global_device_ids=true, to_apply=%region_17.18 | all-reduce | flops 1 | bytes 8 | tf_op jit(solution)/shard_map/psum | solution.py:156
  620.3 3.7 fusion.40
  624.4 1.5 fusion.366
  626.2 2.0 constant_dynamic-update-slice_fusion.47
  631.8 2.6 fusion.4
  634.4 5.0 fusion.25
  642.5 2.7 collective-permute-done.21
  645.4 2.0 fusion.716
  647.4 2.2 copy.339
  649.6 4.5 collective-permute-start.22
  654.0 2.2 copy.342
  657.5 2.6 slice.1707
  660.1 2.2 copy.340
  663.7 2.3 copy.341
  666.0 4.8 scatter-add.30
  670.8 2.3 slice.1710
  673.0 2.2 copy.343
  676.6 2.3 copy.344
  678.9 16.4 %scatter-add.31 = f32[2,48,16,128]{3,2,0,1:T(8,128)} dynamic-update-slice(f32[2,48,16,128]{3,2,0,1:T(8,128)} %scatter-add.30, f32[2,48,16,2]{3,2,0,1:T(8,128)} %copy.344, s32[]{:T(128)} %constant.206.clone.1, s32[]{:T(128)} %constant.206.clone.1, s32[]{:T(128)} %constant.206.clone.1, s32[]{:T(128)} %constant.213.clone.1) | dynamic-update-slice | bytes 24580 | tf_op jit(solution)/shard_map/scatter-add | solution.py:201
  699.6 4.6 collective-permute-start.24
  705.0 2.4 collective-permute-start.26
  708.8 2.4 collective-permute-done.27
  712.0 81.1 %all-reduce.25 = (f32[]{:T(128)}, f32[]{:T(128)}) all-reduce(f32[]{:T(128)} %get-tuple-element.102, f32[]{:T(128)} %get-tuple-element.101), channel_id=1, replica_groups=mesh['gx'=32,'gy'=8] {'gx','gy'}, use_global_device_ids=true, to_apply=%region_20.21 | all-reduce | flops 2 | bytes 16 | tf_op jit(solution)/shard_map/psum | solution.py:86
  794.9 73.6 %psum.122 = f32[]{:T(128)} all-reduce(f32[]{:T(128)} %multiply_reduce_fusion.6), channel_id=1, replica_groups=mesh['gx'=32,'gy'=8] {'gx','gy'}, use_global_device_ids=true, to_apply=%region_24.25 | all-reduce | flops 1 | bytes 8 | tf_op jit(solution)/shard_map/psum | solution.py:86
  871.2 2.2 collective-permute-done.28
  876.4 1.9 collective-permute-done.31
  879.8 79.3 %psum.123 = f32[]{:T(128)} all-reduce(f32[]{:T(128)} %get-tuple-element.184), channel_id=1, replica_groups=mesh['gx'=32,'gy'=8] {'gx','gy'}, use_global_device_ids=true, to_apply=%region_26.27 | all-reduce | flops 1 | bytes 8 | tf_op jit(solution)/shard_map/psum | solution.py:156
  961.0 73.3 %psum.124 = f32[]{:T(128)} all-reduce(f32[]{:T(128)} %get-tuple-element.182), channel_id=1, replica_groups=mesh['gx'=32,'gy'=8] {'gx','gy'}, use_global_device_ids=true, to_apply=%region_28.29 | all-reduce | flops 1 | bytes 8 | tf_op jit(solution)/shard_map/psum | solution.py:86
  1037.5 2.2 collective-permute-done.32
  1042.4 2.2 collective-permute-done.35
  1046.0 78.5 %psum.125 = f32[]{:T(128)} all-reduce(f32[]{:T(128)} %get-tuple-element.180), channel_id=1, replica_groups=mesh['gx'=32,'gy'=8] {'gx','gy'}, use_global_device_ids=true, to_apply=%region_30.31 | all-reduce | flops 1 | bytes 8 | tf_op jit(solution)/shard_map/psum | solution.py:156
  1126.4 73.3 %psum.126 = f32[]{:T(128)} all-reduce(f32[]{:T(128)} %multiply_reduce_fusion.2), channel_id=1, replica_groups=mesh['gx'=32,'gy'=8] {'gx','gy'}, use_global_device_ids=true, to_apply=%region_32.33 | all-reduce | flops 1 | bytes 8 | tf_op jit(solution)/shard_map/psum | solution.py:86
  1202.8 2.2 collective-permute-done.36
  1207.7 2.2 collective-permute-done.39
  1211.3 78.6 %psum.127 = f32[]{:T(128)} all-reduce(f32[]{:T(128)} %fusion.470), channel_id=1, replica_groups=mesh['gx'=32,'gy'=8] {'gx','gy'}, use_global_device_ids=true, to_apply=%region_34.35 | all-reduce | flops 1 | bytes 8 | tf_op jit(solution)/shard_map/psum | solution.py:156
  1295.4 2.3 constant_dynamic-update-slice_fusion.95
  1301.0 2.6 fusion.12
  1303.7 5.0 fusion.19
  1311.8 2.6 collective-permute-done.41
  1314.5 1.7 fusion.715
  1316.2 1.6 copy.460
  1317.8 3.7 collective-permute-start.42
  1323.7 1.6 copy.461
  1326.0 3.0 scatter-add.36
  1330.5 15.8 %scatter-add.39 = f32[2,48,16,128]{3,2,0,1:T(8,128)S(1)} dynamic-update-slice(f32[2,48,16,128]{3,2,0,1:T(8,128)S(1)} %scatter-add.36, f32[2,48,16,2]{3,2,0,1:T(8,128)S(1)} %copy.465, s32[]{:T(128)} %constant.206.clone.1, s32[]{:T(128)} %constant.206.clone.1, s32[]{:T(128)} %constant.206.clone.1, s32[]{:T(128)} %constant.213.clone.1) | dynamic-update-slice | bytes 24580 | tf_op jit(solution)/shard_map/scatter-add | solution.py:201
  (714 shorter events, 95.5 us)
Async XLA Ops:
  4.0 22.7 %collective-permute-start.5 = (f32[1,128]{1,0:T(1,128)S(1)}, f32[1,128]{1,0:T(1,128)S(1)}, u32[]{:S(2)}, u32[]{:S(2)}) collective-permute-start(f32[1,128]{1,0:T(1,128)S(1)} %get-tuple-element.486), channel_id=1, source_target_pairs={{0,8},{8,16},{16,24},{24,32},{32,40},{40,48},{48,56},{56,64},{64,7... | collective-permute-start | bytes 1544 | tf_op jit(solution)/shard_map/ppermute | solution.py:22
  6.7 20.0 %collective-permute-start.4 = (f32[1,128]{1,0:T(1,128)S(1)}, f32[1,128]{1,0:T(1,128)}, u32[]{:S(2)}, u32[]{:S(2)}) collective-permute-start(f32[1,128]{1,0:T(1,128)S(1)} %get-tuple-element.487), channel_id=1, source_target_pairs={{8,0},{16,8},{24,16},{32,24},{40,32},{48,40},{56,48},{64,56},{72,6... | collective-permute-start | bytes 1544 | tf_op jit(solution)/shard_map/ppermute | solution.py:24
  7.4 20.0 %collective-permute-start = (f32[49,2,128]{2,1,0:T(2,128)S(1)}, f32[49,2,128]{2,1,0:T(2,128)S(1)}, u32[]{:S(2)}, u32[]{:S(2)}) collective-permute-start(f32[49,2,128]{2,1,0:T(2,128)S(1)} %get-tuple-element.374), channel_id=1, source_target_pairs={{0,8},{8,16},{16,24},{24,32},{32,40},{40,48},{48,56},{56,64},{64,7... | collective-permute-start | bytes 150536 | tf_op jit(solution)/shard_map/ppermute | solution.py:22
  8.6 18.9 %collective-permute-start.1 = (f32[49,2,128]{2,1,0:T(2,128)S(1)}, f32[49,2,128]{2,1,0:T(2,128)S(1)}, u32[]{:S(2)}, u32[]{:S(2)}) collective-permute-start(f32[49,2,128]{2,1,0:T(2,128)S(1)} %get-tuple-element.375), channel_id=1, source_target_pairs={{8,0},{16,8},{24,16},{32,24},{40,32},{48,40},{56,48},{64,56},{72,6... | collective-permute-start | bytes 150536 | tf_op jit(solution)/shard_map/ppermute | solution.py:24
  28.6 8.1 collective-permute-start.3
  32.6 3.8 collective-permute-start.2
  32.6 6.1 collective-permute-start.6
  35.3 3.8 collective-permute-start.7
  196.5 3.2 collective-permute-start.9
  198.6 3.0 collective-permute-start.8
  201.7 2.6 collective-permute-start.10
  202.6 3.8 collective-permute-start.11
  361.7 1.8 collective-permute-start.13
  362.7 3.0 collective-permute-start.12
  365.8 2.6 collective-permute-start.14
  366.8 3.8 collective-permute-start.15
  527.0 3.0 collective-permute-start.17
  528.0 3.0 collective-permute-start.16
  531.1 2.6 collective-permute-start.18
  532.0 3.9 collective-permute-start.19
  639.6 2.7 collective-permute-start.20
  640.0 5.2 collective-permute-start.21
  649.6 12.7 collective-permute-start.22
  656.2 19.0 %collective-permute-start.23 = (f32[2,48,16,2]{1,2,3,0:T(8,128)}, f32[2,48,16,2]{1,2,3,0:T(8,128)}, u32[]{:S(2)}, u32[]{:S(2)}) collective-permute-start(f32[2,48,16,2]{1,2,3,0:T(8,128)} %copy.342), channel_id=1, source_target_pairs={{1,0},{2,1},{3,2},{4,3},{5,4},{6,5},{7,6},{9,8},{10,9},{11,10},{12... | collective-permute-start | bytes 36872 | tf_op jit(solution)/shard_map/ppermute | solution.py:39
  697.5 595.7 %copy-start.52 = (f32[1,16,128]{2,1,0:T(8,128)S(1)}, f32[1,16,128]{2,1,0:T(8,128)}, u32[]{:S(2)}) copy-start(f32[1,16,128]{2,1,0:T(8,128)} %copy-done.50) | copy-start | bytes 24580
  697.5 595.7 %copy-start.55 = (f32[1,16,128]{2,1,0:T(8,128)S(1)}, f32[1,16,128]{2,1,0:T(8,128)}, u32[]{:S(2)}) copy-start(f32[1,16,128]{2,1,0:T(8,128)} %copy-done.53) | copy-start | bytes 24580
  697.5 595.7 %copy-start.58 = (f32[1,16,128]{2,1,0:T(8,128)S(1)}, f32[1,16,128]{2,1,0:T(8,128)}, u32[]{:S(2)}) copy-start(f32[1,16,128]{2,1,0:T(8,128)} %copy-done.56) | copy-start | bytes 24580
  697.5 595.7 %copy-start.61 = (f32[1,16,128]{2,1,0:T(8,128)S(1)}, f32[1,16,128]{2,1,0:T(8,128)}, u32[]{:S(2)}) copy-start(f32[1,16,128]{2,1,0:T(8,128)} %copy-done.59) | copy-start | bytes 24580
  697.6 595.7 %copy-start.64 = (f32[1,16,128]{2,1,0:T(8,128)S(1)}, f32[1,16,128]{2,1,0:T(8,128)}, u32[]{:S(2)}) copy-start(f32[1,16,128]{2,1,0:T(8,128)} %copy-done.62) | copy-start | bytes 24580
  697.6 595.7 %copy-start.67 = (f32[1,16,128]{2,1,0:T(8,128)S(1)}, f32[1,16,128]{2,1,0:T(8,128)}, u32[]{:S(2)}) copy-start(f32[1,16,128]{2,1,0:T(8,128)} %copy-done.65) | copy-start | bytes 24580
  697.6 595.7 %copy-start.70 = (f32[1,16,128]{2,1,0:T(8,128)S(1)}, f32[1,16,128]{2,1,0:T(8,128)}, u32[]{:S(2)}) copy-start(f32[1,16,128]{2,1,0:T(8,128)} %copy-done.68) | copy-start | bytes 24580
  697.6 595.7 %copy-start.73 = (f32[1,16,128]{2,1,0:T(8,128)S(1)}, f32[1,16,128]{2,1,0:T(8,128)}, u32[]{:S(2)}) copy-start(f32[1,16,128]{2,1,0:T(8,128)} %copy-done.71) | copy-start | bytes 24580
  697.6 595.7 %copy-start.76 = (f32[1,16,128]{2,1,0:T(8,128)S(1)}, f32[1,16,128]{2,1,0:T(8,128)}, u32[]{:S(2)}) copy-start(f32[1,16,128]{2,1,0:T(8,128)} %copy-done.74) | copy-start | bytes 24580
  697.6 595.7 %copy-start.79 = (f32[1,16,128]{2,1,0:T(8,128)S(1)}, f32[1,16,128]{2,1,0:T(8,128)}, u32[]{:S(2)}) copy-start(f32[1,16,128]{2,1,0:T(8,128)} %copy-done.77) | copy-start | bytes 24580
  697.6 595.7 %copy-start.82 = (f32[1,16,128]{2,1,0:T(8,128)S(1)}, f32[1,16,128]{2,1,0:T(8,128)}, u32[]{:S(2)}) copy-start(f32[1,16,128]{2,1,0:T(8,128)} %copy-done.80) | copy-start | bytes 24580
  697.6 595.7 %copy-start.85 = (f32[1,16,128]{2,1,0:T(8,128)S(1)}, f32[1,16,128]{2,1,0:T(8,128)}, u32[]{:S(2)}) copy-start(f32[1,16,128]{2,1,0:T(8,128)} %copy-done.83) | copy-start | bytes 24580
  697.6 595.7 %copy-start.88 = (f32[1,16,128]{2,1,0:T(8,128)S(1)}, f32[1,16,128]{2,1,0:T(8,128)}, u32[]{:S(2)}) copy-start(f32[1,16,128]{2,1,0:T(8,128)} %copy-done.86) | copy-start | bytes 24580
  697.6 595.7 %copy-start.91 = (f32[1,16,128]{2,1,0:T(8,128)S(1)}, f32[1,16,128]{2,1,0:T(8,128)}, u32[]{:S(2)}) copy-start(f32[1,16,128]{2,1,0:T(8,128)} %copy-done.89) | copy-start | bytes 24580
  697.7 595.7 %copy-start.94 = (f32[1,16,128]{2,1,0:T(8,128)S(1)}, f32[1,16,128]{2,1,0:T(8,128)}, u32[]{:S(2)}) copy-start(f32[1,16,128]{2,1,0:T(8,128)} %copy-done.92) | copy-start | bytes 24580
  697.7 595.7 %copy-start.97 = (f32[1,16,128]{2,1,0:T(8,128)S(1)}, f32[1,16,128]{2,1,0:T(8,128)}, u32[]{:S(2)}) copy-start(f32[1,16,128]{2,1,0:T(8,128)} %copy-done.95) | copy-start | bytes 24580
  697.7 595.7 %copy-start.100 = (f32[1,16,128]{2,1,0:T(8,128)S(1)}, f32[1,16,128]{2,1,0:T(8,128)}, u32[]{:S(2)}) copy-start(f32[1,16,128]{2,1,0:T(8,128)} %copy-done.98) | copy-start | bytes 24580
  697.7 595.7 %copy-start.103 = (f32[1,16,128]{2,1,0:T(8,128)S(1)}, f32[1,16,128]{2,1,0:T(8,128)}, u32[]{:S(2)}) copy-start(f32[1,16,128]{2,1,0:T(8,128)} %copy-done.101) | copy-start | bytes 24580
  697.7 595.7 %copy-start.106 = (f32[1,16,128]{2,1,0:T(8,128)S(1)}, f32[1,16,128]{2,1,0:T(8,128)}, u32[]{:S(2)}) copy-start(f32[1,16,128]{2,1,0:T(8,128)} %copy-done.104) | copy-start | bytes 24580
  697.7 595.7 %copy-start.109 = (f32[1,16,128]{2,1,0:T(8,128)S(1)}, f32[1,16,128]{2,1,0:T(8,128)}, u32[]{:S(2)}) copy-start(f32[1,16,128]{2,1,0:T(8,128)} %copy-done.107) | copy-start | bytes 24580
  699.4 5.2 collective-permute-start.25
  699.6 5.4 collective-permute-start.24
  705.0 3.8 collective-permute-start.26
  707.4 3.8 collective-permute-start.27
  869.8 1.4 collective-permute-start.29
  870.5 3.0 collective-permute-start.28
  873.5 2.9 collective-permute-start.30
  874.5 3.8 collective-permute-start.31
  1035.7 1.8 collective-permute-start.33
  1036.8 3.0 collective-permute-start.32
  1039.8 2.6 collective-permute-start.34
  1040.8 3.8 collective-permute-start.35
  1201.0 1.8 collective-permute-start.37
  1202.1 3.0 collective-permute-start.36
  1205.1 2.6 collective-permute-start.38
  1206.1 3.8 collective-permute-start.39
  1308.8 2.7 collective-permute-start.40
  1309.2 5.2 collective-permute-start.41
  1317.8 7.5 collective-permute-start.42
  1321.9 7.8 collective-permute-start.43
  (200 other events, 17287.4 us)
where the time goes:
time: 1360 us; the launch traced here: 1350 us
  blocking collectives  1070 us (79%)
  local copies, waits for them, and re-layouts  81.4 us (6%)
  other arithmetic  72.6 us (5%)
  starting transfers between devices  52.1 us (4%)
  waiting for transfers between devices  46.9 us (3%)
  between operations  23.3 us (2%)
    psum x8, blocking collectives, squares(): return lax.psum(jnp.sum(residual * residual), ('gx', 'gy'))  600 us
    psum x6, blocking collectives, per_device(): lax.psum(jnp.sum(surface_direction * applied), ('gx', 'gy'))  471 us
    scatter-add x2, local copies, waits for them, and re-layouts, per_device(): tracers = mixed_tracers + step_scale * interior.at[..., :2].add(from_sout...  32.2 us
  transfers between devices with their start and end apart: 44, of which 32 were waited for; matrix products, arithmetic and copies ran while one was open for 4% of the time, Pallas kernels for 0%

commit v1 on v0

v1 whole, which is shorter than its diff:
```python
import functools

import jax
import jax.numpy as jnp
from jax import lax
from jax.experimental import pallas as pl
from jax.experimental.pallas import tpu as pltpu
from jax.sharding import PartitionSpec as P

LEVELS = 48
ROWS = 16
COLS = 128
GROUPS = LEVELS // 4
F32 = jnp.float32
PAIRS = [(i, j) for i in range(4) for j in range(i, 5)]


def two_sum(a, b):
    s = a + b
    t = s - a
    return s, (a - (s - t)) + (b - t)


def fast_two_sum(a, b):
    s = a + b
    return s, b - (s - a)


def split(a):
    c = a * 4097.0
    high = c - (c - a)
    return high, a - high


def two_prod(a, b, a_parts=None, b_parts=None):
    ah, al = split(a) if a_parts is None else a_parts
    bh, bl = split(b) if b_parts is None else b_parts
    p = a * b
    return p, ((ah * bh - p) + ah * bl + al * bh) + al * bl


def pair_add(x, y):
    s, t = two_sum(x[0], y[0])
    return fast_two_sum(s, t + (x[1] + y[1]))


def pair_mul(x, y):
    p, e = two_prod(x[0], y[0])
    return fast_two_sum(p, e + (x[0] * y[1] + x[1] * y[0]))


def pair_neg(x):
    return -x[0], -x[1]


def pair_div(x, y):
    first = x[0] / y[0]
    p, e = two_prod(first, y[0])
    rest = ((x[0] - p) - e + x[1]) - first * y[1]
    return fast_two_sum(first, rest / y[0])


def roll(x, shift, axis):
    shift = shift % x.shape[axis]
    return x if shift == 0 else pltpu.roll(x, shift, axis)


def iota(shape, axis):
    return lax.broadcasted_iota(jnp.int32, shape, axis)


def put_rows(low_ref, high_ref, first, field, group, j, cells):
    at = first + field * GROUPS + group
    low_ref[at, 2 * j : 2 * j + 2, :] = cells[:2]
    high_ref[at, 2 * j : 2 * j + 2, :] = cells[ROWS - 2 :]


def packed(acc, cells, level):
    low, high = acc
    mine = lax.shift_right_logical(iota((ROWS, COLS), 1), 1) == level
    low = jnp.where(mine, pltpu.roll(cells, 2 * level, 1), low)
    high = jnp.where(mine, pltpu.roll(cells, 2 * level + 2, 1), high)
    return low, high


def put_surface(refs, fields):
    row_low, row_high, col_low, col_high = refs
    low = jnp.zeros((ROWS, COLS), F32)
    high = low
    lane_group = iota((ROWS, COLS), 1) // 8
    for n, cells in enumerate(fields):
        row_low[n] = cells[:8]
        row_high[n] = cells[8:]
        low = jnp.where(lane_group == n, roll(cells, 8 * n, 1), low)
        high = jnp.where(lane_group == n, roll(cells, 8 * n + 8, 1), high)
    col_low[0] = low
    col_high[0] = high


def put_corners(col_low, col_high, corners, count):
    south_west, south_east, north_west, north_east = corners
    for n in range(count):
        south_west[n] = col_low[n, :8, :]
        south_east[n] = col_low[n, 8:, :]
        north_west[n] = col_high[n, :8, :]
        north_east[n] = col_high[n, 8:, :]


def prepare_kernel(
    thermal, haline, temp, salt, east, north, mask, bottom, surface, diag,
    row_low, row_high, col_low, col_high, *corners,
):
    last = bottom[...]
    zero = jnp.zeros((ROWS, COLS), F32)

    def body(group, carry):
        total, depth, packs = carry
        for j in range(4):
            level = group * 4 + j
            wet = jnp.where(last > level, mask[level], 0).astype(F32)
            t, s = temp[level], salt[level]
            total = total + wet * (thermal[level] * t - haline[level] * s)
            depth = depth + wet
            for field, cells in enumerate((t, s, wet, east[level])):
                put_rows(row_low, row_high, 3, field, group, j, cells)
            packs = tuple(
                packed(acc, cells, level) for acc, cells in zip(packs, (t, s, wet, north[level]))
            )
        return total, depth, packs

    total, depth, packs = lax.fori_loop(0, GROUPS, body, (zero, zero, ((zero, zero),) * 4))
    for n, (low, high) in enumerate(packs):
        col_low[n + 1] = low
        col_high[n + 1] = high
    put_surface(
        (row_low, row_high, col_low, col_high),
        (surface[...] + total, depth / LEVELS, diag[...]),
    )
    put_corners(col_low, col_high, corners, 4)


def wide_surface(n, own, rows_e, rows_w, cols_n, cols_s, ne, nw, se, sw):
    main = jnp.concatenate([own, rows_e[n], rows_w[n]], axis=0)
    to_north = jnp.concatenate([cols_n[0], ne[0], nw[0]], axis=0)
    to_south = jnp.concatenate([cols_s[0], se[0], sw[0]], axis=0)
    lane = iota((32, COLS), 1)
    side = jnp.where(
        lane < 8,
        roll(to_north, -8 * n, 1),
        jnp.where(lane >= COLS - 8, roll(to_south, 120 - 8 * n, 1), 0.0),
    )
    return jnp.concatenate([main, side], axis=1)


def krylov(c, diag, depth, basis_ref, gram_ref):
    def nb(v):
        return pltpu.roll(v, 31, 0), pltpu.roll(v, 1, 0), pltpu.roll(v, 255, 1), pltpu.roll(v, 1, 1)

    faces = [jnp.minimum(depth, d) for d in nb(depth)]
    centre = (diag - 1.0) + ((faces[0] + faces[1]) + (faces[2] + faces[3]))
    v = c
    own = []
    for k in range(5):
        if k < 4:
            basis_ref[k] = v
        mine = v[:ROWS, :COLS]
        own.append((mine, split(mine)))
        if k < 4:
            e, w, n, s = nb(v)
            v = centre * v - ((faces[0] * e + faces[1] * w) + (faces[2] * n + faces[3] * s))
    highs, lows = [], []
    for i, j in PAIRS:
        p, e = two_prod(own[i][0], own[j][0], own[i][1], own[j][1])
        s, t = two_sum(p[:8], p[8:])
        highs.append(s)
        lows.append(t + (e[:8] + e[8:]))
    pad = [jnp.zeros((8, COLS), F32)] * (16 - len(PAIRS))
    high = jnp.concatenate(highs + pad, axis=0).T
    low = jnp.concatenate(lows + pad, axis=0).T
    parts = [(high[8 * n : 8 * n + 8], low[8 * n : 8 * n + 8]) for n in range(16)]
    while len(parts) > 1:
        parts = [pair_add(a, b) for a, b in zip(parts[::2], parts[1::2])]
    total = parts[0]
    for shift in (4, 2, 1):
        total = pair_add(total, tuple(roll(x, shift, 0) for x in total))
    total = pair_add(total, tuple(roll(x, 124, 1) for x in total))
    first_half = (iota((8, COLS), 1) % 8) < 4
    sums = jnp.where(first_half, total[0], roll(total[1], 4, 1))
    gram_ref[...] = jnp.concatenate([sums] * (gram_ref.shape[0] // 8), axis=0)


def first_surface_kernel(
    own_low, own_high, rows_e, rows_w, cols_n, cols_s, ne, nw, se, sw, basis, gram, fixed
):
    fields = [
        wide_surface(
            n, jnp.concatenate([own_low[n], own_high[n]], axis=0),
            rows_e, rows_w, cols_n, cols_s, ne, nw, se, sw,
        )
        for n in range(3)
    ]
    fixed[0] = fields[1]
    fixed[1] = fields[2]
    krylov(fields[0], fields[2], fields[1], basis, gram)


def next_surface_kernel(
    own_low, own_high, rows_e, rows_w, cols_n, cols_s, ne, nw, se, sw, fixed, basis, gram
):
    c = wide_surface(
        0, jnp.concatenate([own_low[0], own_high[0]], axis=0),
        rows_e, rows_w, cols_n, cols_s, ne, nw, se, sw,
    )
    krylov(c, fixed[1], fixed[0], basis, gram)


def coefficients(gathered):
    parts = [(gathered[8 * n : 8 * n + 8], None) for n in range(gathered.shape[0] // 8)]
    parts = [(p, jnp.zeros_like(p)) for p, _ in parts]
    while len(parts) > 1:
        parts = [pair_add(a, b) for a, b in zip(parts[::2], parts[1::2])]
    total = parts[0]
    for shift in (4, 2, 1):
        total = pair_add(total, tuple(roll(x, shift, 0) for x in total))
    for shift in (4, 2, 1):
        total = pair_add(total, tuple(roll(x, COLS - shift, 1) for x in total))
    table = {}
    for n, (i, j) in enumerate(PAIRS):
        entry = tuple(jnp.broadcast_to(x[:, 8 * n : 8 * n + 1], (8, COLS)) for x in total)
        table[i, j] = table[j, i] = entry
    one = (jnp.ones((8, COLS), F32), jnp.zeros((8, COLS), F32))
    r, p, x = [one], [one], []
    rr = table[0, 0]
    for it in range(4):
        image = [p[0]] + [pair_add(p[k], p[k - 1]) for k in range(1, it + 1)] + [p[it]]
        dot = functools.reduce(
            pair_add, [pair_mul(table[it, k], image[k]) for k in range(it + 2)]
        )
        step = pair_div(rr, pair_mul(p[it], dot))
        x = [
            pair_add(x[k], pair_mul(step, p[k])) if k < len(x) else pair_mul(step, p[k])
            for k in range(it + 1)
        ]
        if it < 3:
            minus = pair_neg(step)
            moved = [pair_mul(minus, a) for a in image]
            r = [pair_add(r[k], moved[k]) if k < len(r) else moved[k] for k in range(it + 2)]
            dot = functools.reduce(
                pair_add, [pair_mul(table[it + 1, k], r[k]) for k in range(it + 2)]
            )
            new = pair_mul(r[it + 1], dot)
            ratio = pair_div(new, rr)
            p = [
                pair_add(r[k], pair_mul(ratio, p[k])) if k < len(p) else r[k]
                for k in range(it + 2)
            ]
            rr = new
    return [a[0] for a in x]


def step_kernel(
    final,
    mix, thermal, haline, temp, salt, east, north, mask, bottom, diag, basis, gathered,
    a_rows_e, a_rows_w, a_cols_n, a_cols_s, a_ne, a_nw, a_se, a_sw,
    *rest,
):
    if final:
        (t_rows_e, t_rows_w, t_cols_n, t_cols_s, t_ne, t_nw, t_se, t_sw,
         new_temp, new_salt, new_surface,
         wet_wide, part_t, part_s, ratios, sides) = rest
        skip = 1
    else:
        (new_temp, new_salt, new_surface, row_low, row_high, col_low, col_high,
         c_sw, c_se, c_nw, c_ne,
         wet_wide, part_t, part_s, ratios, sides) = rest
        t_rows_e, t_rows_w, t_cols_n, t_cols_s, t_ne, t_nw, t_se, t_sw = (
            a_rows_e, a_rows_w, a_cols_n, a_cols_s, a_ne, a_nw, a_se, a_sw
        )
        skip = 3
    sub = iota((8, COLS), 0)
    lane = iota((24, COLS), 1)

    def set_side(n, block, cols, first, second):
        sides[n, :ROWS, :] = cols[block]
        sides[n, ROWS:, :] = jnp.where(sub < 4, first[block], second[block])

    for n, block in enumerate((1, 2)):
        set_side(2 * n, block, t_cols_n, t_ne, t_nw)
        set_side(2 * n + 1, block, t_cols_s, t_se, t_sw)
    set_side(4, 3, a_cols_n, a_ne, a_nw)
    set_side(5, 3, a_cols_s, a_se, a_sw)

    def beyond(north_side, south_side, level, rows):
        shift = COLS - 2 * level
        return jnp.where(
            lane[:rows] < 64,
            pltpu.roll(north_side, shift & 127, 1),
            pltpu.roll(south_side, (shift + 126) & 127, 1),
        )

    def end_rows(rows_e, rows_w, at, j):
        return jnp.where(sub < 4, roll(rows_e[at], -2 * j, 0), roll(rows_w[at], 6 - 2 * j, 0))

    def widened(own, rows_e, rows_w, at, j, side, level):
        main = jnp.concatenate([own, end_rows(rows_e, rows_w, at, j)], axis=0)
        return jnp.concatenate([main, beyond(sides[side], sides[side + 1], level, 24)], axis=1)

    last = bottom[...]

    def wet_body(group, _):
        for j in range(4):
            level = group * 4 + j
            wet = jnp.where(last > level, mask[level], 0).astype(F32)
            wet_wide[level] = widened(
                wet, a_rows_e, a_rows_w, 3 + 2 * GROUPS + group, j, 4, level
            )
        return 0

    lax.fori_loop(0, GROUPS, wet_body, 0)
    wet_wide[LEVELS] = jnp.zeros((24, 2 * COLS), F32)

    weights = coefficients(gathered[...])
    weights = [jnp.concatenate([jnp.concatenate([w] * 4, axis=0)] * 2, axis=1) for w in weights]
    full = sum(weights[k] * basis[k] for k in range(4))
    sub2 = iota((8, 2 * COLS), 0)
    multiplier = jnp.concatenate(
        [full[:ROWS], jnp.where(sub2 < 4, full[16:24], full[24:32])], axis=0
    )
    surface = diag[...] * full[:ROWS, :COLS]
    new_surface[...] = surface

    zero = jnp.zeros((24, 2 * COLS), F32)

    def forward(group, carry):
        up, ratio, pt, ps, wet = carry
        for j in range(4):
            level = group * 4 + j
            below = wet_wide[level + 1]
            down = mix[level] * (wet * below)
            inverse = 1.0 / ((1.0 + up + down) - up * ratio)
            t = widened(temp[level], t_rows_e, t_rows_w, skip + group, j, 0, level)
            s = widened(salt[level], t_rows_e, t_rows_w, skip + GROUPS + group, j, 2, level)
            wm = wet * multiplier
            pt = (t + thermal[level] * wm + up * pt) * inverse
            ps = (s - haline[level] * wm + up * ps) * inverse
            ratio = down * inverse
            part_t[level] = pt
            part_s[level] = ps
            ratios[level] = ratio
            up = down
            wet = below
        return up, ratio, pt, ps, wet

    lax.fori_loop(0, GROUPS, forward, (zero, zero, zero, zero, wet_wide[0]))

    def ends(v):
        return pltpu.roll(v, v.shape[0] - 1, 0), pltpu.roll(v, 1, 0)

    def flanks(v):
        return pltpu.roll(v, 2 * COLS - 1, 1), pltpu.roll(v, 1, 1)

    def backward(count, carry):
        xt, xs, total, packs = carry
        group = GROUPS - 1 - count
        for j in (3, 2, 1, 0):
            level = group * 4 + j
            ratio = ratios[level]
            xt = part_t[level] + ratio * xt
            xs = part_s[level] + ratio * xs
            wet = wet_wide[level]
            we, ww = ends(wet)
            wn, ws = flanks(wet)
            around = wet * ((we + ww) + (wn + ws))
            at = 3 + 3 * GROUPS + group
            fe = jnp.concatenate([east[level], end_rows(a_rows_e, a_rows_w, at, j)], axis=0)
            fn = jnp.concatenate(
                [north[level], beyond(a_cols_n[4], a_cols_s[4], level, ROWS)], axis=1
            )
            own = slice(0, ROWS), slice(0, COLS)
            wet_own = wet[own]
            around_own = around[own]
            diagonal = around_own + wet_own * (
                fe[:ROWS] * (ww - we)[own] + fn[:, :COLS] * (ws - wn)[own]
            )
            done = []
            for x in (xt, xs):
                q = wet * x
                qe, qw = ends(q)
                qn, qs = flanks(q)
                near = (qe + qw) + (qn + qs)
                lap = wet * near - around * x
                le, lw = ends(lap[:, :COLS])
                ln, ls = flanks(lap[:ROWS])
                lap2 = (
                    wet_own * ((le + lw)[:ROWS] + (ln + ls)[:, :COLS]) - around_own * lap[own]
                )
                be, bw = ends(fe * q[:, :COLS])
                dn, ds = flanks(fn * q[:ROWS])
                incoming = near[own] + ((be - bw)[:ROWS] + (dn - ds)[:, :COLS])
                x_own = x[own]
                done.append(
                    x_own + 0.05 * (wet_own * incoming - diagonal * x_own) - 0.01 * lap2
                )
            t, s = done
            new_temp[level] = t
            new_salt[level] = s
            if not final:
                total = total + wet_own * (thermal[level] * t - haline[level] * s)
                for field, cells in enumerate(done):
                    put_rows(row_low, row_high, 1, field, group, j, cells)
                packs = tuple(packed(acc, cells, level) for acc, cells in zip(packs, done))
        return xt, xs, total, packs

    small = jnp.zeros((ROWS, COLS), F32)
    packs = () if final else ((small, small), (small, small))
    xt, xs, total, packs = lax.fori_loop(0, GROUPS, backward, (zero, zero, small, packs))
    if not final:
        for n, (low, high) in enumerate(packs):
            col_low[n + 1] = low
            col_high[n + 1] = high
        put_surface((row_low, row_high, col_low, col_high), (surface + total,))
        put_corners(col_low, col_high, (c_sw, c_se, c_nw, c_ne), 3)


def shape(*dims):
    return jax.ShapeDtypeStruct(dims, F32)


VMEM = pl.BlockSpec(memory_space=pltpu.VMEM)
SMEM = pl.BlockSpec(memory_space=pltpu.SMEM)


def head(*block):
    return pl.BlockSpec(block, lambda i: (0,) * len(block), memory_space=pltpu.VMEM)


def call(kernel, outs, in_specs, out_specs=None, scratch=(), name=None, grid=None):
    extra = {} if grid is None else {"grid": grid}
    return pl.pallas_call(
        kernel,
        out_shape=outs,
        in_specs=in_specs,
        out_specs=[VMEM] * len(outs) if out_specs is None else out_specs,
        scratch_shapes=scratch,
        compiler_params=pltpu.CompilerParams(vmem_limit_bytes=40 * 1024 * 1024),
        name=name,
        **extra,
    )


def message_shapes(surfaces, row_fields, col_fields, corner_fields):
    rows = shape(surfaces + GROUPS * row_fields, 8, COLS)
    cols = shape(1 + col_fields, ROWS, COLS)
    corner = shape(1 + corner_fields, 8, COLS)
    return [rows, rows, cols, cols] + [corner] * 4


def solution(mesh):
    nx, ny = mesh.shape["gx"], mesh.shape["gy"]
    devices = nx * ny
    both = ("gx", "gy")

    def route(di, dj):
        return [
            (i * ny + j, (i + di) % nx * ny + j + dj)
            for i in range(nx)
            for j in range(ny)
            if 0 <= j + dj < ny
        ]

    def exchange(messages):
        row_low, row_high, col_low, col_high, sw, se, nw, ne = messages
        sends = (
            (row_low, -1, 0), (row_high, 1, 0), (col_low, 0, -1), (col_high, 0, 1),
            (sw, -1, -1), (se, 1, -1), (nw, -1, 1), (ne, 1, 1),
        )
        return [lax.ppermute(m, both, route(di, dj)) for m, di, dj in sends]

    def all_sum(block):
        return lax.all_to_all(block, both, 0, 0, tiled=True)

    def surface_specs(count):
        return (
            [head(count, 8, COLS)] * 4
            + [head(1, ROWS, COLS)] * 2
            + [head(1, 8, COLS)] * 4
        )

    basis_shape = shape(4, 32, 2 * COLS)
    gram_shape = shape(devices, COLS)
    field = shape(LEVELS, ROWS, COLS)
    tile = shape(ROWS, COLS)

    def whole(*dims):
        return head(*dims)

    def per_device(
        sens_temp, sens_salt, sens_surface, flow_east, flow_north, mix_profile,
        thermal_weight, haline_weight, surface_diag, land_mask, bottom_level,
    ):
        first = call(
            prepare_kernel, message_shapes(3, 4, 4, 3), [SMEM] * 2 + [VMEM] * 8, name="prepare"
        )(
            thermal_weight, haline_weight, sens_temp, sens_salt, flow_east, flow_north,
            land_mask, bottom_level, sens_surface, surface_diag,
        )
        got = exchange(first)
        basis, gram, fixed = call(
            first_surface_kernel,
            [basis_shape, gram_shape, shape(2, 32, 2 * COLS)],
            surface_specs(3),
            [whole(4, 32, 2 * COLS), whole(devices, COLS), whole(2, 32, 2 * COLS)],
            name="first_surface",
            grid=(1,),
        )(first[0], first[1], *got)
        gathered = all_sum(gram)

        scratch = [
            pltpu.VMEM((LEVELS + 1, 24, 2 * COLS), F32),
            pltpu.VMEM((LEVELS, 24, 2 * COLS), F32),
            pltpu.VMEM((LEVELS, 24, 2 * COLS), F32),
            pltpu.VMEM((LEVELS, 24, 2 * COLS), F32),
            pltpu.VMEM((6, 24, COLS), F32),
        ]

        def step(final, temp, salt, basis, gathered, more, outs):
            return call(
                functools.partial(step_kernel, final),
                outs,
                [SMEM] * 3 + [VMEM] * (17 + len(more)),
                scratch=scratch,
                name="last_step" if final else "first_step",
            )(
                mix_profile, thermal_weight, haline_weight, temp, salt, flow_east, flow_north,
                land_mask, bottom_level, surface_diag, basis, gathered, *got, *more,
            )

        temp, salt, _, *second = step(
            False, sens_temp, sens_salt, basis, gathered, [],
            [field, field, tile] + message_shapes(1, 2, 2, 2),
        )
        more = exchange(second)
        basis, gram = call(
            next_surface_kernel,
            [basis_shape, gram_shape],
            surface_specs(1) + [whole(2, 32, 2 * COLS)],
            [whole(4, 32, 2 * COLS), whole(devices, COLS)],
            name="next_surface",
            grid=(1,),
        )(second[0], second[1], *more, fixed)
        gathered = all_sum(gram)
        return tuple(step(True, temp, salt, basis, gathered, more, [field, field, tile]))

    in_specs = (
        P(None, "gx", "gy"),
        P(None, "gx", "gy"),
        P("gx", "gy"),
        P(None, "gx", "gy"),
        P(None, "gx", "gy"),
        P(),
        P(),
        P(),
        P("gx", "gy"),
        P(None, "gx", "gy"),
        P("gx", "gy"),
    )
    out_specs = (P(None, "gx", "gy"), P(None, "gx", "gy"), P("gx", "gy"))
    return jax.shard_map(
        per_device, mesh=mesh, in_specs=in_specs, out_specs=out_specs, check_vma=False
    )
```

time: 1360 us -> 160 us (0.12)
  blocking collectives: 1070 us -> 66.7 us
  other arithmetic: 72.6 us -> 0 us
  local copies, waits for them, and re-layouts: 81.4 us -> 9.02 us
  waiting for transfers between devices: 46.9 us -> 6.92 us
  Pallas kernels: 0 us -> 32.3 us
  between operations: 23.3 us -> 0.84 us
    psum x14 -> x0, blocking collectives: 1070 us -> none  [the longest x8 600 us: squares(): return lax.psum(jnp.sum(residual * residual), ('gx', 'gy'))]
    all_to_all x0 -> x2, blocking collectives: none -> 66.7 us  [all_sum(): return lax.all_to_all(block, both, 0, 0, tiled=True)]
    scatter-add x4 -> x0, local copies, waits for them, and re-layouts: 40 us -> none  [the longest x2 32.2 us: per_device(): tracers = mixed_tracers + step_scale * interior.at[..., :2].add(from_sout...]
    ppermute x44 -> x16, waiting for transfers between devices: 46.9 us -> 6.92 us  [exchange(): return [lax.ppermute(m, both, route(di, dj)) for m, di, dj in sends]]
    pallas_call x0 -> x5, Pallas kernels: none -> 32.3 us  [the longest x2 28.6 us: step(): call(functools.partial(step_kernel, final), outs, [SMEM] * 3 + [VMEM] * (...]
    mul x30 -> x0, other arithmetic: 26.2 us -> none  [the longest x22 13.9 us: vertical_solve(): ratios[level_index] * solved[-1]]
    slice x33 -> x0, local copies, waits for them, and re-layouts: 19.1 us -> none  [the longest x4 6.32 us: per_device(): from_north = passed_along_2(middle[..., :2], 'gy', -1)]
    reduce_sum x16 -> x0, other arithmetic: 14.8 us -> none  [the longest x8 8.73 us: per_device(): jnp.sum(surface_direction * applied)]
  transfers between devices with their start and end apart: 44 -> 16, of which waited for: 32 -> 5; matrix products, arithmetic and copies ran while one was open for 4% -> 0% of each run, Pallas kernels for 0% -> 0%
where the time goes in v1:
time: 160 us; the launch traced here: 159 us
  blocking collectives  66.7 us (42%)
  starting transfers between devices  42.9 us (27%)
  Pallas kernels  32.3 us (20%)
  local copies, waits for them, and re-layouts  9.02 us (6%)
  waiting for transfers between devices  6.92 us (4%)
    all_to_all x2, blocking collectives, all_sum(): return lax.all_to_all(block, both, 0, 0, tiled=True)  66.7 us
    ppermute x16, starting transfers between devices, exchange(): return [lax.ppermute(m, both, route(di, dj)) for m, di, dj in sends]  42.9 us
    pallas_call x2, Pallas kernels, step(): call(functools.partial(step_kernel, final), outs, [SMEM] * 3 + [VMEM] * (...  28.6 us
    unnamed x34, local copies, waits for them, and re-layouts  9.02 us
    ppermute x16, waiting for transfers between devices, exchange(): return [lax.ppermute(m, both, route(di, dj)) for m, di, dj in sends]  6.92 us
  transfers between devices with their start and end apart: 16, of which 5 were waited for; matrix products, arithmetic and copies ran while one was open for 0% of the time, Pallas kernels for 0%

profile of v1, /device:TPU:1, one launch (start us, length us, event | category | flops | bytes accessed | tf_op | source)
XLA Modules:
  0.0 158.7 jit_solution(13202143744398820630)
XLA Ops:
  0.6 0.0 copy-start
  0.6 1.0 copy-done
  1.6 0.0 copy-start.2
  1.6 1.0 copy-done.2
  2.6 0.0 copy-start.4
  2.6 1.0 copy-done.4
  3.6 0.0 copy-start.6
  3.6 1.0 copy-done.6
  4.6 0.0 copy-start.8
  4.6 1.0 copy-done.8
  5.6 0.0 copy-start.10
  5.6 0.7 copy-done.10
  6.3 0.7 copy-done.11
  7.0 0.7 copy-done.13
  7.7 0.7 copy-done.14
  8.4 0.7 copy-done.15
  9.0 2.3 %prepare.1 = (f32[51,8,128]{2,1,0:T(8,128)S(1)}, f32[51,8,128]{2,1,0:T(8,128)S(1)}, f32[5,16,128]{2,1,0:T(8,128)S(1)}, f32[5,16,128]{2,1,0:T(8,128)S(1)}, f32[4,...) custom-call(f32[48]{0:T(128)S(1)} %copy-done.14, ...), custom_call_target="tpu_custom_call" | custom-call | tf_op jit(solution)/shard_map/prepare/pallas_call | solution.py:501
  11.3 3.3 %collective-permute-start = (f32[51,8,128]{2,1,0:T(8,128)S(1)}, f32[51,8,128]{2,1,0:T(8,128)S(1)}, u32[]{:S(2)}, u32[]{:S(2)}) collective-permute-start(f32[51,8,128]{2,1,0:T(8,128)S(1)} %get-tuple-element.26.own_low), channel_id=1, source_target_pairs={{0,248},{1,249},{2,250},{3,251},{4,252},{5,253},{6,254},{7,255},{8... | collective-permute-start | bytes 626696 | tf_op jit(solution)/shard_map/ppermute | solution.py:477
  14.6 0.0 collective-permute-start.1
  14.6 1.3 collective-permute-start.4
  15.9 1.3 collective-permute-start.5
  17.2 1.3 collective-permute-start.2
  18.5 2.1 %collective-permute-done.4.ne.a_ne = f32[4,8,128]{2,1,0:T(8,128)S(1)} collective-permute-done((f32[4,8,128]{2,1,0:T(8,128)S(1)}, f32[4,8,128]{2,1,0:T(8,128)S(1)}, u32[]{:S(2)}, u32[]{:S(2)}) %collective-permute-start.4) | collective-permute-done | bytes 16416 | tf_op jit(solution)/shard_map/ppermute | solution.py:477
  20.6 6.0 %collective-permute-start.3 = (f32[5,16,128]{2,1,0:T(8,128)S(1)}, f32[5,16,128]{2,1,0:T(8,128)S(1)}, u32[]{:S(2)}, u32[]{:S(2)}) collective-permute-start(f32[5,16,128]{2,1,0:T(8,128)S(1)} %get-tuple-element.29), channel_id=1, source_target_pairs={{0,1},{1,2},{2,3},{3,4},{4,5},{5,6},{6,7},{8,9},{9,10},{10,11},{11... | collective-permute-start | bytes 122888 | tf_op jit(solution)/shard_map/ppermute | solution.py:477
  26.6 2.3 %collective-permute-done.5.nw.a_nw = f32[4,8,128]{2,1,0:T(8,128)S(1)} collective-permute-done((f32[4,8,128]{2,1,0:T(8,128)S(1)}, f32[4,8,128]{2,1,0:T(8,128)S(1)}, u32[]{:S(2)}, u32[]{:S(2)}) %collective-permute-start.5) | collective-permute-done | bytes 16416 | tf_op jit(solution)/shard_map/ppermute | solution.py:477
  28.9 7.8 %collective-permute-start.6 = (f32[4,8,128]{2,1,0:T(8,128)S(1)}, f32[4,8,128]{2,1,0:T(8,128)S(1)}, u32[]{:S(2)}, u32[]{:S(2)}) collective-permute-start(f32[4,8,128]{2,1,0:T(8,128)S(1)} %get-tuple-element.32), channel_id=1, source_target_pairs={{0,249},{1,250},{2,251},{3,252},{4,253},{5,254},{6,255},{8,1},{9,2... | collective-permute-start | bytes 49160 | tf_op jit(solution)/shard_map/ppermute | solution.py:477
  36.7 0.9 collective-permute-done.6.se.a_se
  37.6 1.4 collective-permute-start.7
  39.0 0.9 collective-permute-done.7.sw.a_sw
  39.9 0.0 collective-permute-done.2.cols_n.a_cols_n
  39.9 0.0 collective-permute-done.3.cols_s.a_cols_s
  39.9 0.0 collective-permute-done.rows_e.a_rows_e
  39.9 0.0 collective-permute-done.1.rows_w.a_rows_w
  39.9 0.7 first_surface.1
  40.6 0.0 copy-start.12
  40.6 34.5 %all_to_all.22 = f32[256,1,128]{2,1,0:T(1,128)S(1)} all-to-all(f32[256,1,128]{2,1,0:T(1,128)S(1)} %bitcast.10), channel_id=1, replica_groups=mesh['gx'=32,'gy'=8] {'gx','gy'}, dimensions={0} | all-to-all | bytes 262144 | tf_op jit(solution)/shard_map/all_to_all | solution.py:480
  75.1 0.0 copy-done.9
  75.1 0.0 copy-done.1
  75.1 0.0 copy-done.3
  75.1 0.0 copy-done.7
  75.1 0.0 copy-done.12
  75.1 0.6 copy-done.16
  75.7 14.6 %first_step.1 = (f32[48,16,128]{2,1,0:T(8,128)S(1)}, f32[48,16,128]{2,1,0:T(8,128)S(1)}, f32[16,128]{1,0:T(8,128)}, f32[25,8,128]{2,1,0:T(8,128)S(1)}, f32[25,8,...) custom-call(f32[48]{0:T(128)S(1)} %copy-done.16, ...), custom_call_target="tpu_custom_call" | custom-call | tf_op jit(solution)/shard_map/first_step/pallas_call | solution.py:527
  90.4 0.6 collective-permute-start.8
  91.0 1.2 collective-permute-start.9
  92.1 1.3 collective-permute-start.12
  93.4 1.3 collective-permute-start.13
  94.7 9.2 %collective-permute-start.14 = (f32[3,8,128]{2,1,0:T(8,128)S(1)}, f32[3,8,128]{2,1,0:T(8,128)S(1)}, u32[]{:S(2)}, u32[]{:S(2)}) collective-permute-start(f32[3,8,128]{2,1,0:T(8,128)S(1)} %get-tuple-element.44), channel_id=1, source_target_pairs={{0,249},{1,250},{2,251},{3,252},{4,253},{5,254},{6,255},{8,1},{9,2... | collective-permute-start | bytes 36872 | tf_op jit(solution)/shard_map/ppermute | solution.py:477
  103.9 0.0 collective-permute-done.12.ne.rest_4_
  103.9 1.3 collective-permute-start.10
  105.2 0.0 collective-permute-done.13.nw.rest_5_
  105.2 4.0 %collective-permute-start.11 = (f32[3,16,128]{2,1,0:T(8,128)S(1)}, f32[3,16,128]{2,1,0:T(8,128)S(1)}, u32[]{:S(2)}, u32[]{:S(2)}) collective-permute-start(f32[3,16,128]{2,1,0:T(8,128)S(1)} %get-tuple-element.41), channel_id=1, source_target_pairs={{0,1},{1,2},{2,3},{3,4},{4,5},{5,6},{6,7},{8,9},{9,10},{10,11},{11... | collective-permute-start | bytes 73736 | tf_op jit(solution)/shard_map/ppermute | solution.py:477
  109.2 0.0 collective-permute-done.14.se.rest_6_
  109.2 1.7 %collective-permute-start.15 = (f32[3,8,128]{2,1,0:T(8,128)S(1)}, f32[3,8,128]{2,1,0:T(8,128)S(1)}, u32[]{:S(2)}, u32[]{:S(2)}) collective-permute-start(f32[3,8,128]{2,1,0:T(8,128)S(1)} %get-tuple-element.45), channel_id=1, source_target_pairs={{0,9},{1,10},{2,11},{3,12},{4,13},{5,14},{6,15},{8,17},{9,18},{10,... | collective-permute-start | bytes 36872 | tf_op jit(solution)/shard_map/ppermute | solution.py:477
  110.9 0.8 collective-permute-done.15.sw.rest_7_
  111.8 0.0 collective-permute-done.10.cols_n.rest_2_
  111.8 0.0 collective-permute-done.11.cols_s.rest_3_
  111.8 0.0 collective-permute-done.8.rows_e.rest_0_
  111.8 0.0 collective-permute-done.9.rows_w.rest_1_
  111.8 0.0 copy-start.5
  111.8 0.7 next_surface.1
  112.5 32.3 %all_to_all.23 = f32[256,1,128]{2,1,0:T(1,128)S(1)} all-to-all(f32[256,1,128]{2,1,0:T(1,128)S(1)} %bitcast.11), channel_id=1, replica_groups=mesh['gx'=32,'gy'=8] {'gx','gy'}, dimensions={0} | all-to-all | bytes 262144 | tf_op jit(solution)/shard_map/all_to_all | solution.py:480
  144.7 0.0 copy-done.5
  144.7 14.0 %last_step.1 = (f32[48,16,128]{2,1,0:T(8,128)}, f32[48,16,128]{2,1,0:T(8,128)}, f32[16,128]{1,0:T(8,128)}) custom-call(f32[48]{0:T(128)S(1)} %copy-done.16, f32[48]{0:T(128)S(1)} %copy-done.14, f32[48]{0:T(128)S(1)} %copy-done.15, f32[48,16,128]{2,1,0:T(8,128)S(1)} %get-tuple-element.36.temp, f32[48,16,128]{2,1,0:T(8,128)S(1)} %get-tuple-element.37.salt, ...), custom_call_target="tpu_custom_call" | custom-call | tf_op jit(solution)/shard_map/last_step/pallas_call | solution.py:527
  (9 shorter events, 0.0 us)
Async XLA Ops:
  0.6 1.0 copy-start
  1.6 1.0 copy-start.2
  2.6 1.0 copy-start.4
  3.6 1.0 copy-start.6
  4.6 1.0 copy-start.8
  5.6 0.7 copy-start.10
  6.3 0.7 copy-start.11
  7.0 0.7 copy-start.13
  7.7 0.7 copy-start.14
  8.4 0.7 copy-start.15
  9.0 66.1 %copy-start.9 = (f32[48,16,128]{2,1,0:T(8,128)S(1)}, f32[48,16,128]{2,1,0:T(8,128)}, u32[]{:S(2)}) copy-start(f32[48,16,128]{2,1,0:T(8,128)} %salt.3) | copy-start | bytes 1179652
  11.3 28.6 %collective-permute-start = (f32[51,8,128]{2,1,0:T(8,128)S(1)}, f32[51,8,128]{2,1,0:T(8,128)S(1)}, u32[]{:S(2)}, u32[]{:S(2)}) collective-permute-start(f32[51,8,128]{2,1,0:T(8,128)S(1)} %get-tuple-element.26.own_low), channel_id=1, source_target_pairs={{0,248},{1,249},{2,250},{3,251},{4,252},{5,253},{6,254},{7,255},{8... | collective-permute-start | bytes 626696 | tf_op jit(solution)/shard_map/ppermute | solution.py:477
  14.6 25.3 %collective-permute-start.1 = (f32[51,8,128]{2,1,0:T(8,128)S(1)}, f32[51,8,128]{2,1,0:T(8,128)S(1)}, u32[]{:S(2)}, u32[]{:S(2)}) collective-permute-start(f32[51,8,128]{2,1,0:T(8,128)S(1)} %get-tuple-element.27.own_high), channel_id=1, source_target_pairs={{0,8},{1,9},{2,10},{3,11},{4,12},{5,13},{6,14},{7,15},{8,16},{9,17... | collective-permute-start | bytes 626696 | tf_op jit(solution)/shard_map/ppermute | solution.py:477
  14.6 5.9 %collective-permute-start.4 = (f32[4,8,128]{2,1,0:T(8,128)S(1)}, f32[4,8,128]{2,1,0:T(8,128)S(1)}, u32[]{:S(2)}, u32[]{:S(2)}) collective-permute-start(f32[4,8,128]{2,1,0:T(8,128)S(1)} %get-tuple-element.30), channel_id=1, source_target_pairs={{1,248},{2,249},{3,250},{4,251},{5,252},{6,253},{7,254},{9,0},{10,... | collective-permute-start | bytes 49160 | tf_op jit(solution)/shard_map/ppermute | solution.py:477
  15.9 13.0 %collective-permute-start.5 = (f32[4,8,128]{2,1,0:T(8,128)S(1)}, f32[4,8,128]{2,1,0:T(8,128)S(1)}, u32[]{:S(2)}, u32[]{:S(2)}) collective-permute-start(f32[4,8,128]{2,1,0:T(8,128)S(1)} %get-tuple-element.31), channel_id=1, source_target_pairs={{1,8},{2,9},{3,10},{4,11},{5,12},{6,13},{7,14},{9,16},{10,17},{11,... | collective-permute-start | bytes 49160 | tf_op jit(solution)/shard_map/ppermute | solution.py:477
  17.2 22.7 %collective-permute-start.2 = (f32[5,16,128]{2,1,0:T(8,128)S(1)}, f32[5,16,128]{2,1,0:T(8,128)S(1)}, u32[]{:S(2)}, u32[]{:S(2)}) collective-permute-start(f32[5,16,128]{2,1,0:T(8,128)S(1)} %get-tuple-element.28), channel_id=1, source_target_pairs={{1,0},{2,1},{3,2},{4,3},{5,4},{6,5},{7,6},{9,8},{10,9},{11,10},{12... | collective-permute-start | bytes 122888 | tf_op jit(solution)/shard_map/ppermute | solution.py:477
  20.6 19.3 %collective-permute-start.3 = (f32[5,16,128]{2,1,0:T(8,128)S(1)}, f32[5,16,128]{2,1,0:T(8,128)S(1)}, u32[]{:S(2)}, u32[]{:S(2)}) collective-permute-start(f32[5,16,128]{2,1,0:T(8,128)S(1)} %get-tuple-element.29), channel_id=1, source_target_pairs={{0,1},{1,2},{2,3},{3,4},{4,5},{5,6},{6,7},{8,9},{9,10},{10,11},{11... | collective-permute-start | bytes 122888 | tf_op jit(solution)/shard_map/ppermute | solution.py:477
  28.9 8.7 %collective-permute-start.6 = (f32[4,8,128]{2,1,0:T(8,128)S(1)}, f32[4,8,128]{2,1,0:T(8,128)S(1)}, u32[]{:S(2)}, u32[]{:S(2)}) collective-permute-start(f32[4,8,128]{2,1,0:T(8,128)S(1)} %get-tuple-element.32), channel_id=1, source_target_pairs={{0,249},{1,250},{2,251},{3,252},{4,253},{5,254},{6,255},{8,1},{9,2... | collective-permute-start | bytes 49160 | tf_op jit(solution)/shard_map/ppermute | solution.py:477
  37.6 37.5 %copy-start.1 = (f32[48,16,128]{2,1,0:T(8,128)S(1)}, f32[48,16,128]{2,1,0:T(8,128)}, u32[]{:S(2)}) copy-start(f32[48,16,128]{2,1,0:T(8,128)} %east.5) | copy-start | bytes 1179652
  37.6 37.5 %copy-start.3 = (f32[48,16,128]{2,1,0:T(8,128)S(1)}, f32[48,16,128]{2,1,0:T(8,128)}, u32[]{:S(2)}) copy-start(f32[48,16,128]{2,1,0:T(8,128)} %north.5) | copy-start | bytes 1179652
  37.6 37.5 %copy-start.7 = (f32[48,16,128]{2,1,0:T(8,128)S(1)}, f32[48,16,128]{2,1,0:T(8,128)}, u32[]{:S(2)}) copy-start(f32[48,16,128]{2,1,0:T(8,128)} %temp.3) | copy-start | bytes 1179652
  37.6 2.3 %collective-permute-start.7 = (f32[4,8,128]{2,1,0:T(8,128)S(1)}, f32[4,8,128]{2,1,0:T(8,128)S(1)}, u32[]{:S(2)}, u32[]{:S(2)}) collective-permute-start(f32[4,8,128]{2,1,0:T(8,128)S(1)} %get-tuple-element.33), channel_id=1, source_target_pairs={{0,9},{1,10},{2,11},{3,12},{4,13},{5,14},{6,15},{8,17},{9,18},{10,... | collective-permute-start | bytes 49160 | tf_op jit(solution)/shard_map/ppermute | solution.py:477
  40.6 34.5 %copy-start.12 = (f32[16,128]{1,0:T(8,128)S(1)}, f32[16,128]{1,0:T(8,128)}, u32[]{:S(2)}) copy-start(f32[16,128]{1,0:T(8,128)} %diag.5) | copy-start | bytes 24580
  75.1 0.7 copy-start.16
  90.4 21.4 %collective-permute-start.8 = (f32[25,8,128]{2,1,0:T(8,128)S(1)}, f32[25,8,128]{2,1,0:T(8,128)S(1)}, u32[]{:S(2)}, u32[]{:S(2)}) collective-permute-start(f32[25,8,128]{2,1,0:T(8,128)S(1)} %get-tuple-element.38.own_low), channel_id=1, source_target_pairs={{0,248},{1,249},{2,250},{3,251},{4,252},{5,253},{6,254},{7,255},{8... | collective-permute-start | bytes 307208 | tf_op jit(solution)/shard_map/ppermute | solution.py:477
  91.0 20.8 %collective-permute-start.9 = (f32[25,8,128]{2,1,0:T(8,128)S(1)}, f32[25,8,128]{2,1,0:T(8,128)S(1)}, u32[]{:S(2)}, u32[]{:S(2)}) collective-permute-start(f32[25,8,128]{2,1,0:T(8,128)S(1)} %get-tuple-element.39.own_high), channel_id=1, source_target_pairs={{0,8},{1,9},{2,10},{3,11},{4,12},{5,13},{6,14},{7,15},{8,16},{9,17... | collective-permute-start | bytes 307208 | tf_op jit(solution)/shard_map/ppermute | solution.py:477
  92.1 11.8 %collective-permute-start.12 = (f32[3,8,128]{2,1,0:T(8,128)S(1)}, f32[3,8,128]{2,1,0:T(8,128)S(1)}, u32[]{:S(2)}, u32[]{:S(2)}) collective-permute-start(f32[3,8,128]{2,1,0:T(8,128)S(1)} %get-tuple-element.42), channel_id=1, source_target_pairs={{1,248},{2,249},{3,250},{4,251},{5,252},{6,253},{7,254},{9,0},{10,... | collective-permute-start | bytes 36872 | tf_op jit(solution)/shard_map/ppermute | solution.py:477
  93.4 11.8 %collective-permute-start.13 = (f32[3,8,128]{2,1,0:T(8,128)S(1)}, f32[3,8,128]{2,1,0:T(8,128)S(1)}, u32[]{:S(2)}, u32[]{:S(2)}) collective-permute-start(f32[3,8,128]{2,1,0:T(8,128)S(1)} %get-tuple-element.43), channel_id=1, source_target_pairs={{1,8},{2,9},{3,10},{4,11},{5,12},{6,13},{7,14},{9,16},{10,17},{11,... | collective-permute-start | bytes 36872 | tf_op jit(solution)/shard_map/ppermute | solution.py:477
  94.7 14.5 %collective-permute-start.14 = (f32[3,8,128]{2,1,0:T(8,128)S(1)}, f32[3,8,128]{2,1,0:T(8,128)S(1)}, u32[]{:S(2)}, u32[]{:S(2)}) collective-permute-start(f32[3,8,128]{2,1,0:T(8,128)S(1)} %get-tuple-element.44), channel_id=1, source_target_pairs={{0,249},{1,250},{2,251},{3,252},{4,253},{5,254},{6,255},{8,1},{9,2... | collective-permute-start | bytes 36872 | tf_op jit(solution)/shard_map/ppermute | solution.py:477
  103.9 7.9 %collective-permute-start.10 = (f32[3,16,128]{2,1,0:T(8,128)S(1)}, f32[3,16,128]{2,1,0:T(8,128)S(1)}, u32[]{:S(2)}, u32[]{:S(2)}) collective-permute-start(f32[3,16,128]{2,1,0:T(8,128)S(1)} %get-tuple-element.40), channel_id=1, source_target_pairs={{1,0},{2,1},{3,2},{4,3},{5,4},{6,5},{7,6},{9,8},{10,9},{11,10},{12... | collective-permute-start | bytes 73736 | tf_op jit(solution)/shard_map/ppermute | solution.py:477
  105.2 6.6 %collective-permute-start.11 = (f32[3,16,128]{2,1,0:T(8,128)S(1)}, f32[3,16,128]{2,1,0:T(8,128)S(1)}, u32[]{:S(2)}, u32[]{:S(2)}) collective-permute-start(f32[3,16,128]{2,1,0:T(8,128)S(1)} %get-tuple-element.41), channel_id=1, source_target_pairs={{0,1},{1,2},{2,3},{3,4},{4,5},{5,6},{6,7},{8,9},{9,10},{10,11},{11... | collective-permute-start | bytes 73736 | tf_op jit(solution)/shard_map/ppermute | solution.py:477
  109.2 2.6 %collective-permute-start.15 = (f32[3,8,128]{2,1,0:T(8,128)S(1)}, f32[3,8,128]{2,1,0:T(8,128)S(1)}, u32[]{:S(2)}, u32[]{:S(2)}) collective-permute-start(f32[3,8,128]{2,1,0:T(8,128)S(1)} %get-tuple-element.45), channel_id=1, source_target_pairs={{0,9},{1,10},{2,11},{3,12},{4,13},{5,14},{6,15},{8,17},{9,18},{10,... | collective-permute-start | bytes 36872 | tf_op jit(solution)/shard_map/ppermute | solution.py:477
  111.8 33.0 %copy-start.5 = (s32[48,16,128]{2,1,0:T(8,128)S(1)}, s32[48,16,128]{2,1,0:T(8,128)}, u32[]{:S(2)}) copy-start(s32[48,16,128]{2,1,0:T(8,128)} %mask.5) | copy-start | bytes 1179652

commit v2 on v1

--- a/solution.py
+++ b/solution.py
@@ -11,6 +11,7 @@
 ROWS = 16
 COLS = 128
 GROUPS = LEVELS // 4
+CHUNK = 12
 F32 = jnp.float32
 PAIRS = [(i, j) for i in range(4) for j in range(i, 5)]
 
@@ -83,35 +84,62 @@
     return low, high
 
 
-def put_surface(refs, fields):
+def put_surface(refs, first, fields):
     row_low, row_high, col_low, col_high = refs
     low = jnp.zeros((ROWS, COLS), F32)
     high = low
     lane_group = iota((ROWS, COLS), 1) // 8
     for n, cells in enumerate(fields):
-        row_low[n] = cells[:8]
-        row_high[n] = cells[8:]
+        row_low[first + n] = cells[:8]
+        row_high[first + n] = cells[8:]
         low = jnp.where(lane_group == n, roll(cells, 8 * n, 1), low)
         high = jnp.where(lane_group == n, roll(cells, 8 * n + 8, 1), high)
-    col_low[0] = low
-    col_high[0] = high
-
-
-def put_corners(col_low, col_high, corners, count):
-    south_west, south_east, north_west, north_east = corners
-    for n in range(count):
-        south_west[n] = col_low[n, :8, :]
-        south_east[n] = col_low[n, 8:, :]
-        north_west[n] = col_high[n, :8, :]
-        north_east[n] = col_high[n, 8:, :]
+    put_cols(refs, 0, low, high)
+
+
+def put_cols(refs, n, low, high):
+    row_low, row_high, col_low, col_high = refs
+    count = corners_of(row_low)
+    for col, side, cells in ((col_low, 0, low), (col_high, count, high)):
+        col[2 * n] = cells[:8]
+        col[2 * n + 1] = cells[8:]
+        if n < count:
+            row_low[side + n] = cells[:8]
+            row_high[side + n] = cells[8:]
+
+
+def corners_of(rows):
+    return {3 + 4 * GROUPS + 8: 4, 1 + 2 * GROUPS + 6: 3}[rows.shape[0]]
+
+
+def forward_kernel(own_low, own_high, rows_e, rows_w, to_south, to_north):
+    count = rows_e.shape[0] // 2
+    own = own_low.shape[0]
+    for out, mine, side in ((to_south, own_low, 0), (to_north, own_high, count)):
+        out[:own] = mine[...]
+        out[own : own + count] = rows_e[side : side + count]
+        out[own + count :] = rows_w[side : side + count]
 
 
 def prepare_kernel(
-    thermal, haline, temp, salt, east, north, mask, bottom, surface, diag,
-    row_low, row_high, col_low, col_high, *corners,
+    thermal, haline, temp_in, salt_in, east_in, north_in, mask_in, bottom, surface, diag,
+    row_low, row_high, col_low, col_high,
+    temp, salt, east, north, mask, sems,
 ):
     last = bottom[...]
     zero = jnp.zeros((ROWS, COLS), F32)
+    fields = list(
+        zip((temp_in, salt_in, mask_in, east_in, north_in), (temp, salt, mask, east, north))
+    )
+
+    def copy(n, part):
+        source, target = fields[n]
+        levels = pl.ds(part * CHUNK, CHUNK)
+        return pltpu.make_async_copy(source.at[levels], target.at[levels], sems.at[n, part])
+
+    for part in range(LEVELS // CHUNK):
+        for n in range(5):
+            copy(n, part).start()
 
     def body(group, carry):
         total, depth, packs = carry
@@ -122,27 +150,29 @@
             total = total + wet * (thermal[level] * t - haline[level] * s)
             depth = depth + wet
             for field, cells in enumerate((t, s, wet, east[level])):
-                put_rows(row_low, row_high, 3, field, group, j, cells)
+                put_rows(row_low, row_high, 11, field, group, j, cells)
             packs = tuple(
                 packed(acc, cells, level) for acc, cells in zip(packs, (t, s, wet, north[level]))
             )
         return total, depth, packs
 
-    total, depth, packs = lax.fori_loop(0, GROUPS, body, (zero, zero, ((zero, zero),) * 4))
+    carry = (zero, zero, ((zero, zero),) * 4)
+    step = CHUNK // 4
+    for part in range(LEVELS // CHUNK):
+        for n in range(5):
+            copy(n, part).wait()
+        carry = lax.fori_loop(part * step, (part + 1) * step, body, carry)
+    total, depth, packs = carry
+    refs = row_low, row_high, col_low, col_high
+    put_surface(refs, 8, (surface[...] + total, depth / LEVELS, diag[...]))
     for n, (low, high) in enumerate(packs):
-        col_low[n + 1] = low
-        col_high[n + 1] = high
-    put_surface(
-        (row_low, row_high, col_low, col_high),
-        (surface[...] + total, depth / LEVELS, diag[...]),
-    )
-    put_corners(col_low, col_high, corners, 4)
-
-
-def wide_surface(n, own, rows_e, rows_w, cols_n, cols_s, ne, nw, se, sw):
-    main = jnp.concatenate([own, rows_e[n], rows_w[n]], axis=0)
-    to_north = jnp.concatenate([cols_n[0], ne[0], nw[0]], axis=0)
-    to_south = jnp.concatenate([cols_s[0], se[0], sw[0]], axis=0)
+        put_cols(refs, n + 1, low, high)
+
+
+def wide_surface(n, own, rows_e, rows_w, from_north, from_south):
+    main = jnp.concatenate([own, rows_e, rows_w], axis=0)
+    to_north = jnp.concatenate(from_north, axis=0)
+    to_south = jnp.concatenate(from_south, axis=0)
     lane = iota((32, COLS), 1)
     side = jnp.where(
         lane < 8,
@@ -189,28 +219,32 @@
     gram_ref[...] = jnp.concatenate([sums] * (gram_ref.shape[0] // 8), axis=0)
 
 
-def first_surface_kernel(
-    own_low, own_high, rows_e, rows_w, cols_n, cols_s, ne, nw, se, sw, basis, gram, fixed
-):
-    fields = [
+def surface_fields(low, high, rows_e, rows_w, cols_n, cols_s, count):
+    corners = count + 1 if count == 3 else 3
+    first = 2 * corners
+
+    def column(cols):
+        own = cols.shape[0] - 2 * corners
+        return [cols[0], cols[1], cols[own], cols[own + corners]]
+
+    return [
         wide_surface(
-            n, jnp.concatenate([own_low[n], own_high[n]], axis=0),
-            rows_e, rows_w, cols_n, cols_s, ne, nw, se, sw,
+            n, jnp.concatenate([low[first + n], high[first + n]], axis=0),
+            rows_e[first + n], rows_w[first + n], column(cols_n), column(cols_s),
         )
-        for n in range(3)
+        for n in range(count)
     ]
-    fixed[0] = fields[1]
-    fixed[1] = fields[2]
-    krylov(fields[0], fields[2], fields[1], basis, gram)
-
-
-def next_surface_kernel(
-    own_low, own_high, rows_e, rows_w, cols_n, cols_s, ne, nw, se, sw, fixed, basis, gram
-):
-    c = wide_surface(
-        0, jnp.concatenate([own_low[0], own_high[0]], axis=0),
-        rows_e, rows_w, cols_n, cols_s, ne, nw, se, sw,
-    )
+
+
+def first_surface_kernel(low, high, rows_e, rows_w, cols_n, cols_s, basis, gram, fixed):
+    c, depth, diag = surface_fields(low, high, rows_e, rows_w, cols_n, cols_s, 3)
+    fixed[0] = depth
+    fixed[1] = diag
+    krylov(c, diag, depth, basis, gram)
+
+
+def next_surface_kernel(low, high, rows_e, rows_w, cols_n, cols_s, fixed, basis, gram):
+    (c,) = surface_fields(low, high, rows_e, rows_w, cols_n, cols_s, 1)
     krylov(c, fixed[1], fixed[0], basis, gram)
 
 
@@ -261,34 +295,36 @@
 def step_kernel(
     final,
     mix, thermal, haline, temp, salt, east, north, mask, bottom, diag, basis, gathered,
-    a_rows_e, a_rows_w, a_cols_n, a_cols_s, a_ne, a_nw, a_se, a_sw,
+    a_rows_e, a_rows_w, a_cols_n, a_cols_s,
     *rest,
 ):
     if final:
-        (t_rows_e, t_rows_w, t_cols_n, t_cols_s, t_ne, t_nw, t_se, t_sw,
+        (t_rows_e, t_rows_w, t_cols_n, t_cols_s,
          new_temp, new_salt, new_surface,
          wet_wide, part_t, part_s, ratios, sides) = rest
-        skip = 1
+        skip = 7
     else:
         (new_temp, new_salt, new_surface, row_low, row_high, col_low, col_high,
-         c_sw, c_se, c_nw, c_ne,
          wet_wide, part_t, part_s, ratios, sides) = rest
-        t_rows_e, t_rows_w, t_cols_n, t_cols_s, t_ne, t_nw, t_se, t_sw = (
-            a_rows_e, a_rows_w, a_cols_n, a_cols_s, a_ne, a_nw, a_se, a_sw
-        )
-        skip = 3
+        t_rows_e, t_rows_w, t_cols_n, t_cols_s = a_rows_e, a_rows_w, a_cols_n, a_cols_s
+        skip = 11
     sub = iota((8, COLS), 0)
     lane = iota((24, COLS), 1)
 
-    def set_side(n, block, cols, first, second):
-        sides[n, :ROWS, :] = cols[block]
-        sides[n, ROWS:, :] = jnp.where(sub < 4, first[block], second[block])
+    def set_side(n, block, cols):
+        corners = (cols.shape[0] - 10) // 2 if cols.shape[0] == 18 else 3
+        own = cols.shape[0] - 2 * corners
+        sides[n, :8, :] = cols[2 * block]
+        sides[n, 8:ROWS, :] = cols[2 * block + 1]
+        sides[n, ROWS:, :] = jnp.where(sub < 4, cols[own + block], cols[own + corners + block])
 
     for n, block in enumerate((1, 2)):
-        set_side(2 * n, block, t_cols_n, t_ne, t_nw)
-        set_side(2 * n + 1, block, t_cols_s, t_se, t_sw)
-    set_side(4, 3, a_cols_n, a_ne, a_nw)
-    set_side(5, 3, a_cols_s, a_se, a_sw)
+        set_side(2 * n, block, t_cols_n)
+        set_side(2 * n + 1, block, t_cols_s)
+    set_side(4, 3, a_cols_n)
+    set_side(5, 3, a_cols_s)
+    north_n = jnp.concatenate([a_cols_n[8], a_cols_n[9]], axis=0)
+    north_s = jnp.concatenate([a_cols_s[8], a_cols_s[9]], axis=0)
 
     def beyond(north_side, south_side, level, rows):
         shift = COLS - 2 * level
@@ -312,7 +348,7 @@
             level = group * 4 + j
             wet = jnp.where(last > level, mask[level], 0).astype(F32)
             wet_wide[level] = widened(
-                wet, a_rows_e, a_rows_w, 3 + 2 * GROUPS + group, j, 4, level
+                wet, a_rows_e, a_rows_w, 11 + 2 * GROUPS + group, j, 4, level
             )
         return 0
 
@@ -371,10 +407,10 @@
             we, ww = ends(wet)
             wn, ws = flanks(wet)
             around = wet * ((we + ww) + (wn + ws))
-            at = 3 + 3 * GROUPS + group
+            at = 11 + 3 * GROUPS + group
             fe = jnp.concatenate([east[level], end_rows(a_rows_e, a_rows_w, at, j)], axis=0)
             fn = jnp.concatenate(
-                [north[level], beyond(a_cols_n[4], a_cols_s[4], level, ROWS)], axis=1
+                [north[level], beyond(north_n, north_s, level, ROWS)], axis=1
             )
             own = slice(0, ROWS), slice(0, COLS)
             wet_own = wet[own]
@@ -407,7 +443,7 @@
             if not final:
                 total = total + wet_own * (thermal[level] * t - haline[level] * s)
                 for field, cells in enumerate(done):
-                    put_rows(row_low, row_high, 1, field, group, j, cells)
+                    put_rows(row_low, row_high, 7, field, group, j, cells)
                 packs = tuple(packed(acc, cells, level) for acc, cells in zip(packs, done))
         return xt, xs, total, packs
 
@@ -415,11 +451,10 @@
     packs = () if final else ((small, small), (small, small))
     xt, xs, total, packs = lax.fori_loop(0, GROUPS, backward, (zero, zero, small, packs))
     if not final:
+        refs = row_low, row_high, col_low, col_high
+        put_surface(refs, 6, (surface + total,))
         for n, (low, high) in enumerate(packs):
-            col_low[n + 1] = low
-            col_high[n + 1] = high
-        put_surface((row_low, row_high, col_low, col_high), (surface + total,))
-        put_corners(col_low, col_high, (c_sw, c_se, c_nw, c_ne), 3)
+            put_cols(refs, n + 1, low, high)
 
 
 def shape(*dims):
@@ -427,6 +462,7 @@
 
 
 VMEM = pl.BlockSpec(memory_space=pltpu.VMEM)
+HBM = pl.BlockSpec(memory_space=pltpu.HBM)
 SMEM = pl.BlockSpec(memory_space=pltpu.SMEM)
 
 
@@ -449,42 +485,41 @@
 
 
 def message_shapes(surfaces, row_fields, col_fields, corner_fields):
-    rows = shape(surfaces + GROUPS * row_fields, 8, COLS)
-    cols = shape(1 + col_fields, ROWS, COLS)
-    corner = shape(1 + corner_fields, 8, COLS)
-    return [rows, rows, cols, cols] + [corner] * 4
+    rows = shape(2 * (1 + corner_fields) + surfaces + GROUPS * row_fields, 8, COLS)
+    cols = shape(2 * (1 + col_fields), 8, COLS)
+    return [rows, rows, cols, cols]
 
 
 def solution(mesh):
     nx, ny = mesh.shape["gx"], mesh.shape["gy"]
     devices = nx * ny
     both = ("gx", "gy")
-
-    def route(di, dj):
-        return [
-            (i * ny + j, (i + di) % nx * ny + j + dj)
-            for i in range(nx)
-            for j in range(ny)
-            if 0 <= j + dj < ny
-        ]
-
-    def exchange(messages):
-        row_low, row_high, col_low, col_high, sw, se, nw, ne = messages
-        sends = (
-            (row_low, -1, 0), (row_high, 1, 0), (col_low, 0, -1), (col_high, 0, 1),
-            (sw, -1, -1), (se, 1, -1), (nw, -1, 1), (ne, 1, 1),
-        )
-        return [lax.ppermute(m, both, route(di, dj)) for m, di, dj in sends]
+    eastward = [(i, (i + 1) % nx) for i in range(nx)]
+    northward = [(j, j + 1) for j in range(ny - 1)]
+
+    def back(pairs):
+        return [(b, a) for a, b in pairs]
+
+    def exchange(messages, corners):
+        row_low, row_high, col_low, col_high = messages
+        rows_e = lax.ppermute(row_low, "gx", back(eastward))
+        rows_w = lax.ppermute(row_high, "gx", eastward)
+        own = col_low.shape[0]
+        out = shape(own + 2 * corners, 8, COLS)
+        to_south, to_north = call(
+            forward_kernel, [out, out],
+            [head(own, 8, COLS)] * 2 + [head(2 * corners, 8, COLS)] * 2,
+            [head(*out.shape)] * 2, name="corners", grid=(1,),
+        )(col_low, col_high, rows_e, rows_w)
+        cols_n = lax.ppermute(to_south, "gy", back(northward))
+        cols_s = lax.ppermute(to_north, "gy", northward)
+        return [rows_e, rows_w, cols_n, cols_s]
 
     def all_sum(block):
         return lax.all_to_all(block, both, 0, 0, tiled=True)
 
-    def surface_specs(count):
-        return (
-            [head(count, 8, COLS)] * 4
-            + [head(1, ROWS, COLS)] * 2
-            + [head(1, 8, COLS)] * 4
-        )
+    def surface_specs(rows, cols):
+        return [head(rows, 8, COLS)] * 4 + [head(cols, 8, COLS)] * 2
 
     basis_shape = shape(4, 32, 2 * COLS)
     gram_shape = shape(devices, COLS)
@@ -499,16 +534,22 @@
         thermal_weight, haline_weight, surface_diag, land_mask, bottom_level,
     ):
         first = call(
-            prepare_kernel, message_shapes(3, 4, 4, 3), [SMEM] * 2 + [VMEM] * 8, name="prepare"
+            prepare_kernel, message_shapes(3, 4, 4, 3), [SMEM] * 2 + [HBM] * 5 + [VMEM] * 3,
+            scratch=[pltpu.VMEM((LEVELS, ROWS, COLS), F32)] * 4
+            + [
+                pltpu.VMEM((LEVELS, ROWS, COLS), jnp.int32),
+                pltpu.SemaphoreType.DMA((5, LEVELS // CHUNK)),
+            ],
+            name="prepare",
         )(
             thermal_weight, haline_weight, sens_temp, sens_salt, flow_east, flow_north,
             land_mask, bottom_level, sens_surface, surface_diag,
         )
-        got = exchange(first)
+        got = exchange(first, 4)
         basis, gram, fixed = call(
             first_surface_kernel,
             [basis_shape, gram_shape, shape(2, 32, 2 * COLS)],
-            surface_specs(3),
+            surface_specs(11, 18),
             [whole(4, 32, 2 * COLS), whole(devices, COLS), whole(2, 32, 2 * COLS)],
             name="first_surface",
             grid=(1,),
@@ -527,7 +568,7 @@
             return call(
                 functools.partial(step_kernel, final),
                 outs,
-                [SMEM] * 3 + [VMEM] * (17 + len(more)),
+                [SMEM] * 3 + [VMEM] * (13 + len(more)),
                 scratch=scratch,
                 name="last_step" if final else "first_step",
             )(
@@ -539,11 +580,11 @@
             False, sens_temp, sens_salt, basis, gathered, [],
             [field, field, tile] + message_shapes(1, 2, 2, 2),
         )
-        more = exchange(second)
+        more = exchange(second, 3)
         basis, gram = call(
             next_surface_kernel,
             [basis_shape, gram_shape],
-            surface_specs(1) + [whole(2, 32, 2 * COLS)],
+            surface_specs(7, 12) + [whole(2, 32, 2 * COLS)],
             [whole(4, 32, 2 * COLS), whole(devices, COLS)],
             name="next_surface",
             grid=(1,),

time: 160 us -> 129 us (0.81)
  starting transfers between devices: 42.9 us -> 15.9 us
  blocking collectives: 66.7 us -> 58.7 us
  Pallas kernels: 32.3 us -> 34.8 us
  waiting for transfers between devices: 6.92 us -> 9.05 us
    ppermute x16 -> x8, starting transfers between devices: 42.9 us -> 15.9 us  [the longest x2 8.16 us: exchange(): cols_s = lax.ppermute(to_north, 'gy', northward)]
    all_to_all x2, blocking collectives: 66.7 us -> 58.7 us  [all_sum(): return lax.all_to_all(block, both, 0, 0, tiled=True)]
    pallas_call x2 -> x4, Pallas kernels: 2.95 us -> 5.71 us  [the longest x1 5.01 us: per_device(): call(prepare_kernel, message_shapes(3, 4, 4, 3), [SMEM] * 2 + [HBM] * 5 +...]
    ppermute x16 -> x8, waiting for transfers between devices: 6.92 us -> 9.05 us  [the longest x2 5.88 us: exchange(): rows_e = lax.ppermute(row_low, 'gx', back(eastward))]
  transfers between devices with their start and end apart: 16 -> 8, of which waited for: 5 -> 6; matrix products, arithmetic and copies ran while one was open for 0% -> 0% of each run, Pallas kernels for 0% -> 0%
where the time goes in v2:
time: 129 us; the launch traced here: 128 us
  blocking collectives  58.7 us (46%)
  Pallas kernels  34.8 us (27%)
  starting transfers between devices  15.9 us (12%)
  waiting for transfers between devices  9.05 us (7%)
  local copies, waits for them, and re-layouts  9.02 us (7%)
    all_to_all x2, blocking collectives, all_sum(): return lax.all_to_all(block, both, 0, 0, tiled=True)  58.7 us
    pallas_call x2, Pallas kernels, step(): call(functools.partial(step_kernel, final), outs, [SMEM] * 3 + [VMEM] * (...  28.4 us
    unnamed x34, local copies, waits for them, and re-layouts  9.02 us
    ppermute x2, starting transfers between devices, exchange(): cols_s = lax.ppermute(to_north, 'gy', northward)  8.16 us
    ppermute x2, waiting for transfers between devices, exchange(): rows_e = lax.ppermute(row_low, 'gx', back(eastward))  5.88 us
    pallas_call x1, Pallas kernels, per_device(): call(prepare_kernel, message_shapes(3, 4, 4, 3), [SMEM] * 2 + [HBM] * 5 +...  5.01 us
    ppermute x2, starting transfers between devices, exchange(): rows_e = lax.ppermute(row_low, 'gx', back(eastward))  3.91 us
    ppermute x2, starting transfers between devices, exchange(): cols_n = lax.ppermute(to_south, 'gy', back(northward))  2.72 us
  transfers between devices with their start and end apart: 8, of which 6 were waited for; matrix products, arithmetic and copies ran while one was open for 0% of the time, Pallas kernels for 0%

profile of v2, /device:TPU:1, one launch (start us, length us, event | category | flops | bytes accessed | tf_op | source)
XLA Modules:
  0.0 128.2 jit_solution(11784970983582767937)
XLA Ops:
  0.6 0.0 copy-start
  0.6 1.0 copy-done
  1.6 0.0 copy-start.2
  1.6 1.0 copy-done.2
  2.6 0.0 copy-start.4
  2.6 1.0 copy-done.4
  3.6 0.0 copy-start.6
  3.6 1.0 copy-done.6
  4.6 0.0 copy-start.8
  4.6 1.0 copy-done.8
  5.6 0.0 copy-start.10
  5.6 0.7 copy-done.10
  6.3 0.0 copy-start.11
  6.3 0.7 copy-done.11
  7.0 0.0 copy-start.13
  7.0 0.7 copy-done.13
  7.7 0.0 copy-start.14
  7.7 0.7 copy-done.14
  8.4 0.0 copy-start.15
  8.4 0.7 copy-done.15
  9.0 5.0 %prepare.1 = (f32[59,8,128]{2,1,0:T(8,128)S(1)}, f32[59,8,128]{2,1,0:T(8,128)S(1)}, f32[10,8,128]{2,1,0:T(8,128)S(1)}, f32[10,8,128]{2,1,0:T(8,128)S(1)}) custom-call(f32[48]{0:T(128)S(1)} %copy-done.14, f32[48]{0:T(128)S(1)} %copy-done.15, f32[48,16,128]{2,1,0:T(8,128)S(1)} %copy-done.6, f32[48,16,128]{2,1,0:T(8,128)S(1)} %copy-done.8, ...), custom_call_target="tpu_custom_call" | custom-call | tf_op jit(solution)/shard_map/prepare/pallas_call | solution.py:536
  14.0 3.3 %collective-permute-start = (f32[59,8,128]{2,1,0:T(8,128)S(1)}, f32[59,8,128]{2,1,0:T(8,128)S(1)}, u32[]{:S(2)}, u32[]{:S(2)}) collective-permute-start(f32[59,8,128]{2,1,0:T(8,128)S(1)} %get-tuple-element.22.low), channel_id=1, source_target_pairs={{8,0},{16,8},{24,16},{32,24},{40,32},{48,40},{56,48},{64,56},{72,6... | collective-permute-start | bytes 725000 | tf_op jit(solution)/shard_map/ppermute | solution.py:505
  17.4 0.0 collective-permute-start.1
  17.4 3.3 %collective-permute-done.rows_e.a_rows_e = f32[59,8,128]{2,1,0:T(8,128)S(1)} collective-permute-done((f32[59,8,128]{2,1,0:T(8,128)S(1)}, f32[59,8,128]{2,1,0:T(8,128)S(1)}, u32[]{:S(2)}, u32[]{:S(2)}) %collective-permute-start) | collective-permute-done | bytes 241696 | tf_op jit(solution)/shard_map/ppermute | solution.py:505
  20.6 0.6 collective-permute-done.1.rows_w.a_rows_w
  21.3 0.0 copy-start.9
  21.3 1.4 %collective-permute-start.2 = (f32[18,8,128]{2,1,0:T(8,128)S(1)}, f32[18,8,128]{2,1,0:T(8,128)S(1)}, u32[]{:S(2)}, u32[]{:S(2)}) collective-permute-start(f32[18,8,128]{2,1,0:T(8,128)S(1)} %get-tuple-element.26), channel_id=1, source_target_pairs={{1,0},{2,1},{3,2},{4,3},{5,4},{6,5},{7,6},{9,8},{10,9},{11,10},{12... | collective-permute-start | bytes 221192 | tf_op jit(solution)/shard_map/ppermute | solution.py:514
  22.7 4.2 %collective-permute-start.3 = (f32[18,8,128]{2,1,0:T(8,128)S(1)}, f32[18,8,128]{2,1,0:T(8,128)S(1)}, u32[]{:S(2)}, u32[]{:S(2)}) collective-permute-start(f32[18,8,128]{2,1,0:T(8,128)S(1)} %get-tuple-element.27), channel_id=1, source_target_pairs={{0,1},{1,2},{2,3},{3,4},{4,5},{5,6},{6,7},{8,9},{9,10},{10,11},{11... | collective-permute-start | bytes 221192 | tf_op jit(solution)/shard_map/ppermute | solution.py:515
  26.9 0.1 collective-permute-done.2.cols_n.a_cols_n
  27.0 1.3 %collective-permute-done.3.cols_s.a_cols_s = f32[18,8,128]{2,1,0:T(8,128)S(1)} collective-permute-done((f32[18,8,128]{2,1,0:T(8,128)S(1)}, f32[18,8,128]{2,1,0:T(8,128)S(1)}, u32[]{:S(2)}, u32[]{:S(2)}) %collective-permute-start.3) | collective-permute-done | bytes 73760 | tf_op jit(solution)/shard_map/ppermute | solution.py:515
  28.3 0.0 copy-start.1
  28.3 0.0 copy-start.3
  28.3 0.0 copy-start.7
  28.3 0.7 first_surface.1
  29.0 0.0 copy-start.12
  29.0 32.4 %all_to_all.22 = f32[256,1,128]{2,1,0:T(1,128)S(1)} all-to-all(f32[256,1,128]{2,1,0:T(1,128)S(1)} %bitcast.10), channel_id=1, replica_groups=mesh['gx'=32,'gy'=8] {'gx','gy'}, dimensions={0} | all-to-all | bytes 262144 | tf_op jit(solution)/shard_map/all_to_all | solution.py:519
  61.4 0.0 copy-start.16
  61.4 0.0 copy-done.9
  61.4 0.0 copy-done.1
  61.4 0.0 copy-done.3
  61.4 0.0 copy-done.7
  61.4 0.0 copy-done.12
  61.4 0.6 copy-done.16
  62.1 14.5 %first_step.1 = (f32[48,16,128]{2,1,0:T(8,128)S(1)}, f32[48,16,128]{2,1,0:T(8,128)S(1)}, f32[16,128]{1,0:T(8,128)}, f32[31,8,128]{2,1,0:T(8,128)S(1)}, f32[31,8,...) custom-call(f32[48]{0:T(128)S(1)} %copy-done.16, f32[48]{0:T(128)S(1)} %copy-done.14, ...), custom_call_target="tpu_custom_call" | custom-call | tf_op jit(solution)/shard_map/first_step/pallas_call | solution.py:568
  76.5 0.6 collective-permute-start.4
  77.1 1.2 collective-permute-start.5
  78.3 2.6 %collective-permute-done.4.rows_e.rest_0_ = f32[31,8,128]{2,1,0:T(8,128)S(1)} collective-permute-done((f32[31,8,128]{2,1,0:T(8,128)S(1)}, f32[31,8,128]{2,1,0:T(8,128)S(1)}, u32[]{:S(2)}, u32[]{:S(2)}) %collective-permute-start.4) | collective-permute-done | bytes 127008 | tf_op jit(solution)/shard_map/ppermute | solution.py:505
  80.9 0.0 collective-permute-done.5.rows_w.rest_1_
  80.9 1.3 %collective-permute-start.6 = (f32[12,8,128]{2,1,0:T(8,128)S(1)}, f32[12,8,128]{2,1,0:T(8,128)S(1)}, u32[]{:S(2)}, u32[]{:S(2)}) collective-permute-start(f32[12,8,128]{2,1,0:T(8,128)S(1)} %get-tuple-element.36), channel_id=1, source_target_pairs={{1,0},{2,1},{3,2},{4,3},{5,4},{6,5},{7,6},{9,8},{10,9},{11,10},{12... | collective-permute-start | bytes 147464 | tf_op jit(solution)/shard_map/ppermute | solution.py:514
  82.2 4.0 %collective-permute-start.7 = (f32[12,8,128]{2,1,0:T(8,128)S(1)}, f32[12,8,128]{2,1,0:T(8,128)S(1)}, u32[]{:S(2)}, u32[]{:S(2)}) collective-permute-start(f32[12,8,128]{2,1,0:T(8,128)S(1)} %get-tuple-element.37), channel_id=1, source_target_pairs={{0,1},{1,2},{2,3},{3,4},{4,5},{5,6},{6,7},{8,9},{9,10},{10,11},{11... | collective-permute-start | bytes 147464 | tf_op jit(solution)/shard_map/ppermute | solution.py:515
  86.2 0.0 collective-permute-done.6.cols_n.rest_2_
  86.2 1.1 collective-permute-done.7.cols_s.rest_3_
  87.3 0.0 copy-start.5
  87.3 0.7 next_surface.1
  88.0 26.2 %all_to_all.23 = f32[256,1,128]{2,1,0:T(1,128)S(1)} all-to-all(f32[256,1,128]{2,1,0:T(1,128)S(1)} %bitcast.11), channel_id=1, replica_groups=mesh['gx'=32,'gy'=8] {'gx','gy'}, dimensions={0} | all-to-all | bytes 262144 | tf_op jit(solution)/shard_map/all_to_all | solution.py:519
  114.3 0.0 copy-done.5
  114.3 14.0 %last_step.1 = (f32[48,16,128]{2,1,0:T(8,128)}, f32[48,16,128]{2,1,0:T(8,128)}, f32[16,128]{1,0:T(8,128)}) custom-call(f32[48]{0:T(128)S(1)} %copy-done.16, f32[48]{0:T(128)S(1)} %copy-done.14, f32[48]{0:T(128)S(1)} %copy-done.15, f32[48,16,128]{2,1,0:T(8,128)S(1)} %get-tuple-element.30.temp, f32[48,16,128]{2,1,0:T(8,128)S(1)} %get-tuple-element.31.salt, ...), custom_call_target="tpu_custom_call" | custom-call | tf_op jit(solution)/shard_map/last_step/pallas_call | solution.py:568
  (2 shorter events, 0.0 us)
Async XLA Ops:
  0.6 1.0 copy-start
  1.6 1.0 copy-start.2
  2.6 1.0 copy-start.4
  3.6 1.0 copy-start.6
  4.6 1.0 copy-start.8
  5.6 0.7 copy-start.10
  6.3 0.7 copy-start.11
  7.0 0.7 copy-start.13
  7.7 0.7 copy-start.14
  8.4 0.7 copy-start.15
  14.0 6.6 %collective-permute-start = (f32[59,8,128]{2,1,0:T(8,128)S(1)}, f32[59,8,128]{2,1,0:T(8,128)S(1)}, u32[]{:S(2)}, u32[]{:S(2)}) collective-permute-start(f32[59,8,128]{2,1,0:T(8,128)S(1)} %get-tuple-element.22.low), channel_id=1, source_target_pairs={{8,0},{16,8},{24,16},{32,24},{40,32},{48,40},{56,48},{64,56},{72,6... | collective-permute-start | bytes 725000 | tf_op jit(solution)/shard_map/ppermute | solution.py:505
  17.4 3.9 %collective-permute-start.1 = (f32[59,8,128]{2,1,0:T(8,128)S(1)}, f32[59,8,128]{2,1,0:T(8,128)S(1)}, u32[]{:S(2)}, u32[]{:S(2)}) collective-permute-start(f32[59,8,128]{2,1,0:T(8,128)S(1)} %get-tuple-element.23.high), channel_id=1, source_target_pairs={{0,8},{8,16},{16,24},{24,32},{32,40},{40,48},{48,56},{56,64},{64,7... | collective-permute-start | bytes 725000 | tf_op jit(solution)/shard_map/ppermute | solution.py:506
  21.3 40.1 %copy-start.9 = (f32[48,16,128]{2,1,0:T(8,128)S(1)}, f32[48,16,128]{2,1,0:T(8,128)}, u32[]{:S(2)}) copy-start(f32[48,16,128]{2,1,0:T(8,128)} %salt.1) | copy-start | bytes 1179652
  21.3 5.7 %collective-permute-start.2 = (f32[18,8,128]{2,1,0:T(8,128)S(1)}, f32[18,8,128]{2,1,0:T(8,128)S(1)}, u32[]{:S(2)}, u32[]{:S(2)}) collective-permute-start(f32[18,8,128]{2,1,0:T(8,128)S(1)} %get-tuple-element.26), channel_id=1, source_target_pairs={{1,0},{2,1},{3,2},{4,3},{5,4},{6,5},{7,6},{9,8},{10,9},{11,10},{12... | collective-permute-start | bytes 221192 | tf_op jit(solution)/shard_map/ppermute | solution.py:514
  22.7 5.6 %collective-permute-start.3 = (f32[18,8,128]{2,1,0:T(8,128)S(1)}, f32[18,8,128]{2,1,0:T(8,128)S(1)}, u32[]{:S(2)}, u32[]{:S(2)}) collective-permute-start(f32[18,8,128]{2,1,0:T(8,128)S(1)} %get-tuple-element.27), channel_id=1, source_target_pairs={{0,1},{1,2},{2,3},{3,4},{4,5},{5,6},{6,7},{8,9},{9,10},{10,11},{11... | collective-permute-start | bytes 221192 | tf_op jit(solution)/shard_map/ppermute | solution.py:515
  28.3 33.1 %copy-start.1 = (f32[48,16,128]{2,1,0:T(8,128)S(1)}, f32[48,16,128]{2,1,0:T(8,128)}, u32[]{:S(2)}) copy-start(f32[48,16,128]{2,1,0:T(8,128)} %east.3) | copy-start | bytes 1179652
  28.3 33.1 %copy-start.3 = (f32[48,16,128]{2,1,0:T(8,128)S(1)}, f32[48,16,128]{2,1,0:T(8,128)}, u32[]{:S(2)}) copy-start(f32[48,16,128]{2,1,0:T(8,128)} %north.3) | copy-start | bytes 1179652
  28.3 33.1 %copy-start.7 = (f32[48,16,128]{2,1,0:T(8,128)S(1)}, f32[48,16,128]{2,1,0:T(8,128)}, u32[]{:S(2)}) copy-start(f32[48,16,128]{2,1,0:T(8,128)} %temp.1) | copy-start | bytes 1179652
  29.0 32.5 %copy-start.12 = (f32[16,128]{1,0:T(8,128)S(1)}, f32[16,128]{1,0:T(8,128)}, u32[]{:S(2)}) copy-start(f32[16,128]{1,0:T(8,128)} %diag.5) | copy-start | bytes 24580
  61.4 0.7 copy-start.16
  76.5 4.3 %collective-permute-start.4 = (f32[31,8,128]{2,1,0:T(8,128)S(1)}, f32[31,8,128]{2,1,0:T(8,128)S(1)}, u32[]{:S(2)}, u32[]{:S(2)}) collective-permute-start(f32[31,8,128]{2,1,0:T(8,128)S(1)} %get-tuple-element.32.low), channel_id=1, source_target_pairs={{8,0},{16,8},{24,16},{32,24},{40,32},{48,40},{56,48},{64,56},{72,6... | collective-permute-start | bytes 380936 | tf_op jit(solution)/shard_map/ppermute | solution.py:505
  77.1 3.8 %collective-permute-start.5 = (f32[31,8,128]{2,1,0:T(8,128)S(1)}, f32[31,8,128]{2,1,0:T(8,128)S(1)}, u32[]{:S(2)}, u32[]{:S(2)}) collective-permute-start(f32[31,8,128]{2,1,0:T(8,128)S(1)} %get-tuple-element.33.high), channel_id=1, source_target_pairs={{0,8},{8,16},{16,24},{24,32},{32,40},{40,48},{48,56},{56,64},{64,7... | collective-permute-start | bytes 380936 | tf_op jit(solution)/shard_map/ppermute | solution.py:506
  80.9 5.3 %collective-permute-start.6 = (f32[12,8,128]{2,1,0:T(8,128)S(1)}, f32[12,8,128]{2,1,0:T(8,128)S(1)}, u32[]{:S(2)}, u32[]{:S(2)}) collective-permute-start(f32[12,8,128]{2,1,0:T(8,128)S(1)} %get-tuple-element.36), channel_id=1, source_target_pairs={{1,0},{2,1},{3,2},{4,3},{5,4},{6,5},{7,6},{9,8},{10,9},{11,10},{12... | collective-permute-start | bytes 147464 | tf_op jit(solution)/shard_map/ppermute | solution.py:514
  82.2 5.2 %collective-permute-start.7 = (f32[12,8,128]{2,1,0:T(8,128)S(1)}, f32[12,8,128]{2,1,0:T(8,128)S(1)}, u32[]{:S(2)}, u32[]{:S(2)}) collective-permute-start(f32[12,8,128]{2,1,0:T(8,128)S(1)} %get-tuple-element.37), channel_id=1, source_target_pairs={{0,1},{1,2},{2,3},{3,4},{4,5},{5,6},{6,7},{8,9},{9,10},{10,11},{11... | collective-permute-start | bytes 147464 | tf_op jit(solution)/shard_map/ppermute | solution.py:515
  87.3 26.9 %copy-start.5 = (s32[48,16,128]{2,1,0:T(8,128)S(1)}, s32[48,16,128]{2,1,0:T(8,128)}, u32[]{:S(2)}) copy-start(s32[48,16,128]{2,1,0:T(8,128)} %mask.3) | copy-start | bytes 1179652

commit v3 on v2

v3 whole, which is shorter than its diff:
```python
import functools

import jax
import jax.numpy as jnp
from jax import lax
from jax.experimental import pallas as pl
from jax.experimental.pallas import tpu as pltpu
from jax.sharding import PartitionSpec as P

LEVELS = 48
ROWS = 16
COLS = 128
GROUPS = LEVELS // 4
CHUNK = 12
F32 = jnp.float32
PAIRS = [(i, j) for i in range(4) for j in range(i, 5)]


def two_sum(a, b):
    s = a + b
    t = s - a
    return s, (a - (s - t)) + (b - t)


def fast_two_sum(a, b):
    s = a + b
    return s, b - (s - a)


def split(a):
    c = a * 4097.0
    high = c - (c - a)
    return high, a - high


def two_prod(a, b, a_parts=None, b_parts=None):
    ah, al = split(a) if a_parts is None else a_parts
    bh, bl = split(b) if b_parts is None else b_parts
    p = a * b
    return p, ((ah * bh - p) + ah * bl + al * bh) + al * bl


def pair_add(x, y):
    s, t = two_sum(x[0], y[0])
    return fast_two_sum(s, t + (x[1] + y[1]))


def pair_mul(x, y):
    p, e = two_prod(x[0], y[0])
    return fast_two_sum(p, e + (x[0] * y[1] + x[1] * y[0]))


def pair_neg(x):
    return -x[0], -x[1]


def pair_div(x, y):
    first = x[0] / y[0]
    p, e = two_prod(first, y[0])
    rest = ((x[0] - p) - e + x[1]) - first * y[1]
    return fast_two_sum(first, rest / y[0])


def roll(x, shift, axis):
    shift = shift % x.shape[axis]
    return x if shift == 0 else pltpu.roll(x, shift, axis)


def iota(shape, axis):
    return lax.broadcasted_iota(jnp.int32, shape, axis)


A_CORNERS, T_CORNERS = 6, 3
A_SURFACE, T_SURFACE = 2 * A_CORNERS, 2 * T_CORNERS
A_ROWS, T_ROWS = A_SURFACE + 3, T_SURFACE + 1


def put_rows(low_ref, high_ref, first, field, group, j, cells):
    at = first + field * GROUPS + group
    low_ref[at, 2 * j : 2 * j + 2, :] = cells[:2]
    high_ref[at, 2 * j : 2 * j + 2, :] = cells[ROWS - 2 :]


def packed(acc, cells, level):
    low, high = acc
    mine = lax.shift_right_logical(iota((ROWS, COLS), 1), 1) == level
    low = jnp.where(mine, pltpu.roll(cells, 2 * level, 1), low)
    high = jnp.where(mine, pltpu.roll(cells, 2 * level + 2, 1), high)
    return low, high


def put_surface(refs, first, fields):
    row_low, row_high, col_low, col_high = refs
    low = jnp.zeros((ROWS, COLS), F32)
    high = low
    lane_group = iota((ROWS, COLS), 1) // 8
    for n, cells in enumerate(fields):
        row_low[first + n] = cells[:8]
        row_high[first + n] = cells[8:]
        low = jnp.where(lane_group == n, roll(cells, 8 * n, 1), low)
        high = jnp.where(lane_group == n, roll(cells, 8 * n + 8, 1), high)
    put_cols(refs, 0, low, high)


def put_cols(refs, n, low, high):
    row_low, row_high, col_low, col_high = refs
    count = corners_of(row_low)
    for col, side, cells in ((col_low, 0, low), (col_high, count, high)):
        col[2 * n] = cells[:8]
        col[2 * n + 1] = cells[8:]
        if n < count:
            row_low[side + n] = cells[:8]
            row_high[side + n] = cells[8:]


def corners_of(rows):
    return A_CORNERS if rows.shape[0] == A_ROWS + 6 * GROUPS else T_CORNERS


def forward_kernel(own_low, own_high, rows_e, rows_w, to_south, to_north):
    count = rows_e.shape[0] // 2
    own = own_low.shape[0]
    for out, mine, side in ((to_south, own_low, 0), (to_north, own_high, count)):
        out[:own] = mine[...]
        out[own : own + count] = rows_e[side : side + count]
        out[own + count :] = rows_w[side : side + count]


def wet_at(mask, last, level):
    return jnp.where(last > level, mask[jnp.minimum(level, LEVELS - 1)], 0).astype(F32)


def prepare_kernel(
    mix, thermal, haline, temp_in, salt_in, east_in, north_in, mask_in, bottom, surface, diag,
    row_low, row_high, col_low, col_high, *rest,
):
    solved, (inverses, ratios, temp, salt, east, north, mask, sems) = rest[:4], rest[4:]
    last = bottom[...]
    zero = jnp.zeros((ROWS, COLS), F32)
    pair = (zero, zero)
    fields = list(
        zip((mask_in, temp_in, salt_in, east_in, north_in), (mask, temp, salt, east, north))
    )

    def copy(n, part):
        source, target = fields[n]
        levels = pl.ds(part * CHUNK, CHUNK)
        return pltpu.make_async_copy(source.at[levels], target.at[levels], sems.at[n, part])

    parts = LEVELS // CHUNK
    for part in range(parts):
        copy(0, part).start()
    for part in range(parts):
        for n in range(1, 5):
            copy(n, part).start()

    def down_body(group, carry):
        total, depth, up, ratio, values, wet, packs = carry
        for j in range(4):
            level = group * 4 + j
            below = wet_at(mask, last, level + 1)
            down = mix[level] * (wet * below)
            inverse = 1.0 / ((1.0 + up + down) - up * ratio)
            t, s = temp[level], salt[level]
            tw, hw = thermal[level] * wet, haline[level] * wet
            total = total + (tw * t - hw * s)
            depth = depth + wet
            values = tuple((r + up * v) * inverse for r, v in zip((t, s, tw, hw), values))
            for ref, v in zip(solved, values):
                ref[level] = v
            ratio = down * inverse
            inverses[level] = inverse
            ratios[level] = ratio
            put_rows(row_low, row_high, A_ROWS, 2, group, j, wet)
            put_rows(row_low, row_high, A_ROWS, 5, group, j, east[level])
            packs = tuple(packed(acc, v, level) for acc, v in zip(packs, (wet, north[level])))
            up = down
            wet = below
        return total, depth, up, ratio, values, wet, packs

    for part in range(parts):
        copy(0, part).wait()
    carry = (zero, zero, zero, zero, (zero,) * 4, wet_at(mask, last, 0), (pair, pair))
    step = CHUNK // 4
    for part in range(parts):
        for n in range(1, 5):
            copy(n, part).wait()
        carry = lax.fori_loop(part * step, (part + 1) * step, down_body, carry)
    total, depth, _, _, _, _, packs = carry
    refs = row_low, row_high, col_low, col_high
    put_surface(refs, A_SURFACE, (surface[...] + total, depth / LEVELS, diag[...]))
    put_cols(refs, 3, *packs[0])
    put_cols(refs, 6, *packs[1])
    back_substitute(refs, A_ROWS, solved, ratios, ((0, 1), (1, 2), (3, 4), (4, 5)))


def back_substitute(refs, first, solved, ratios, places):
    row_low, row_high = refs[:2]
    zero = jnp.zeros((ROWS, COLS), F32)

    def up_body(count, carry):
        values, packs = carry
        group = GROUPS - 1 - count
        for j in (3, 2, 1, 0):
            level = group * 4 + j
            ratio = ratios[level]
            values = tuple(ref[level] + ratio * v for ref, v in zip(solved, values))
            for ref, v, (field, _) in zip(solved, values, places):
                ref[level] = v
                put_rows(row_low, row_high, first, field, group, j, v)
            packs = tuple(packed(acc, v, level) for acc, v in zip(packs, values))
        return values, packs

    n = len(places)
    _, packs = lax.fori_loop(0, GROUPS, up_body, ((zero,) * n, ((zero, zero),) * n))
    for (_, block), acc in zip(places, packs):
        put_cols(refs, block, *acc)


def wide_surface(n, own, rows_e, rows_w, from_north, from_south):
    main = jnp.concatenate([own, rows_e, rows_w], axis=0)
    to_north = jnp.concatenate(from_north, axis=0)
    to_south = jnp.concatenate(from_south, axis=0)
    lane = iota((32, COLS), 1)
    side = jnp.where(
        lane < 8,
        roll(to_north, -8 * n, 1),
        jnp.where(lane >= COLS - 8, roll(to_south, 120 - 8 * n, 1), 0.0),
    )
    return jnp.concatenate([main, side], axis=1)


def krylov(c, diag, depth, basis_ref, gram_ref):
    def nb(v):
        return pltpu.roll(v, 31, 0), pltpu.roll(v, 1, 0), pltpu.roll(v, 255, 1), pltpu.roll(v, 1, 1)

    faces = [jnp.minimum(depth, d) for d in nb(depth)]
    centre = (diag - 1.0) + ((faces[0] + faces[1]) + (faces[2] + faces[3]))
    v = c
    own = []
    for k in range(5):
        if k < 4:
            basis_ref[k] = v
        mine = v[:ROWS, :COLS]
        own.append((mine, split(mine)))
        if k < 4:
            e, w, n, s = nb(v)
            v = centre * v - ((faces[0] * e + faces[1] * w) + (faces[2] * n + faces[3] * s))
    highs, lows = [], []
    for i, j in PAIRS:
        p, e = two_prod(own[i][0], own[j][0], own[i][1], own[j][1])
        s, t = two_sum(p[:8], p[8:])
        highs.append(s)
        lows.append(t + (e[:8] + e[8:]))
    pad = [jnp.zeros((8, COLS), F32)] * (16 - len(PAIRS))
    high = jnp.concatenate(highs + pad, axis=0).T
    low = jnp.concatenate(lows + pad, axis=0).T
    parts = [(high[8 * n : 8 * n + 8], low[8 * n : 8 * n + 8]) for n in range(16)]
    while len(parts) > 1:
        parts = [pair_add(a, b) for a, b in zip(parts[::2], parts[1::2])]
    total = parts[0]
    for shift in (4, 2, 1):
        total = pair_add(total, tuple(roll(x, shift, 0) for x in total))
    total = pair_add(total, tuple(roll(x, 124, 1) for x in total))
    first_half = (iota((8, COLS), 1) % 8) < 4
    sums = jnp.where(first_half, total[0], roll(total[1], 4, 1))
    gram_ref[...] = jnp.concatenate([sums] * (gram_ref.shape[0] // 8), axis=0)


def surface_fields(low, high, rows_e, rows_w, cols_n, cols_s, count):
    corners = A_CORNERS if count == 3 else T_CORNERS
    first = 2 * corners

    def column(cols):
        own = cols.shape[0] - 2 * corners
        return [cols[0], cols[1], cols[own], cols[own + corners]]

    return [
        wide_surface(
            n, jnp.concatenate([low[first + n], high[first + n]], axis=0),
            rows_e[first + n], rows_w[first + n], column(cols_n), column(cols_s),
        )
        for n in range(count)
    ]


def first_surface_kernel(low, high, rows_e, rows_w, cols_n, cols_s, basis, gram, fixed):
    c, depth, diag = surface_fields(low, high, rows_e, rows_w, cols_n, cols_s, 3)
    fixed[0] = depth
    fixed[1] = diag
    krylov(c, diag, depth, basis, gram)


def next_surface_kernel(low, high, rows_e, rows_w, cols_n, cols_s, fixed, basis, gram):
    (c,) = surface_fields(low, high, rows_e, rows_w, cols_n, cols_s, 1)
    krylov(c, fixed[1], fixed[0], basis, gram)


def coefficients(gathered):
    parts = [(gathered[8 * n : 8 * n + 8], None) for n in range(gathered.shape[0] // 8)]
    parts = [(p, jnp.zeros_like(p)) for p, _ in parts]
    while len(parts) > 1:
        parts = [pair_add(a, b) for a, b in zip(parts[::2], parts[1::2])]
    total = parts[0]
    for shift in (4, 2, 1):
        total = pair_add(total, tuple(roll(x, shift, 0) for x in total))
    for shift in (4, 2, 1):
        total = pair_add(total, tuple(roll(x, COLS - shift, 1) for x in total))
    table = {}
    for n, (i, j) in enumerate(PAIRS):
        entry = tuple(jnp.broadcast_to(x[:, 8 * n : 8 * n + 1], (8, COLS)) for x in total)
        table[i, j] = table[j, i] = entry
    one = (jnp.ones((8, COLS), F32), jnp.zeros((8, COLS), F32))
    r, p, x = [one], [one], []
    rr = table[0, 0]
    for it in range(4):
        image = [p[0]] + [pair_add(p[k], p[k - 1]) for k in range(1, it + 1)] + [p[it]]
        dot = functools.reduce(
            pair_add, [pair_mul(table[it, k], image[k]) for k in range(it + 2)]
        )
        step = pair_div(rr, pair_mul(p[it], dot))
        x = [
            pair_add(x[k], pair_mul(step, p[k])) if k < len(x) else pair_mul(step, p[k])
            for k in range(it + 1)
        ]
        if it < 3:
            minus = pair_neg(step)
            moved = [pair_mul(minus, a) for a in image]
            r = [pair_add(r[k], moved[k]) if k < len(r) else moved[k] for k in range(it + 2)]
            dot = functools.reduce(
                pair_add, [pair_mul(table[it + 1, k], r[k]) for k in range(it + 2)]
            )
            new = pair_mul(r[it + 1], dot)
            ratio = pair_div(new, rr)
            p = [
                pair_add(r[k], pair_mul(ratio, p[k])) if k < len(p) else r[k]
                for k in range(it + 2)
            ]
            rr = new
    return [a[0] for a in x]


class Halo:
    def __init__(self, refs, first, corners):
        self.low, self.high, self.own_s, self.own_n, self.e, self.w, self.n, self.s = refs
        self.first, self.corners = first, corners
        self.even_row = iota((8, COLS), 0) % 2 == 0
        self.even_lane = iota((8, COLS), 1) % 2 == 0
        self.sub = iota((8, COLS), 0)

    def rows(self, field, group):
        at = self.first + field * GROUPS + group
        e, w = self.e[at], self.w[at]
        return (
            jnp.where(self.even_row, roll(self.high[at], -1, 0), roll(self.low[at], 1, 0)),
            jnp.where(self.even_row, e, w),
            jnp.where(self.even_row, roll(e, -1, 0), roll(w, 1, 0)),
        )

    def edge_rows(self, field, group):
        at = self.first + field * GROUPS + group
        return jnp.where(self.even_row, self.e[at], self.w[at])

    def edge_columns(self, block):
        return jnp.concatenate(
            [
                jnp.where(self.even_lane, self.n[2 * block + h], self.s[2 * block + h])
                for h in range(2)
            ],
            axis=0,
        )

    def columns(self, block):
        inner, outer = [], []
        for h in range(2):
            at = 2 * block + h
            inner.append(
                jnp.where(self.even_lane, roll(self.own_n[at], -1, 1), roll(self.own_s[at], 1, 1))
            )
            outer.append(jnp.where(self.even_lane, roll(self.n[at], -1, 1), roll(self.s[at], 1, 1)))
        east = self.n.shape[0] - 2 * self.corners + block
        west = east + self.corners
        corner = jnp.where(
            self.sub < 4,
            jnp.where(self.even_lane, self.n[east], self.s[east]),
            jnp.where(self.even_lane, self.n[west], self.s[west]),
        )
        return (
            jnp.concatenate(inner, axis=0),
            jnp.concatenate([self.edge_columns(block), corner], axis=0),
            jnp.concatenate(outer, axis=0),
        )


def ends(v):
    return pltpu.roll(v, v.shape[0] - 1, 0), pltpu.roll(v, 1, 0)


def step_kernel(
    final,
    mix, thermal, haline, temp, salt, temp_response, salt_response, east, north, mask, bottom,
    diag, basis, gathered,
    *refs,
):
    a_halo = Halo(refs[:8], A_ROWS, A_CORNERS)
    if final:
        t_halo = Halo(refs[8:16], T_ROWS, T_CORNERS)
        new_temp, new_salt, new_surface = refs[16:]
    else:
        t_halo = a_halo
        inverses, ratios, new_temp, new_salt, row_low, row_high, col_low, col_high = refs[8:]
    tracers = ((temp, temp_response, 0, 3, 1.0), (salt, salt_response, 1, 4, -1.0))

    weights = coefficients(gathered[...])
    weights = [jnp.concatenate([jnp.concatenate([w] * 4, axis=0)] * 2, axis=1) for w in weights]
    full = sum(weights[k] * basis[k] for k in range(4))
    multiplier = full[:ROWS, :COLS]
    surface = diag[...] * multiplier
    if final:
        new_surface[...] = surface

    sub = iota((8, COLS), 0)
    even_row = sub % 2 == 0
    ring = jnp.concatenate([full[:ROWS], jnp.where(
        iota((8, 2 * COLS), 0) < 4, full[16:24], full[24:])], axis=0)
    even_lane = iota((24, COLS), 1) % 2 == 0

    def lanes(a, b):
        return jnp.where(
            even_lane,
            jnp.broadcast_to(ring[:, a : a + 1], (24, COLS)),
            jnp.broadcast_to(ring[:, b : b + 1], (24, COLS)),
        )

    def both_rows(a, b):
        return jnp.where(
            even_row,
            jnp.broadcast_to(full[a : a + 1, :COLS], (8, COLS)),
            jnp.broadcast_to(full[b : b + 1, :COLS], (8, COLS)),
        )

    column_m = [lanes(127, 0)[:ROWS], lanes(128, 255), lanes(129, 254)[:ROWS]]
    row_m = [both_rows(15, 0), both_rows(16, 31), both_rows(17, 30)]

    own = slice(0, ROWS)
    lane_sign = jnp.where(even_lane[own], 0.05, -0.05)
    wet0, wet1, wet2 = a_halo.columns(3)
    north1 = lane_sign * a_halo.edge_columns(6)
    e, w = ends(wet1)
    around1 = wet1[own] * ((e + w)[own] + (wet0 + wet2))
    column_wet = wet1
    column_q, column_out = [], []
    for _, _, field, response, sign in tracers:
        g = [
            b + (sign * m) * a
            for b, m, a in zip(t_halo.columns(field + 1), column_m, a_halo.columns(response + 1))
        ]
        q = wet1 * g[1]
        e, w = ends(q)
        near = (e + w)[own] + (wet0 * g[0] + wet2 * g[2])
        lap = wet1[own] * near - around1 * g[1][own]
        column_q.append(q)
        column_out.append(north1 * q[own] - 0.01 * lap)

    def corner_rows(v):
        return jnp.where(
            even_row,
            jnp.broadcast_to(v[16:17], (8, COLS)),
            jnp.broadcast_to(v[23:24], (8, COLS)),
        )

    corner_wet = corner_rows(column_wet)
    corner_q = [corner_rows(q) for q in column_q]
    column_wet = column_wet[own]
    column_q = [q[own] for q in column_q]

    lane8 = iota((8, COLS), 1)
    lane = iota((ROWS, COLS), 1)
    row = iota((ROWS, COLS), 0)
    row_sign = jnp.where(even_row, 0.05, -0.05)
    last = bottom[...]

    def beside(v, corner):
        return jnp.where(lane8 == COLS - 1, corner, pltpu.roll(v, COLS - 1, 1)) + jnp.where(
            lane8 == 0, corner, pltpu.roll(v, 1, 1)
        )

    def strips(group):
        shifts = [(127 - 2 * (group * 4 + j)) & 127 for j in range(4)]

        def corners(v):
            out = pltpu.roll(v, shifts[0], 1)
            for j in range(1, 4):
                out = jnp.where(sub // 2 == j, pltpu.roll(v, shifts[j], 1), out)
            return out

        wet0, wet1, wet2 = a_halo.rows(2, group)
        east1 = row_sign * a_halo.edge_rows(5, group)
        around1 = wet1 * ((wet0 + wet2) + beside(wet1, corners(corner_wet)))
        qs, outs = [], []
        for n, (_, _, field, response, sign) in enumerate(tracers):
            g = [
                b + (sign * m) * a
                for b, m, a in zip(
                    t_halo.rows(field, group), row_m, a_halo.rows(response, group)
                )
            ]
            q = wet1 * g[1]
            near = (wet0 * g[0] + wet2 * g[2]) + beside(q, corners(corner_q[n]))
            lap = wet1 * near - around1 * g[1]
            qs.append(q)
            outs.append(east1 * q - 0.01 * lap)
        return wet1, qs, outs

    def body(group, carry):
        row_wet, row_q, row_out = strips(group)
        for j in range(4):
            level = group * 4 + j
            shift = (127 - 2 * level) & 127

            def four(ve, vw, vn, vs, row_strip, column_strip):
                r = roll(row_strip, 7 - 2 * j, 0)
                r = jnp.concatenate([r, r], axis=0)
                c = pltpu.roll(column_strip, shift, 1)
                return (
                    jnp.where(row == ROWS - 1, r, pltpu.roll(ve, ROWS - 1, 0)),
                    jnp.where(row == 0, r, pltpu.roll(vw, 1, 0)),
                    jnp.where(lane == COLS - 1, c, pltpu.roll(vn, COLS - 1, 1)),
                    jnp.where(lane == 0, c, pltpu.roll(vs, 1, 1)),
                )

            wet = wet_at(mask, last, level)
            fe, fn = east[level], north[level]
            we, ww, wn, ws = four(wet, wet, wet, wet, row_wet, column_wet)
            around = wet * ((we + ww) + (wn + ws))
            diagonal = around + wet * (fe * (ww - we) + fn * (ws - wn))
            done = []
            for n, (field, response, _, _, sign) in enumerate(tracers):
                g = field[level] + (sign * multiplier) * response[level]
                q = wet * g
                e, w, no, so = four(q, q, q, q, row_q[n], column_q[n])
                near = wet * ((e + w) + (no + so))
                small = 0.01 * (near - around * g)
                u, v = (0.05 * fe) * q, (0.05 * fn) * q
                e, w, no, so = four(
                    u - small, -u - small, v - small, -v - small, row_out[n], column_out[n]
                )
                done.append(
                    (g + 0.05 * (near - diagonal * g))
                    + (wet * ((e + w) + (no + so)) + around * small)
                )
            t, s = done
            if final:
                new_temp[level] = t
                new_salt[level] = s
            else:
                above, total, pt, ps = carry
                total = total + wet * (thermal[level] * t - haline[level] * s)
                up = mix[jnp.maximum(level - 1, 0)] * (above * wet)
                inverse = inverses[level]
                pt = (t + up * pt) * inverse
                ps = (s + up * ps) * inverse
                new_temp[level] = pt
                new_salt[level] = ps
                carry = (wet, total, pt, ps)
        return carry

    zero = jnp.zeros((ROWS, COLS), F32)
    if final:
        lax.fori_loop(0, GROUPS, body, 0)
    else:
        _, total, _, _ = lax.fori_loop(0, GROUPS, body, (zero,) * 4)
        messages = row_low, row_high, col_low, col_high
        put_surface(messages, T_SURFACE, (surface + total,))
        back_substitute(messages, T_ROWS, (new_temp, new_salt), ratios, ((0, 1), (1, 2)))


def shape(*dims):
    return jax.ShapeDtypeStruct(dims, F32)


VMEM = pl.BlockSpec(memory_space=pltpu.VMEM)
HBM = pl.BlockSpec(memory_space=pltpu.HBM)
SMEM = pl.BlockSpec(memory_space=pltpu.SMEM)


def head(*block):
    return pl.BlockSpec(block, lambda i: (0,) * len(block), memory_space=pltpu.VMEM)


def call(kernel, outs, in_specs, out_specs=None, scratch=(), name=None, grid=None, room=40):
    extra = {} if grid is None else {"grid": grid}
    return pl.pallas_call(
        kernel,
        out_shape=outs,
        in_specs=in_specs,
        out_specs=[VMEM] * len(outs) if out_specs is None else out_specs,
        scratch_shapes=scratch,
        compiler_params=pltpu.CompilerParams(vmem_limit_bytes=room * 1024 * 1000),
        name=name,
        **extra,
    )


def message_shapes(surfaces, row_fields, col_fields, corner_fields):
    rows = shape(2 * (1 + corner_fields) + surfaces + GROUPS * row_fields, 8, COLS)
    cols = shape(2 * (1 + col_fields), 8, COLS)
    return [rows, rows, cols, cols]


def solution(mesh):
    nx, ny = mesh.shape["gx"], mesh.shape["gy"]
    devices = nx * ny
    both = ("gx", "gy")
    eastward = [(i, (i + 1) % nx) for i in range(nx)]
    northward = [(j, j + 1) for j in range(ny - 1)]

    def back(pairs):
        return [(b, a) for a, b in pairs]

    def exchange(messages, corners):
        row_low, row_high, col_low, col_high = messages
        rows_e = lax.ppermute(row_low, "gx", back(eastward))
        rows_w = lax.ppermute(row_high, "gx", eastward)
        own = col_low.shape[0]
        out = shape(own + 2 * corners, 8, COLS)
        to_south, to_north = call(
            forward_kernel, [out, out],
            [head(own, 8, COLS)] * 2 + [head(2 * corners, 8, COLS)] * 2,
            [head(*out.shape)] * 2, name="corners", grid=(1,),
        )(col_low, col_high, rows_e, rows_w)
        cols_n = lax.ppermute(to_south, "gy", back(northward))
        cols_s = lax.ppermute(to_north, "gy", northward)
        return [rows_e, rows_w, cols_n, cols_s]

    def all_sum(block):
        return lax.all_to_all(block, both, 0, 0, tiled=True)

    def surface_specs(rows, cols):
        return [head(rows, 8, COLS)] * 4 + [head(cols, 8, COLS)] * 2

    basis_shape = shape(4, 32, 2 * COLS)
    gram_shape = shape(devices, COLS)
    field = shape(LEVELS, ROWS, COLS)
    tile = shape(ROWS, COLS)

    def whole(*dims):
        return head(*dims)

    def per_device(
        sens_temp, sens_salt, sens_surface, flow_east, flow_north, mix_profile,
        thermal_weight, haline_weight, surface_diag, land_mask, bottom_level,
    ):
        *first, temp, salt, temp_response, salt_response, inverses, ratios = call(
            prepare_kernel, message_shapes(3, 6, 6, 5) + [field] * 6,
            [SMEM] * 3 + [HBM] * 5 + [VMEM] * 3,
            scratch=[pltpu.VMEM((LEVELS, ROWS, COLS), F32)] * 4
            + [
                pltpu.VMEM((LEVELS, ROWS, COLS), jnp.int32),
                pltpu.SemaphoreType.DMA((5, LEVELS // CHUNK)),
            ],
            name="prepare",
            room=62,
        )(
            mix_profile, thermal_weight, haline_weight, sens_temp, sens_salt, flow_east,
            flow_north, land_mask, bottom_level, sens_surface, surface_diag,
        )
        got = exchange(first, A_CORNERS)
        basis, gram, fixed = call(
            first_surface_kernel,
            [basis_shape, gram_shape, shape(2, 32, 2 * COLS)],
            surface_specs(A_ROWS, 2 * 7 + 2 * A_CORNERS),
            [head(4, 32, 2 * COLS), head(devices, COLS), head(2, 32, 2 * COLS)],
            name="first_surface",
            grid=(1,),
        )(first[0], first[1], *got)
        gathered = all_sum(gram)

        def step(final, temp, salt, basis, gathered, more, outs):
            return call(
                functools.partial(step_kernel, final),
                outs,
                [SMEM] * 3 + [VMEM] * (19 + len(more)),
                name="last_step" if final else "first_step",
            )(
                mix_profile, thermal_weight, haline_weight, temp, salt, temp_response,
                salt_response, flow_east, flow_north, land_mask, bottom_level, surface_diag,
                basis, gathered, *first, *got, *more,
            )

        temp, salt, *second = step(
            False, temp, salt, basis, gathered, [inverses, ratios],
            [field, field] + message_shapes(1, 2, 2, 2),
        )
        more = exchange(second, T_CORNERS)
        basis, gram = call(
            next_surface_kernel,
            [basis_shape, gram_shape],
            surface_specs(T_ROWS, 2 * 3 + 2 * T_CORNERS) + [head(2, 32, 2 * COLS)],
            [head(4, 32, 2 * COLS), head(devices, COLS)],
            name="next_surface",
            grid=(1,),
        )(second[0], second[1], *more, fixed)
        gathered = all_sum(gram)
        return tuple(
            step(True, temp, salt, basis, gathered, [*second, *more], [field, field, tile])
        )

    in_specs = (
        P(None, "gx", "gy"),
        P(None, "gx", "gy"),
        P("gx", "gy"),
        P(None, "gx", "gy"),
        P(None, "gx", "gy"),
        P(),
        P(),
        P(),
        P("gx", "gy"),
        P(None, "gx", "gy"),
        P("gx", "gy"),
    )
    out_specs = (P(None, "gx", "gy"), P(None, "gx", "gy"), P("gx", "gy"))
    return jax.shard_map(
        per_device, mesh=mesh, in_specs=in_specs, out_specs=out_specs, check_vma=False
    )
```

time: 129 us -> 114 us (0.88)
  Pallas kernels: 34.8 us -> 20.7 us
  local copies, waits for them, and re-layouts: 9.02 us -> 6.29 us
    pallas_call x2, Pallas kernels: 28.4 us -> 12.5 us  [step(): call(functools.partial(step_kernel, final), outs, [SMEM] * 3 + [VMEM] * (...]
    unnamed x34 -> x40, local copies, waits for them, and re-layouts: 9.02 us -> 6.29 us
    pallas_call x2, Pallas kernels: 5.69 us -> 7.51 us  [the longest x1 6.82 us: per_device(): call(prepare_kernel, message_shapes(3, 6, 6, 5) + [field] * 6, [SMEM] * 3...]
    ppermute x2, waiting for transfers between devices: 5.88 us -> 7.32 us  [exchange(): rows_e = lax.ppermute(row_low, 'gx', back(eastward))]
  transfers between devices with their start and end apart: 8 -> 8, of which waited for: 6 -> 5; matrix products, arithmetic and copies ran while one was open for 0% -> 0% of each run, Pallas kernels for 0% -> 0%
where the time goes in v3:
time: 114 us; the launch traced here: 113 us
  blocking collectives  59.3 us (52%)
  Pallas kernels  20.7 us (18%)
  starting transfers between devices  16 us (14%)
  waiting for transfers between devices  10.2 us (9%)
  local copies, waits for them, and re-layouts  6.29 us (6%)
    all_to_all x2, blocking collectives, all_sum(): return lax.all_to_all(block, both, 0, 0, tiled=True)  59.3 us
    pallas_call x2, Pallas kernels, step(): call(functools.partial(step_kernel, final), outs, [SMEM] * 3 + [VMEM] * (...  12.5 us
    ppermute x2, starting transfers between devices, exchange(): cols_s = lax.ppermute(to_north, 'gy', northward)  8.16 us
    ppermute x2, waiting for transfers between devices, exchange(): rows_e = lax.ppermute(row_low, 'gx', back(eastward))  7.32 us
    pallas_call x1, Pallas kernels, per_device(): call(prepare_kernel, message_shapes(3, 6, 6, 5) + [field] * 6, [SMEM] * 3...  6.82 us
    unnamed x40, local copies, waits for them, and re-layouts  6.29 us
    ppermute x2, starting transfers between devices, exchange(): rows_e = lax.ppermute(row_low, 'gx', back(eastward))  3.98 us
    ppermute x2, starting transfers between devices, exchange(): cols_n = lax.ppermute(to_south, 'gy', back(northward))  2.72 us
  transfers between devices with their start and end apart: 8, of which 5 were waited for; matrix products, arithmetic and copies ran while one was open for 0% of the time, Pallas kernels for 0%

profile of v3, /device:TPU:1, one launch (start us, length us, event | category | flops | bytes accessed | tf_op | source)
XLA Modules:
  0.0 113.3 jit_solution(3556176743241762338)
XLA Ops:
  0.6 0.0 copy-start.16
  0.6 6.8 %prepare.1 = (f32[87,8,128]{2,1,0:T(8,128)}, f32[87,8,128]{2,1,0:T(8,128)}, f32[14,8,128]{2,1,0:T(8,128)}, f32[14,8,128]{2,1,0:T(8,128)}, f32[48,16,128]{2,1,0:T...) custom-call(f32[48]{0:T(128)} %mix.5, f32[48]{0:T(128)} %thermal.5, ...), custom_call_target="tpu_custom_call" | custom-call | tf_op jit(solution)/shard_map/prepare/pallas_call | solution.py:654
  7.5 3.3 %collective-permute-start = (f32[87,8,128]{2,1,0:T(8,128)}, f32[87,8,128]{2,1,0:T(8,128)S(1)}, u32[]{:S(2)}, u32[]{:S(2)}) collective-permute-start(f32[87,8,128]{2,1,0:T(8,128)} %get-tuple-element.32.low.refs_0_), channel_id=1, source_target_pairs={{8,0},{16,8},{24,16},{32,24},{40,32},{48,40},{56,48},{64,56},{72,6... | collective-permute-start | bytes 1069064 | tf_op jit(solution)/shard_map/ppermute | solution.py:623
  10.8 0.0 collective-permute-start.1
  10.8 4.7 %collective-permute-done.rows_e.refs_4_ = f32[87,8,128]{2,1,0:T(8,128)S(1)} collective-permute-done((f32[87,8,128]{2,1,0:T(8,128)}, f32[87,8,128]{2,1,0:T(8,128)S(1)}, u32[]{:S(2)}, u32[]{:S(2)}) %collective-permute-start) | collective-permute-done | bytes 356384 | tf_op jit(solution)/shard_map/ppermute | solution.py:623
  15.5 0.0 collective-permute-done.1.rows_w.refs_5_
  15.5 0.0 copy-start.7
  15.5 0.8 copy-done.7
  16.3 0.0 copy-start.9
  16.3 0.8 copy-done.9
  17.2 0.0 copy-start.3
  17.2 0.0 copy-start.4
  17.2 0.0 copy-start.6
  17.2 1.4 %collective-permute-start.2 = (f32[26,8,128]{2,1,0:T(8,128)S(1)}, f32[26,8,128]{2,1,0:T(8,128)S(1)}, u32[]{:S(2)}, u32[]{:S(2)}) collective-permute-start(f32[26,8,128]{2,1,0:T(8,128)S(1)} %get-tuple-element.36), channel_id=1, source_target_pairs={{1,0},{2,1},{3,2},{4,3},{5,4},{6,5},{7,6},{9,8},{10,9},{11,10},{12... | collective-permute-start | bytes 319496 | tf_op jit(solution)/shard_map/ppermute | solution.py:632
  18.6 4.2 %collective-permute-start.3 = (f32[26,8,128]{2,1,0:T(8,128)S(1)}, f32[26,8,128]{2,1,0:T(8,128)S(1)}, u32[]{:S(2)}, u32[]{:S(2)}) collective-permute-start(f32[26,8,128]{2,1,0:T(8,128)S(1)} %get-tuple-element.37), channel_id=1, source_target_pairs={{0,1},{1,2},{2,3},{3,4},{4,5},{5,6},{6,7},{8,9},{9,10},{10,11},{11... | collective-permute-start | bytes 319496 | tf_op jit(solution)/shard_map/ppermute | solution.py:633
  22.8 0.4 collective-permute-done.2.cols_n.refs_6_
  23.2 1.2 %collective-permute-done.3.cols_s.refs_7_ = f32[26,8,128]{2,1,0:T(8,128)S(1)} collective-permute-done((f32[26,8,128]{2,1,0:T(8,128)S(1)}, f32[26,8,128]{2,1,0:T(8,128)S(1)}, u32[]{:S(2)}, u32[]{:S(2)}) %collective-permute-start.3) | collective-permute-done | bytes 106528 | tf_op jit(solution)/shard_map/ppermute | solution.py:633
  24.5 0.0 copy-done.3
  24.5 0.0 copy-done.4
  24.5 0.0 copy-start
  24.5 0.0 copy-start.1
  24.5 0.0 copy-start.2
  24.5 0.0 copy-start.5
  24.5 0.7 first_surface.1
  25.2 0.0 copy-start.8
  25.2 33.1 %all_to_all.22 = f32[256,1,128]{2,1,0:T(1,128)S(1)} all-to-all(f32[256,1,128]{2,1,0:T(1,128)S(1)} %bitcast.10), channel_id=1, replica_groups=mesh['gx'=32,'gy'=8] {'gx','gy'}, dimensions={0} | all-to-all | bytes 262144 | tf_op jit(solution)/shard_map/all_to_all | solution.py:637
  58.3 0.0 copy-start.15
  58.3 0.0 copy-start.17
  58.3 0.0 copy-start.18
  58.3 0.0 copy-start.19
  58.3 0.0 copy-done.16
  58.3 0.0 copy-done.6
  58.3 0.0 copy-done
  58.4 0.0 copy-done.1
  58.4 0.0 copy-done.2
  58.4 0.0 copy-done.5
  58.4 0.0 copy-done.8
  58.4 0.6 copy-done.15
  59.0 0.0 copy-done.17
  59.0 0.0 copy-done.18
  59.0 0.0 copy-done.19
  59.0 0.0 copy-start.11
  59.0 1.0 copy-done.11
  60.0 0.0 copy-start.12
  60.0 1.0 copy-done.12
  61.0 0.0 copy-start.13
  61.0 1.0 copy-done.13
  62.0 0.0 copy-start.14
  62.0 1.0 copy-done.14
  63.0 6.5 %first_step.1 = (f32[48,16,128]{2,1,0:T(8,128)S(1)}, f32[48,16,128]{2,1,0:T(8,128)S(1)}, f32[31,8,128]{2,1,0:T(8,128)S(1)}, f32[31,8,128]{2,1,0:T(8,128)S(1)}, f...) custom-call(f32[48]{0:T(128)S(1)} %copy-done.17, f32[48]{0:T(128)S(1)} %copy-done.18, f32[48]{0:T(128)S(1)} %copy-done.19, ...), custom_call_target="tpu_custom_call" | custom-call | tf_op jit(solution)/shard_map/first_step/pallas_call | solution.py:680
  69.5 0.7 collective-permute-start.4
  70.2 1.2 %collective-permute-start.5 = (f32[31,8,128]{2,1,0:T(8,128)S(1)}, f32[31,8,128]{2,1,0:T(8,128)S(1)}, u32[]{:S(2)}, u32[]{:S(2)}) collective-permute-start(f32[31,8,128]{2,1,0:T(8,128)S(1)} %get-tuple-element.45.high.refs_9_), channel_id=1, source_target_pairs={{0,8},{8,16},{16,24},{24,32},{32,40},{40,48},{48,56},{56,64},{64,7... | collective-permute-start | bytes 380936 | tf_op jit(solution)/shard_map/ppermute | solution.py:624
  71.3 2.6 %collective-permute-done.4.rows_e.refs_12_ = f32[31,8,128]{2,1,0:T(8,128)S(1)} collective-permute-done((f32[31,8,128]{2,1,0:T(8,128)S(1)}, f32[31,8,128]{2,1,0:T(8,128)S(1)}, u32[]{:S(2)}, u32[]{:S(2)}) %collective-permute-start.4) | collective-permute-done | bytes 127008 | tf_op jit(solution)/shard_map/ppermute | solution.py:623
  73.9 0.0 collective-permute-done.5.rows_w.refs_13_
  73.9 1.3 %collective-permute-start.6 = (f32[12,8,128]{2,1,0:T(8,128)S(1)}, f32[12,8,128]{2,1,0:T(8,128)S(1)}, u32[]{:S(2)}, u32[]{:S(2)}) collective-permute-start(f32[12,8,128]{2,1,0:T(8,128)S(1)} %get-tuple-element.48), channel_id=1, source_target_pairs={{1,0},{2,1},{3,2},{4,3},{5,4},{6,5},{7,6},{9,8},{10,9},{11,10},{12... | collective-permute-start | bytes 147464 | tf_op jit(solution)/shard_map/ppermute | solution.py:632
  75.2 4.0 %collective-permute-start.7 = (f32[12,8,128]{2,1,0:T(8,128)S(1)}, f32[12,8,128]{2,1,0:T(8,128)S(1)}, u32[]{:S(2)}, u32[]{:S(2)}) collective-permute-start(f32[12,8,128]{2,1,0:T(8,128)S(1)} %get-tuple-element.49), channel_id=1, source_target_pairs={{0,1},{1,2},{2,3},{3,4},{4,5},{5,6},{6,7},{8,9},{9,10},{10,11},{11... | collective-permute-start | bytes 147464 | tf_op jit(solution)/shard_map/ppermute | solution.py:633
  79.2 0.0 collective-permute-done.6.cols_n.refs_14_
  79.2 1.1 %collective-permute-done.7.cols_s.refs_15_ = f32[12,8,128]{2,1,0:T(8,128)S(1)} collective-permute-done((f32[12,8,128]{2,1,0:T(8,128)S(1)}, f32[12,8,128]{2,1,0:T(8,128)S(1)}, u32[]{:S(2)}, u32[]{:S(2)}) %collective-permute-start.7) | collective-permute-done | bytes 49184 | tf_op jit(solution)/shard_map/ppermute | solution.py:633
  80.4 0.7 next_surface.1
  81.1 0.0 copy-start.10
  81.1 26.2 %all_to_all.23 = f32[256,1,128]{2,1,0:T(1,128)S(1)} all-to-all(f32[256,1,128]{2,1,0:T(1,128)S(1)} %bitcast.11), channel_id=1, replica_groups=mesh['gx'=32,'gy'=8] {'gx','gy'}, dimensions={0} | all-to-all | bytes 262144 | tf_op jit(solution)/shard_map/all_to_all | solution.py:637
  107.3 0.0 copy-done.10
  107.3 6.0 %last_step.1 = (f32[48,16,128]{2,1,0:T(8,128)}, f32[48,16,128]{2,1,0:T(8,128)}, f32[16,128]{1,0:T(8,128)}) custom-call(f32[48]{0:T(128)S(1)} %copy-done.17, f32[48]{0:T(128)S(1)} %copy-done.18, f32[48]{0:T(128)S(1)} %copy-done.19, f32[48,16,128]{2,1,0:T(8,128)S(1)} %get-tuple-element.42.temp, f32[48,16,128]{2,1,0:T(8,128)S(1)} %get-tuple-element.43.salt, ...), custom_call_target="tpu_custom_call" | custom-call | tf_op jit(solution)/shard_map/last_step/pallas_call | solution.py:680
  (2 shorter events, 0.0 us)
Async XLA Ops:
  0.6 57.7 %copy-start.16 = (f32[16,128]{1,0:T(8,128)S(1)}, f32[16,128]{1,0:T(8,128)}, u32[]{:S(2)}) copy-start(f32[16,128]{1,0:T(8,128)} %diag.5) | copy-start | bytes 24580
  7.5 8.0 %collective-permute-start = (f32[87,8,128]{2,1,0:T(8,128)}, f32[87,8,128]{2,1,0:T(8,128)S(1)}, u32[]{:S(2)}, u32[]{:S(2)}) collective-permute-start(f32[87,8,128]{2,1,0:T(8,128)} %get-tuple-element.32.low.refs_0_), channel_id=1, source_target_pairs={{8,0},{16,8},{24,16},{32,24},{40,32},{48,40},{56,48},{64,56},{72,6... | collective-permute-start | bytes 1069064 | tf_op jit(solution)/shard_map/ppermute | solution.py:623
  10.8 4.7 %collective-permute-start.1 = (f32[87,8,128]{2,1,0:T(8,128)}, f32[87,8,128]{2,1,0:T(8,128)S(1)}, u32[]{:S(2)}, u32[]{:S(2)}) collective-permute-start(f32[87,8,128]{2,1,0:T(8,128)} %get-tuple-element.33.high.refs_1_), channel_id=1, source_target_pairs={{0,8},{8,16},{16,24},{24,32},{32,40},{40,48},{48,56},{56,64},{64,7... | collective-permute-start | bytes 1069064 | tf_op jit(solution)/shard_map/ppermute | solution.py:624
  15.5 0.8 copy-start.7
  16.3 0.8 copy-start.9
  17.2 7.3 %copy-start.3 = (f32[87,8,128]{2,1,0:T(8,128)S(1)}, f32[87,8,128]{2,1,0:T(8,128)}, u32[]{:S(2)}) copy-start(f32[87,8,128]{2,1,0:T(8,128)} %get-tuple-element.32.low.refs_0_) | copy-start | bytes 1069060
  17.2 7.3 %copy-start.4 = (f32[87,8,128]{2,1,0:T(8,128)S(1)}, f32[87,8,128]{2,1,0:T(8,128)}, u32[]{:S(2)}) copy-start(f32[87,8,128]{2,1,0:T(8,128)} %get-tuple-element.33.high.refs_1_) | copy-start | bytes 1069060
  17.2 41.2 %copy-start.6 = (f32[48,16,128]{2,1,0:T(8,128)S(1)}, f32[48,16,128]{2,1,0:T(8,128)}, u32[]{:S(2)}) copy-start(f32[48,16,128]{2,1,0:T(8,128)} %get-tuple-element.31.salt_response) | copy-start | bytes 1179652
  17.2 6.1 %collective-permute-start.2 = (f32[26,8,128]{2,1,0:T(8,128)S(1)}, f32[26,8,128]{2,1,0:T(8,128)S(1)}, u32[]{:S(2)}, u32[]{:S(2)}) collective-permute-start(f32[26,8,128]{2,1,0:T(8,128)S(1)} %get-tuple-element.36), channel_id=1, source_target_pairs={{1,0},{2,1},{3,2},{4,3},{5,4},{6,5},{7,6},{9,8},{10,9},{11,10},{12... | collective-permute-start | bytes 319496 | tf_op jit(solution)/shard_map/ppermute | solution.py:632
  18.6 5.9 %collective-permute-start.3 = (f32[26,8,128]{2,1,0:T(8,128)S(1)}, f32[26,8,128]{2,1,0:T(8,128)S(1)}, u32[]{:S(2)}, u32[]{:S(2)}) collective-permute-start(f32[26,8,128]{2,1,0:T(8,128)S(1)} %get-tuple-element.37), channel_id=1, source_target_pairs={{0,1},{1,2},{2,3},{3,4},{4,5},{5,6},{6,7},{8,9},{9,10},{10,11},{11... | collective-permute-start | bytes 319496 | tf_op jit(solution)/shard_map/ppermute | solution.py:633
  24.5 33.9 %copy-start = (f32[48,16,128]{2,1,0:T(8,128)S(1)}, f32[48,16,128]{2,1,0:T(8,128)}, u32[]{:S(2)}) copy-start(f32[48,16,128]{2,1,0:T(8,128)} %east.3) | copy-start | bytes 1179652
  24.5 33.9 %copy-start.1 = (f32[48,16,128]{2,1,0:T(8,128)S(1)}, f32[48,16,128]{2,1,0:T(8,128)}, u32[]{:S(2)}) copy-start(f32[48,16,128]{2,1,0:T(8,128)} %north.3) | copy-start | bytes 1179652
  24.5 33.9 %copy-start.2 = (s32[48,16,128]{2,1,0:T(8,128)S(1)}, s32[48,16,128]{2,1,0:T(8,128)}, u32[]{:S(2)}) copy-start(s32[48,16,128]{2,1,0:T(8,128)} %mask.3) | copy-start | bytes 1179652
  24.5 33.9 %copy-start.5 = (f32[48,16,128]{2,1,0:T(8,128)S(1)}, f32[48,16,128]{2,1,0:T(8,128)}, u32[]{:S(2)}) copy-start(f32[48,16,128]{2,1,0:T(8,128)} %get-tuple-element.30.temp_response) | copy-start | bytes 1179652
  25.2 33.2 %copy-start.8 = (f32[14,8,128]{2,1,0:T(8,128)S(1)}, f32[14,8,128]{2,1,0:T(8,128)}, u32[]{:S(2)}) copy-start(f32[14,8,128]{2,1,0:T(8,128)} %get-tuple-element.34.own_low.refs_2_) | copy-start | bytes 172036
  58.3 0.7 copy-start.15
  58.3 0.7 copy-start.17
  58.3 0.7 copy-start.18
  58.3 0.7 copy-start.19
  59.0 1.0 copy-start.11
  60.0 1.0 copy-start.12
  61.0 1.0 copy-start.13
  62.0 1.0 copy-start.14
  69.5 4.4 %collective-permute-start.4 = (f32[31,8,128]{2,1,0:T(8,128)S(1)}, f32[31,8,128]{2,1,0:T(8,128)S(1)}, u32[]{:S(2)}, u32[]{:S(2)}) collective-permute-start(f32[31,8,128]{2,1,0:T(8,128)S(1)} %get-tuple-element.44.low.refs_8_), channel_id=1, source_target_pairs={{8,0},{16,8},{24,16},{32,24},{40,32},{48,40},{56,48},{64,56},{72,6... | collective-permute-start | bytes 380936 | tf_op jit(solution)/shard_map/ppermute | solution.py:623
  70.2 3.8 %collective-permute-start.5 = (f32[31,8,128]{2,1,0:T(8,128)S(1)}, f32[31,8,128]{2,1,0:T(8,128)S(1)}, u32[]{:S(2)}, u32[]{:S(2)}) collective-permute-start(f32[31,8,128]{2,1,0:T(8,128)S(1)} %get-tuple-element.45.high.refs_9_), channel_id=1, source_target_pairs={{0,8},{8,16},{16,24},{24,32},{32,40},{40,48},{48,56},{56,64},{64,7... | collective-permute-start | bytes 380936 | tf_op jit(solution)/shard_map/ppermute | solution.py:624
  73.9 5.3 %collective-permute-start.6 = (f32[12,8,128]{2,1,0:T(8,128)S(1)}, f32[12,8,128]{2,1,0:T(8,128)S(1)}, u32[]{:S(2)}, u32[]{:S(2)}) collective-permute-start(f32[12,8,128]{2,1,0:T(8,128)S(1)} %get-tuple-element.48), channel_id=1, source_target_pairs={{1,0},{2,1},{3,2},{4,3},{5,4},{6,5},{7,6},{9,8},{10,9},{11,10},{12... | collective-permute-start | bytes 147464 | tf_op jit(solution)/shard_map/ppermute | solution.py:632
  75.2 5.2 %collective-permute-start.7 = (f32[12,8,128]{2,1,0:T(8,128)S(1)}, f32[12,8,128]{2,1,0:T(8,128)S(1)}, u32[]{:S(2)}, u32[]{:S(2)}) collective-permute-start(f32[12,8,128]{2,1,0:T(8,128)S(1)} %get-tuple-element.49), channel_id=1, source_target_pairs={{0,1},{1,2},{2,3},{3,4},{4,5},{5,6},{6,7},{8,9},{9,10},{10,11},{11... | collective-permute-start | bytes 147464 | tf_op jit(solution)/shard_map/ppermute | solution.py:633
  81.1 26.3 %copy-start.10 = (f32[14,8,128]{2,1,0:T(8,128)S(1)}, f32[14,8,128]{2,1,0:T(8,128)}, u32[]{:S(2)}) copy-start(f32[14,8,128]{2,1,0:T(8,128)} %get-tuple-element.35.own_high.refs_3_) | copy-start | bytes 172036

commit v4 on v3

--- a/solution.py
+++ b/solution.py
@@ -45,20 +45,24 @@
     return fast_two_sum(s, t + (x[1] + y[1]))
 
 
-def pair_mul(x, y):
-    p, e = two_prod(x[0], y[0])
-    return fast_two_sum(p, e + (x[0] * y[1] + x[1] * y[0]))
-
-
-def pair_neg(x):
-    return -x[0], -x[1]
-
-
-def pair_div(x, y):
-    first = x[0] / y[0]
-    p, e = two_prod(first, y[0])
-    rest = ((x[0] - p) - e + x[1]) - first * y[1]
-    return fast_two_sum(first, rest / y[0])
+def pair_scale(x, c):
+    p, e = two_prod(x[0], c)
+    return fast_two_sum(p, e + x[1] * c)
+
+
+def pair_dot(xs, ys):
+    terms, rest = [], []
+    for x, y in zip(xs, ys):
+        p, e = two_prod(x[0], y[0])
+        terms.append(p)
+        rest.append(e + (x[0] * y[1] + x[1] * y[0]))
+    while len(terms) > 1:
+        sums = [two_sum(a, b) for a, b in zip(terms[::2], terms[1::2])]
+        rest += [e for _, e in sums]
+        terms = [s for s, _ in sums] + terms[len(sums) * 2 :]
+    while len(rest) > 1:
+        rest = [a + b for a, b in zip(rest[::2], rest[1::2])] + rest[len(rest) // 2 * 2 :]
+    return terms[0] + rest[0]
 
 
 def roll(x, shift, axis):
@@ -120,10 +124,13 @@
 def forward_kernel(own_low, own_high, rows_e, rows_w, to_south, to_north):
     count = rows_e.shape[0] // 2
     own = own_low.shape[0]
-    for out, mine, side in ((to_south, own_low, 0), (to_north, own_high, count)):
-        out[:own] = mine[...]
-        out[own : own + count] = rows_e[side : side + count]
-        out[own + count :] = rows_w[side : side + count]
+    place = lax.axis_index("gy")
+    ends_at = 0, lax.axis_size("gy") - 1
+    for out, mine, side, end in zip((to_south, to_north), (own_low, own_high), (0, count), ends_at):
+        inner = place != end
+        out[:own] = jnp.where(inner, mine[...], 0.0)
+        out[own : own + count] = jnp.where(inner, rows_e[side : side + count], 0.0)
+        out[own + count :] = jnp.where(inner, rows_w[side : side + count], 0.0)
 
 
 def wet_at(mask, last, level):
@@ -134,7 +141,7 @@
     mix, thermal, haline, temp_in, salt_in, east_in, north_in, mask_in, bottom, surface, diag,
     row_low, row_high, col_low, col_high, *rest,
 ):
-    solved, (inverses, ratios, temp, salt, east, north, mask, sems) = rest[:4], rest[4:]
+    solved, (inverses, ratios, east, north, mask, temp, salt, sems) = rest[:4], rest[4:]
     last = bottom[...]
     zero = jnp.zeros((ROWS, COLS), F32)
     pair = (zero, zero)
@@ -310,34 +317,26 @@
     for n, (i, j) in enumerate(PAIRS):
         entry = tuple(jnp.broadcast_to(x[:, 8 * n : 8 * n + 1], (8, COLS)) for x in total)
         table[i, j] = table[j, i] = entry
+    imaged = {(i, k): pair_add(table[i, k], table[i, k + 1]) for i in range(4) for k in range(i + 1)}
     one = (jnp.ones((8, COLS), F32), jnp.zeros((8, COLS), F32))
     r, p, x = [one], [one], []
-    rr = table[0, 0]
+    rr = table[0, 0][0]
     for it in range(4):
-        image = [p[0]] + [pair_add(p[k], p[k - 1]) for k in range(1, it + 1)] + [p[it]]
-        dot = functools.reduce(
-            pair_add, [pair_mul(table[it, k], image[k]) for k in range(it + 2)]
-        )
-        step = pair_div(rr, pair_mul(p[it], dot))
-        x = [
-            pair_add(x[k], pair_mul(step, p[k])) if k < len(x) else pair_mul(step, p[k])
-            for k in range(it + 1)
-        ]
+        den = pair_dot([imaged[it, k] for k in range(it + 1)], p)
+        step = rr / (p[it][0] * den)
+        x = [x[k] + step * p[k][0] if k < len(x) else step * p[k][0] for k in range(it + 1)]
         if it < 3:
-            minus = pair_neg(step)
-            moved = [pair_mul(minus, a) for a in image]
+            image = [p[0]] + [pair_add(p[k], p[k - 1]) for k in range(1, it + 1)] + [p[it]]
+            moved = [pair_scale(a, -step) for a in image]
             r = [pair_add(r[k], moved[k]) if k < len(r) else moved[k] for k in range(it + 2)]
-            dot = functools.reduce(
-                pair_add, [pair_mul(table[it + 1, k], r[k]) for k in range(it + 2)]
-            )
-            new = pair_mul(r[it + 1], dot)
-            ratio = pair_div(new, rr)
+            new = r[it + 1][0] * pair_dot([table[it + 1, k] for k in range(it + 2)], r)
+            ratio = new / rr
             p = [
-                pair_add(r[k], pair_mul(ratio, p[k])) if k < len(p) else r[k]
+                pair_add(r[k], pair_scale(p[k], ratio)) if k < len(p) else r[k]
                 for k in range(it + 2)
             ]
             rr = new
-    return [a[0] for a in x]
+    return x
 
 
 class Halo:
@@ -398,10 +397,12 @@
 
 def step_kernel(
     final,
-    mix, thermal, haline, temp, salt, temp_response, salt_response, east, north, mask, bottom,
+    temp, salt, temp_response, salt_response, east, north, mask, bottom,
     diag, basis, gathered,
     *refs,
 ):
+    if not final:
+        (mix, thermal, haline), refs = refs[:3], refs[3:]
     a_halo = Halo(refs[:8], A_ROWS, A_CORNERS)
     if final:
         t_halo = Halo(refs[8:16], T_ROWS, T_CORNERS)
@@ -613,7 +614,7 @@
     devices = nx * ny
     both = ("gx", "gy")
     eastward = [(i, (i + 1) % nx) for i in range(nx)]
-    northward = [(j, j + 1) for j in range(ny - 1)]
+    northward = [(j, (j + 1) % ny) for j in range(ny)]
 
     def back(pairs):
         return [(b, a) for a, b in pairs]
@@ -651,19 +652,23 @@
         sens_temp, sens_salt, sens_surface, flow_east, flow_north, mix_profile,
         thermal_weight, haline_weight, surface_diag, land_mask, bottom_level,
     ):
-        *first, temp, salt, temp_response, salt_response, inverses, ratios = call(
-            prepare_kernel, message_shapes(3, 6, 6, 5) + [field] * 6,
+        *first, temp, salt, temp_response, salt_response, inverses, ratios, east, north, mask = call(
+            prepare_kernel,
+            message_shapes(3, 6, 6, 5)
+            + [field] * 8
+            + [jax.ShapeDtypeStruct((LEVELS, ROWS, COLS), jnp.int32)],
             [SMEM] * 3 + [HBM] * 5 + [VMEM] * 3,
-            scratch=[pltpu.VMEM((LEVELS, ROWS, COLS), F32)] * 4
-            + [
-                pltpu.VMEM((LEVELS, ROWS, COLS), jnp.int32),
-                pltpu.SemaphoreType.DMA((5, LEVELS // CHUNK)),
-            ],
+            scratch=[pltpu.VMEM((LEVELS, ROWS, COLS), F32)] * 2
+            + [pltpu.SemaphoreType.DMA((5, LEVELS // CHUNK))],
             name="prepare",
-            room=62,
         )(
-            mix_profile, thermal_weight, haline_weight, sens_temp, sens_salt, flow_east,
-            flow_north, land_mask, bottom_level, sens_surface, surface_diag,
+            *(
+                pltpu.with_memory_space_constraint(x, pltpu.HBM)
+                for x in (
+                    mix_profile, thermal_weight, haline_weight, sens_temp, sens_salt, flow_east,
+                    flow_north, land_mask, bottom_level, sens_surface, surface_diag,
+                )
+            )
         )
         got = exchange(first, A_CORNERS)
         basis, gram, fixed = call(
@@ -677,15 +682,15 @@
         gathered = all_sum(gram)
 
         def step(final, temp, salt, basis, gathered, more, outs):
+            weights = [] if final else [mix_profile, thermal_weight, haline_weight]
             return call(
                 functools.partial(step_kernel, final),
                 outs,
-                [SMEM] * 3 + [VMEM] * (19 + len(more)),
+                [VMEM] * 11 + [SMEM] * len(weights) + [VMEM] * (8 + len(more)),
                 name="last_step" if final else "first_step",
             )(
-                mix_profile, thermal_weight, haline_weight, temp, salt, temp_response,
-                salt_response, flow_east, flow_north, land_mask, bottom_level, surface_diag,
-                basis, gathered, *first, *got, *more,
+                temp, salt, temp_response, salt_response, east, north, mask, bottom_level,
+                surface_diag, basis, gathered, *weights, *first, *got, *more,
             )
 
         temp, salt, *second = step(

time: 114 us -> 99.2 us (0.87)
  blocking collectives: 59.3 us -> 52.3 us
  local copies, waits for them, and re-layouts: 6.29 us -> 0.71 us
  waiting for transfers between devices: 10.2 us -> 14.9 us
  starting transfers between devices: 16 us -> 12.3 us
  Pallas kernels: 20.7 us -> 18 us
    all_to_all x2, blocking collectives: 59.3 us -> 52.3 us  [all_sum(): return lax.all_to_all(block, both, 0, 0, tiled=True)]
    ppermute x2, starting transfers between devices: 8.16 us -> 1.35 us  [exchange(): cols_s = lax.ppermute(to_north, 'gy', northward)]
    unnamed x40 -> x10, local copies, waits for them, and re-layouts: 6.29 us -> 0.71 us
    ppermute x2, starting transfers between devices: 2.72 us -> 5.85 us  [exchange(): cols_n = lax.ppermute(to_south, 'gy', back(northward))]
    ppermute x2, waiting for transfers between devices: 0.45 us -> 3.48 us  [exchange(): cols_n = lax.ppermute(to_south, 'gy', back(northward))]
    pallas_call x3, Pallas kernels: 19.3 us -> 16.6 us  [the longest x2 11.3 us: step(): call(functools.partial(step_kernel, final), outs, [VMEM] * 11 + [SMEM] *...]
    ppermute x2, waiting for transfers between devices: 2.4 us -> 4.28 us  [exchange(): cols_s = lax.ppermute(to_north, 'gy', northward)]
  transfers between devices with their start and end apart: 8 -> 8, of which waited for: 5 -> 6; matrix products, arithmetic and copies ran while one was open for 0% -> 0% of each run, Pallas kernels for 0% -> 0%
where the time goes in v4:
time: 99.2 us; the launch traced here: 98.9 us
  blocking collectives  52.3 us (53%)
  Pallas kernels  18 us (18%)
  waiting for transfers between devices  14.9 us (15%)
  starting transfers between devices  12.3 us (12%)
    all_to_all x2, blocking collectives, all_sum(): return lax.all_to_all(block, both, 0, 0, tiled=True)  52.3 us
    pallas_call x2, Pallas kernels, step(): call(functools.partial(step_kernel, final), outs, [VMEM] * 11 + [SMEM] *...  11.3 us
    ppermute x2, waiting for transfers between devices, exchange(): rows_e = lax.ppermute(row_low, 'gx', back(eastward))  7.11 us
    ppermute x2, starting transfers between devices, exchange(): cols_n = lax.ppermute(to_south, 'gy', back(northward))  5.85 us
    pallas_call x1, Pallas kernels, per_device(): call(prepare_kernel, message_shapes(3, 6, 6, 5) + [field] * 8 + [jax.Shap...  5.27 us
    ppermute x2, waiting for transfers between devices, exchange(): cols_s = lax.ppermute(to_north, 'gy', northward)  4.28 us
    ppermute x2, starting transfers between devices, exchange(): rows_e = lax.ppermute(row_low, 'gx', back(eastward))  3.98 us
    ppermute x2, waiting for transfers between devices, exchange(): cols_n = lax.ppermute(to_south, 'gy', back(northward))  3.48 us
  transfers between devices with their start and end apart: 8, of which 6 were waited for; matrix products, arithmetic and copies ran while one was open for 0% of the time, Pallas kernels for 0%

profile of v4, /device:TPU:1, one launch (start us, length us, event | category | flops | bytes accessed | tf_op | source)
XLA Modules:
  0.0 98.9 jit_solution(4397347860191784555)
XLA Ops:
  0.6 5.3 %prepare.1 = (f32[87,8,128]{2,1,0:T(8,128)S(1)}, f32[87,8,128]{2,1,0:T(8,128)S(1)}, f32[14,8,128]{2,1,0:T(8,128)S(1)}, f32[14,8,128]{2,1,0:T(8,128)S(1)}, f32[48...) custom-call(f32[48]{0:T(128)} %refs_0_.1, ...), custom_call_target="tpu_custom_call" | custom-call | tf_op jit(solution)/shard_map/prepare/pallas_call | solution.py:655
  5.9 3.3 %collective-permute-start = (f32[87,8,128]{2,1,0:T(8,128)S(1)}, f32[87,8,128]{2,1,0:T(8,128)S(1)}, u32[]{:S(2)}, u32[]{:S(2)}) collective-permute-start(f32[87,8,128]{2,1,0:T(8,128)S(1)} %get-tuple-element.38.low.refs_3_.refs_0_), channel_id=1, source_target_pairs={{8,0},{16,8},{24,16},{32,24},{40,32},{48,40},{56,48},{64,56},{72,6... | collective-permute-start | bytes 1069064 | tf_op jit(solution)/shard_map/ppermute | solution.py:624
  9.2 0.0 collective-permute-start.1
  9.2 4.5 %collective-permute-done.rows_e.refs_7_.refs_4_ = f32[87,8,128]{2,1,0:T(8,128)S(1)} collective-permute-done((f32[87,8,128]{2,1,0:T(8,128)S(1)}, f32[87,8,128]{2,1,0:T(8,128)S(1)}, u32[]{:S(2)}, u32[]{:S(2)}) %collective-permute-start) | collective-permute-done | bytes 356384 | tf_op jit(solution)/shard_map/ppermute | solution.py:624
  13.7 0.0 collective-permute-done.1.rows_w.refs_8_.refs_5_
  13.8 5.7 %collective-permute-start.2 = (f32[26,8,128]{2,1,0:T(8,128)S(1)}, f32[26,8,128]{2,1,0:T(8,128)S(1)}, u32[]{:S(2)}, u32[]{:S(2)}) collective-permute-start(f32[26,8,128]{2,1,0:T(8,128)S(1)} %get-tuple-element.42), channel_id=1, source_target_pairs={{1,0},{2,1},{3,2},{4,3},{5,4},{6,5},{7,6},{0,7},{9,8},{10,9},{11,1... | collective-permute-start | bytes 319496 | tf_op jit(solution)/shard_map/ppermute | solution.py:633
  19.4 0.0 collective-permute-start.3
  19.4 1.7 %collective-permute-done.2.cols_n.refs_9_.refs_6_ = f32[26,8,128]{2,1,0:T(8,128)S(1)} collective-permute-done((f32[26,8,128]{2,1,0:T(8,128)S(1)}, f32[26,8,128]{2,1,0:T(8,128)S(1)}, u32[]{:S(2)}, u32[]{:S(2)}) %collective-permute-start.2) | collective-permute-done | bytes 106528 | tf_op jit(solution)/shard_map/ppermute | solution.py:633
  21.1 3.0 %collective-permute-done.3.cols_s.refs_10_.refs_7_ = f32[26,8,128]{2,1,0:T(8,128)S(1)} collective-permute-done((f32[26,8,128]{2,1,0:T(8,128)S(1)}, f32[26,8,128]{2,1,0:T(8,128)S(1)}, u32[]{:S(2)}, u32[]{:S(2)}) %collective-permute-start.3) | collective-permute-done | bytes 106528 | tf_op jit(solution)/shard_map/ppermute | solution.py:634
  24.2 0.7 first_surface.1
  24.9 0.0 copy-start.4
  24.9 27.8 %all_to_all.22 = f32[256,1,128]{2,1,0:T(1,128)S(1)} all-to-all(f32[256,1,128]{2,1,0:T(1,128)S(1)} %bitcast.10), channel_id=1, replica_groups=mesh['gx'=32,'gy'=8] {'gx','gy'}, dimensions={0} | all-to-all | bytes 262144 | tf_op jit(solution)/shard_map/all_to_all | solution.py:638
  52.7 0.0 copy-start.1
  52.7 0.0 copy-start
  52.7 0.0 copy-start.2
  52.7 0.0 copy-start.3
  52.7 0.0 copy-done.4
  52.8 0.7 copy-done.1
  53.4 0.0 copy-done
  53.4 0.0 copy-done.2
  53.5 0.0 copy-done.3
  53.5 6.2 %first_step.1 = (f32[48,16,128]{2,1,0:T(8,128)S(1)}, f32[48,16,128]{2,1,0:T(8,128)S(1)}, f32[31,8,128]{2,1,0:T(8,128)S(1)}, f32[31,8,128]{2,1,0:T(8,128)S(1)}, f...) custom-call(f32[48,16,128]{2,1,0:T(8,128)S(1)} %get-tuple-element.31.temp, f32[48,16,128]{2,1,0:T(8,128)S(1)} %get-tuple-element.32.salt, ...), custom_call_target="tpu_custom_call" | custom-call | tf_op jit(solution)/shard_map/first_step/pallas_call | solution.py:686
  59.6 0.7 collective-permute-start.4
  60.3 1.2 %collective-permute-start.5 = (f32[31,8,128]{2,1,0:T(8,128)S(1)}, f32[31,8,128]{2,1,0:T(8,128)S(1)}, u32[]{:S(2)}, u32[]{:S(2)}) collective-permute-start(f32[31,8,128]{2,1,0:T(8,128)S(1)} %get-tuple-element.51.high.refs_9_), channel_id=1, source_target_pairs={{0,8},{8,16},{16,24},{24,32},{32,40},{40,48},{48,56},{56,64},{64,7... | collective-permute-start | bytes 380936 | tf_op jit(solution)/shard_map/ppermute | solution.py:625
  61.5 2.6 %collective-permute-done.4.rows_e.refs_12_ = f32[31,8,128]{2,1,0:T(8,128)S(1)} collective-permute-done((f32[31,8,128]{2,1,0:T(8,128)S(1)}, f32[31,8,128]{2,1,0:T(8,128)S(1)}, u32[]{:S(2)}, u32[]{:S(2)}) %collective-permute-start.4) | collective-permute-done | bytes 127008 | tf_op jit(solution)/shard_map/ppermute | solution.py:624
  64.1 0.0 collective-permute-done.5.rows_w.refs_13_
  64.1 0.2 collective-permute-start.6
  64.3 1.4 %collective-permute-start.7 = (f32[12,8,128]{2,1,0:T(8,128)S(1)}, f32[12,8,128]{2,1,0:T(8,128)S(1)}, u32[]{:S(2)}, u32[]{:S(2)}) collective-permute-start(f32[12,8,128]{2,1,0:T(8,128)S(1)} %get-tuple-element.55), channel_id=1, source_target_pairs={{0,1},{1,2},{2,3},{3,4},{4,5},{5,6},{6,7},{7,0},{8,9},{9,10},{10,1... | collective-permute-start | bytes 147464 | tf_op jit(solution)/shard_map/ppermute | solution.py:634
  65.6 1.8 %collective-permute-done.6.cols_n.refs_14_ = f32[12,8,128]{2,1,0:T(8,128)S(1)} collective-permute-done((f32[12,8,128]{2,1,0:T(8,128)S(1)}, f32[12,8,128]{2,1,0:T(8,128)S(1)}, u32[]{:S(2)}, u32[]{:S(2)}) %collective-permute-start.6) | collective-permute-done | bytes 49184 | tf_op jit(solution)/shard_map/ppermute | solution.py:633
  67.4 1.2 %collective-permute-done.7.cols_s.refs_15_ = f32[12,8,128]{2,1,0:T(8,128)S(1)} collective-permute-done((f32[12,8,128]{2,1,0:T(8,128)S(1)}, f32[12,8,128]{2,1,0:T(8,128)S(1)}, u32[]{:S(2)}, u32[]{:S(2)}) %collective-permute-start.7) | collective-permute-done | bytes 49184 | tf_op jit(solution)/shard_map/ppermute | solution.py:634
  68.6 0.7 next_surface.1
  69.3 24.5 %all_to_all.23 = f32[256,1,128]{2,1,0:T(1,128)S(1)} all-to-all(f32[256,1,128]{2,1,0:T(1,128)S(1)} %bitcast.11), channel_id=1, replica_groups=mesh['gx'=32,'gy'=8] {'gx','gy'}, dimensions={0} | all-to-all | bytes 262144 | tf_op jit(solution)/shard_map/all_to_all | solution.py:638
  93.8 5.1 %last_step.1 = (f32[48,16,128]{2,1,0:T(8,128)}, f32[48,16,128]{2,1,0:T(8,128)}, f32[16,128]{1,0:T(8,128)}) custom-call(f32[48,16,128]{2,1,0:T(8,128)S(1)} %get-tuple-element.48.temp, f32[48,16,128]{2,1,0:T(8,128)S(1)} %get-tuple-element.49.salt, f32[48,16,128]{2,1,0:T(8,128)S(1)} %get-tuple-element.33.temp_response, ...), custom_call_target="tpu_custom_call" | custom-call | tf_op jit(solution)/shard_map/last_step/pallas_call | solution.py:686
  (2 shorter events, 0.0 us)
Async XLA Ops:
  5.9 7.8 %collective-permute-start = (f32[87,8,128]{2,1,0:T(8,128)S(1)}, f32[87,8,128]{2,1,0:T(8,128)S(1)}, u32[]{:S(2)}, u32[]{:S(2)}) collective-permute-start(f32[87,8,128]{2,1,0:T(8,128)S(1)} %get-tuple-element.38.low.refs_3_.refs_0_), channel_id=1, source_target_pairs={{8,0},{16,8},{24,16},{32,24},{40,32},{48,40},{56,48},{64,56},{72,6... | collective-permute-start | bytes 1069064 | tf_op jit(solution)/shard_map/ppermute | solution.py:624
  9.2 4.5 %collective-permute-start.1 = (f32[87,8,128]{2,1,0:T(8,128)S(1)}, f32[87,8,128]{2,1,0:T(8,128)S(1)}, u32[]{:S(2)}, u32[]{:S(2)}) collective-permute-start(f32[87,8,128]{2,1,0:T(8,128)S(1)} %get-tuple-element.39.high.refs_4_.refs_1_), channel_id=1, source_target_pairs={{0,8},{8,16},{16,24},{24,32},{32,40},{40,48},{48,56},{56,64},{64,7... | collective-permute-start | bytes 1069064 | tf_op jit(solution)/shard_map/ppermute | solution.py:625
  13.8 7.4 %collective-permute-start.2 = (f32[26,8,128]{2,1,0:T(8,128)S(1)}, f32[26,8,128]{2,1,0:T(8,128)S(1)}, u32[]{:S(2)}, u32[]{:S(2)}) collective-permute-start(f32[26,8,128]{2,1,0:T(8,128)S(1)} %get-tuple-element.42), channel_id=1, source_target_pairs={{1,0},{2,1},{3,2},{4,3},{5,4},{6,5},{7,6},{0,7},{9,8},{10,9},{11,1... | collective-permute-start | bytes 319496 | tf_op jit(solution)/shard_map/ppermute | solution.py:633
  19.4 4.8 %collective-permute-start.3 = (f32[26,8,128]{2,1,0:T(8,128)S(1)}, f32[26,8,128]{2,1,0:T(8,128)S(1)}, u32[]{:S(2)}, u32[]{:S(2)}) collective-permute-start(f32[26,8,128]{2,1,0:T(8,128)S(1)} %get-tuple-element.43), channel_id=1, source_target_pairs={{0,1},{1,2},{2,3},{3,4},{4,5},{5,6},{6,7},{7,0},{8,9},{9,10},{10,1... | collective-permute-start | bytes 319496 | tf_op jit(solution)/shard_map/ppermute | solution.py:634
  24.9 27.9 %copy-start.4 = (f32[48]{0:T(128)S(1)}, f32[48]{0:T(128)}, u32[]{:S(2)}) copy-start(f32[48]{0:T(128)} %refs_2_.1) | copy-start | bytes 580
  52.7 0.7 copy-start.1
  52.7 0.7 copy-start
  52.7 0.7 copy-start.2
  52.7 0.7 copy-start.3
  59.6 4.4 %collective-permute-start.4 = (f32[31,8,128]{2,1,0:T(8,128)S(1)}, f32[31,8,128]{2,1,0:T(8,128)S(1)}, u32[]{:S(2)}, u32[]{:S(2)}) collective-permute-start(f32[31,8,128]{2,1,0:T(8,128)S(1)} %get-tuple-element.50.low.refs_8_), channel_id=1, source_target_pairs={{8,0},{16,8},{24,16},{32,24},{40,32},{48,40},{56,48},{64,56},{72,6... | collective-permute-start | bytes 380936 | tf_op jit(solution)/shard_map/ppermute | solution.py:624
  60.3 3.8 %collective-permute-start.5 = (f32[31,8,128]{2,1,0:T(8,128)S(1)}, f32[31,8,128]{2,1,0:T(8,128)S(1)}, u32[]{:S(2)}, u32[]{:S(2)}) collective-permute-start(f32[31,8,128]{2,1,0:T(8,128)S(1)} %get-tuple-element.51.high.refs_9_), channel_id=1, source_target_pairs={{0,8},{8,16},{16,24},{24,32},{32,40},{40,48},{48,56},{56,64},{64,7... | collective-permute-start | bytes 380936 | tf_op jit(solution)/shard_map/ppermute | solution.py:625
  64.1 3.3 %collective-permute-start.6 = (f32[12,8,128]{2,1,0:T(8,128)S(1)}, f32[12,8,128]{2,1,0:T(8,128)S(1)}, u32[]{:S(2)}, u32[]{:S(2)}) collective-permute-start(f32[12,8,128]{2,1,0:T(8,128)S(1)} %get-tuple-element.54), channel_id=1, source_target_pairs={{1,0},{2,1},{3,2},{4,3},{5,4},{6,5},{7,6},{0,7},{9,8},{10,9},{11,1... | collective-permute-start | bytes 147464 | tf_op jit(solution)/shard_map/ppermute | solution.py:633
  64.3 4.4 %collective-permute-start.7 = (f32[12,8,128]{2,1,0:T(8,128)S(1)}, f32[12,8,128]{2,1,0:T(8,128)S(1)}, u32[]{:S(2)}, u32[]{:S(2)}) collective-permute-start(f32[12,8,128]{2,1,0:T(8,128)S(1)} %get-tuple-element.55), channel_id=1, source_target_pairs={{0,1},{1,2},{2,3},{3,4},{4,5},{5,6},{6,7},{7,0},{8,9},{9,10},{10,1... | collective-permute-start | bytes 147464 | tf_op jit(solution)/shard_map/ppermute | solution.py:634

commit v5 on v4

--- a/solution.py
+++ b/solution.py
@@ -118,7 +118,7 @@
 
 
 def corners_of(rows):
-    return A_CORNERS if rows.shape[0] == A_ROWS + 6 * GROUPS else T_CORNERS
+    return A_CORNERS if rows.shape[0] == A_ROWS else T_CORNERS
 
 
 def forward_kernel(own_low, own_high, rows_e, rows_w, to_south, to_north):
@@ -139,9 +139,10 @@
 
 def prepare_kernel(
     mix, thermal, haline, temp_in, salt_in, east_in, north_in, mask_in, bottom, surface, diag,
-    row_low, row_high, col_low, col_high, *rest,
+    row_low, row_high, col_low, col_high, strip_low, strip_high, *rest,
 ):
-    solved, (inverses, ratios, east, north, mask, temp, salt, sems) = rest[:4], rest[4:]
+    solved, rest = rest[:4], rest[4:]
+    inverses, ratios, east, north, wets, kept, temp, salt, mask, sems = rest
     last = bottom[...]
     zero = jnp.zeros((ROWS, COLS), F32)
     pair = (zero, zero)
@@ -172,14 +173,17 @@
             tw, hw = thermal[level] * wet, haline[level] * wet
             total = total + (tw * t - hw * s)
             depth = depth + wet
+            wets[level] = wet
+            for n, weight in enumerate((mix, thermal, haline)):
+                kept[n, level] = jnp.full((8, COLS), weight[level], F32)
             values = tuple((r + up * v) * inverse for r, v in zip((t, s, tw, hw), values))
             for ref, v in zip(solved, values):
                 ref[level] = v
             ratio = down * inverse
             inverses[level] = inverse
             ratios[level] = ratio
-            put_rows(row_low, row_high, A_ROWS, 2, group, j, wet)
-            put_rows(row_low, row_high, A_ROWS, 5, group, j, east[level])
+            put_rows(strip_low, strip_high, 0, 2, group, j, wet)
+            put_rows(strip_low, strip_high, 0, 5, group, j, east[level])
             packs = tuple(packed(acc, v, level) for acc, v in zip(packs, (wet, north[level])))
             up = down
             wet = below
@@ -198,11 +202,11 @@
     put_surface(refs, A_SURFACE, (surface[...] + total, depth / LEVELS, diag[...]))
     put_cols(refs, 3, *packs[0])
     put_cols(refs, 6, *packs[1])
-    back_substitute(refs, A_ROWS, solved, ratios, ((0, 1), (1, 2), (3, 4), (4, 5)))
-
-
-def back_substitute(refs, first, solved, ratios, places):
-    row_low, row_high = refs[:2]
+    strips = strip_low, strip_high
+    back_substitute(refs, strips, 0, solved, ratios, ((0, 1), (1, 2), (3, 4), (4, 5)))
+
+
+def back_substitute(refs, strips, first, solved, ratios, places):
     zero = jnp.zeros((ROWS, COLS), F32)
 
     def up_body(count, carry):
@@ -214,7 +218,7 @@
             values = tuple(ref[level] + ratio * v for ref, v in zip(solved, values))
             for ref, v, (field, _) in zip(solved, values, places):
                 ref[level] = v
-                put_rows(row_low, row_high, first, field, group, j, v)
+                put_rows(*strips, first, field, group, j, v)
             packs = tuple(packed(acc, v, level) for acc, v in zip(packs, values))
         return values, packs
 
@@ -397,26 +401,30 @@
 
 def step_kernel(
     final,
-    temp, salt, temp_response, salt_response, east, north, mask, bottom,
-    diag, basis, gathered,
+    temp, salt, temp_response, salt_response, east, north, wets, fixed, basis, gathered,
     *refs,
 ):
     if not final:
-        (mix, thermal, haline), refs = refs[:3], refs[3:]
-    a_halo = Halo(refs[:8], A_ROWS, A_CORNERS)
+        kept, refs = refs[0], refs[1:]
+
+        def weight(n, level):
+            value = kept[n, level]
+            return jnp.concatenate([value, value], axis=0)
+
+    a_halo = Halo(refs[:8], 0, A_CORNERS)
     if final:
         t_halo = Halo(refs[8:16], T_ROWS, T_CORNERS)
         new_temp, new_salt, new_surface = refs[16:]
     else:
         t_halo = a_halo
-        inverses, ratios, new_temp, new_salt, row_low, row_high, col_low, col_high = refs[8:]
+        inverses, ratios, new_temp, new_salt, *messages = refs[8:]
     tracers = ((temp, temp_response, 0, 3, 1.0), (salt, salt_response, 1, 4, -1.0))
 
     weights = coefficients(gathered[...])
     weights = [jnp.concatenate([jnp.concatenate([w] * 4, axis=0)] * 2, axis=1) for w in weights]
     full = sum(weights[k] * basis[k] for k in range(4))
     multiplier = full[:ROWS, :COLS]
-    surface = diag[...] * multiplier
+    surface = fixed[1, :ROWS, :COLS] * multiplier
     if final:
         new_surface[...] = surface
 
@@ -479,7 +487,6 @@
     lane = iota((ROWS, COLS), 1)
     row = iota((ROWS, COLS), 0)
     row_sign = jnp.where(even_row, 0.05, -0.05)
-    last = bottom[...]
 
     def beside(v, corner):
         return jnp.where(lane8 == COLS - 1, corner, pltpu.roll(v, COLS - 1, 1)) + jnp.where(
@@ -530,7 +537,7 @@
                     jnp.where(lane == 0, c, pltpu.roll(vs, 1, 1)),
                 )
 
-            wet = wet_at(mask, last, level)
+            wet = wets[level]
             fe, fn = east[level], north[level]
             we, ww, wn, ws = four(wet, wet, wet, wet, row_wet, column_wet)
             around = wet * ((we + ww) + (wn + ws))
@@ -556,8 +563,8 @@
                 new_salt[level] = s
             else:
                 above, total, pt, ps = carry
-                total = total + wet * (thermal[level] * t - haline[level] * s)
-                up = mix[jnp.maximum(level - 1, 0)] * (above * wet)
+                total = total + wet * (weight(1, level) * t - weight(2, level) * s)
+                up = weight(0, jnp.maximum(level - 1, 0)) * (above * wet)
                 inverse = inverses[level]
                 pt = (t + up * pt) * inverse
                 ps = (s + up * ps) * inverse
@@ -571,9 +578,10 @@
         lax.fori_loop(0, GROUPS, body, 0)
     else:
         _, total, _, _ = lax.fori_loop(0, GROUPS, body, (zero,) * 4)
-        messages = row_low, row_high, col_low, col_high
         put_surface(messages, T_SURFACE, (surface + total,))
-        back_substitute(messages, T_ROWS, (new_temp, new_salt), ratios, ((0, 1), (1, 2)))
+        back_substitute(
+            messages, messages[:2], T_ROWS, (new_temp, new_salt), ratios, ((0, 1), (1, 2))
+        )
 
 
 def shape(*dims):
@@ -634,6 +642,10 @@
         cols_s = lax.ppermute(to_north, "gy", northward)
         return [rows_e, rows_w, cols_n, cols_s]
 
+    def exchange_strips(low, high, after):
+        low, high, _ = lax.optimization_barrier((low, high, after))
+        return [lax.ppermute(low, "gx", back(eastward)), lax.ppermute(high, "gx", eastward)]
+
     def all_sum(block):
         return lax.all_to_all(block, both, 0, 0, tiled=True)
 
@@ -652,13 +664,15 @@
         sens_temp, sens_salt, sens_surface, flow_east, flow_north, mix_profile,
         thermal_weight, haline_weight, surface_diag, land_mask, bottom_level,
     ):
-        *first, temp, salt, temp_response, salt_response, inverses, ratios, east, north, mask = call(
+        *sent, strip_low, strip_high, temp, salt, temp_response, salt_response, inverses, ratios, east, north, wets, kept = call(
             prepare_kernel,
-            message_shapes(3, 6, 6, 5)
-            + [field] * 8
-            + [jax.ShapeDtypeStruct((LEVELS, ROWS, COLS), jnp.int32)],
+            message_shapes(3, 0, 6, 5)
+            + [shape(6 * GROUPS, 8, COLS)] * 2
+            + [field] * 9
+            + [shape(3, LEVELS, 8, COLS)],
             [SMEM] * 3 + [HBM] * 5 + [VMEM] * 3,
             scratch=[pltpu.VMEM((LEVELS, ROWS, COLS), F32)] * 2
+            + [pltpu.VMEM((LEVELS, ROWS, COLS), jnp.int32)]
             + [pltpu.SemaphoreType.DMA((5, LEVELS // CHUNK))],
             name="prepare",
         )(
@@ -670,7 +684,9 @@
                 )
             )
         )
-        got = exchange(first, A_CORNERS)
+        got = exchange(sent, A_CORNERS)
+        strips = exchange_strips(strip_low, strip_high, got[2])
+        halo = [strip_low, strip_high, *sent[2:], *strips, *got[2:]]
         basis, gram, fixed = call(
             first_surface_kernel,
             [basis_shape, gram_shape, shape(2, 32, 2 * COLS)],
@@ -678,19 +694,19 @@
             [head(4, 32, 2 * COLS), head(devices, COLS), head(2, 32, 2 * COLS)],
             name="first_surface",
             grid=(1,),
-        )(first[0], first[1], *got)
+        )(sent[0], sent[1], *got)
         gathered = all_sum(gram)
 
         def step(final, temp, salt, basis, gathered, more, outs):
-            weights = [] if final else [mix_profile, thermal_weight, haline_weight]
+            weights = [] if final else [kept]
             return call(
                 functools.partial(step_kernel, final),
                 outs,
-                [VMEM] * 11 + [SMEM] * len(weights) + [VMEM] * (8 + len(more)),
+                [VMEM] * (18 + len(weights) + len(more)),
                 name="last_step" if final else "first_step",
             )(
-                temp, salt, temp_response, salt_response, east, north, mask, bottom_level,
-                surface_diag, basis, gathered, *weights, *first, *got, *more,
+                temp, salt, temp_response, salt_response, east, north, wets, fixed,
+                basis, gathered, *weights, *halo, *more,
             )
 
         temp, salt, *second = step(

time: 99.2 us -> 96.3 us (0.971)
  starting transfers between devices: 12.3 us -> 19.4 us
  blocking collectives: 52.3 us -> 47.5 us
  waiting for transfers between devices: 14.9 us -> 11 us
    ppermute x0 -> x2, starting transfers between devices: none -> 7.08 us  [the longest x1 7.08 us: exchange_strips(): lax.ppermute(low, 'gx', back(eastward))]
    all_to_all x2, blocking collectives: 52.3 us -> 47.5 us  [all_sum(): return lax.all_to_all(block, both, 0, 0, tiled=True)]
    ppermute x2, waiting for transfers between devices: 7.11 us -> 3.95 us  [exchange(): rows_e = lax.ppermute(row_low, 'gx', back(eastward))]
    ppermute x2, waiting for transfers between devices: 4.28 us -> 1.22 us  [exchange(): cols_s = lax.ppermute(to_north, 'gy', northward)]
    ppermute x2, waiting for transfers between devices: 0.01 us -> 2.3 us  [exchange(): rows_w = lax.ppermute(row_high, 'gx', eastward)]
  transfers between devices with their start and end apart: 8 -> 10, of which waited for: 6 -> 6; matrix products, arithmetic and copies ran while one was open for 0% -> 0% of each run, Pallas kernels for 0% -> 1%
where the time goes in v5:
time: 96.3 us; the launch traced here: 96.1 us
  blocking collectives  47.5 us (49%)
  starting transfers between devices  19.4 us (20%)
  Pallas kernels  17.6 us (18%)
  waiting for transfers between devices  11 us (11%)
    all_to_all x2, blocking collectives, all_sum(): return lax.all_to_all(block, both, 0, 0, tiled=True)  47.5 us
    pallas_call x2, Pallas kernels, step(): call(functools.partial(step_kernel, final), outs, [VMEM] * (18 + len(weig...  10.8 us
    ppermute x1, starting transfers between devices, exchange_strips(): lax.ppermute(low, 'gx', back(eastward))  7.08 us
    ppermute x2, starting transfers between devices, exchange(): cols_n = lax.ppermute(to_south, 'gy', back(northward))  5.84 us
    pallas_call x1, Pallas kernels, per_device(): call(prepare_kernel, message_shapes(3, 0, 6, 5) + [shape(6 * GROUPS, 8, C...  5.35 us
    ppermute x2, starting transfers between devices, exchange(): rows_e = lax.ppermute(row_low, 'gx', back(eastward))  3.98 us
    ppermute x2, waiting for transfers between devices, exchange(): rows_e = lax.ppermute(row_low, 'gx', back(eastward))  3.95 us
    ppermute x2, waiting for transfers between devices, exchange(): cols_n = lax.ppermute(to_south, 'gy', back(northward))  3.48 us
  transfers between devices with their start and end apart: 10, of which 6 were waited for; matrix products, arithmetic and copies ran while one was open for 0% of the time, Pallas kernels for 1%

profile of v5, /device:TPU:1, one launch (start us, length us, event | category | flops | bytes accessed | tf_op | source)
XLA Modules:
  0.0 96.1 jit_solution(6645262595048298186)
XLA Ops:
  0.6 5.3 %prepare.1 = (f32[15,8,128]{2,1,0:T(8,128)S(1)}, f32[15,8,128]{2,1,0:T(8,128)S(1)}, f32[14,8,128]{2,1,0:T(8,128)S(1)}, f32[14,8,128]{2,1,0:T(8,128)S(1)}, f32[72...) custom-call(f32[48]{0:T(128)} %mix.1, f32[48]{0:T(128)} %thermal.1, ...), custom_call_target="tpu_custom_call" | custom-call | tf_op jit(solution)/shard_map/prepare/pallas_call | solution.py:667
  6.0 3.3 %collective-permute-start = (f32[15,8,128]{2,1,0:T(8,128)S(1)}, f32[15,8,128]{2,1,0:T(8,128)S(1)}, u32[]{:S(2)}, u32[]{:S(2)}) collective-permute-start(f32[15,8,128]{2,1,0:T(8,128)S(1)} %get-tuple-element.43.low), channel_id=1, source_target_pairs={{8,0},{16,8},{24,16},{32,24},{40,32},{48,40},{56,48},{64,56},{72,6... | collective-permute-start | bytes 184328 | tf_op jit(solution)/shard_map/ppermute | solution.py:632
  9.3 0.0 collective-permute-start.1
  9.3 1.3 %collective-permute-done.rows_e = f32[15,8,128]{2,1,0:T(8,128)S(1)} collective-permute-done((f32[15,8,128]{2,1,0:T(8,128)S(1)}, f32[15,8,128]{2,1,0:T(8,128)S(1)}, u32[]{:S(2)}, u32[]{:S(2)}) %collective-permute-start) | collective-permute-done | bytes 61472 | tf_op jit(solution)/shard_map/ppermute | solution.py:632
  10.7 2.3 %collective-permute-done.1.rows_w = f32[15,8,128]{2,1,0:T(8,128)S(1)} collective-permute-done((f32[15,8,128]{2,1,0:T(8,128)S(1)}, f32[15,8,128]{2,1,0:T(8,128)S(1)}, u32[]{:S(2)}, u32[]{:S(2)}) %collective-permute-start.1) | collective-permute-done | bytes 61472 | tf_op jit(solution)/shard_map/ppermute | solution.py:633
  13.0 5.7 %collective-permute-start.2 = (f32[26,8,128]{2,1,0:T(8,128)S(1)}, f32[26,8,128]{2,1,0:T(8,128)S(1)}, u32[]{:S(2)}, u32[]{:S(2)}) collective-permute-start(f32[26,8,128]{2,1,0:T(8,128)S(1)} %get-tuple-element.47), channel_id=1, source_target_pairs={{1,0},{2,1},{3,2},{4,3},{5,4},{6,5},{7,6},{0,7},{9,8},{10,9},{11,1... | collective-permute-start | bytes 319496 | tf_op jit(solution)/shard_map/ppermute | solution.py:641
  18.6 0.0 collective-permute-start.3
  18.7 1.7 %collective-permute-done.2.cols_n.refs_7_.refs_6_ = f32[26,8,128]{2,1,0:T(8,128)S(1)} collective-permute-done((f32[26,8,128]{2,1,0:T(8,128)S(1)}, f32[26,8,128]{2,1,0:T(8,128)S(1)}, u32[]{:S(2)}, u32[]{:S(2)}) %collective-permute-start.2) | collective-permute-done | bytes 106528 | tf_op jit(solution)/shard_map/ppermute | solution.py:641
  20.4 7.1 %collective-permute-start.4 = (f32[72,8,128]{2,1,0:T(8,128)S(1)}, f32[72,8,128]{2,1,0:T(8,128)S(1)}, u32[]{:S(2)}, u32[]{:S(2)}) collective-permute-start(f32[72,8,128]{2,1,0:T(8,128)S(1)} %get-tuple-element.55.refs_1_.refs_0_), channel_id=1, source_target_pairs={{8,0},{16,8},{24,16},{32,24},{40,32},{48,40},{56,48},{64,56},{72,6... | collective-permute-start | bytes 884744 | tf_op jit(solution)/shard_map/ppermute | solution.py:647
  27.4 0.0 collective-permute-start.5
  27.4 0.0 collective-permute-done.3.cols_s.refs_8_.refs_7_
  27.5 0.7 first_surface.1
  28.1 23.0 %all_to_all.22 = f32[256,1,128]{2,1,0:T(1,128)S(1)} all-to-all(f32[256,1,128]{2,1,0:T(1,128)S(1)} %bitcast.10), channel_id=1, replica_groups=mesh['gx'=32,'gy'=8] {'gx','gy'}, dimensions={0} | all-to-all | bytes 262144 | tf_op jit(solution)/shard_map/all_to_all | solution.py:650
  51.1 0.0 collective-permute-done.4.refs_5_.refs_4_
  51.1 0.0 collective-permute-done.5.refs_6_.refs_5_
  51.1 5.7 %first_step.1 = (f32[48,16,128]{2,1,0:T(8,128)S(1)}, f32[48,16,128]{2,1,0:T(8,128)S(1)}, f32[31,8,128]{2,1,0:T(8,128)S(1)}, f32[31,8,128]{2,1,0:T(8,128)S(1)}, f...) custom-call(f32[48,16,128]{2,1,0:T(8,128)S(1)} %get-tuple-element.36.temp, f32[48,16,128]{2,1,0:T(8,128)S(1)} %get-tuple-element.37.salt, ...), custom_call_target="tpu_custom_call" | custom-call | tf_op jit(solution)/shard_map/first_step/pallas_call | solution.py:702
  56.8 0.7 collective-permute-start.6
  57.5 1.2 %collective-permute-start.7 = (f32[31,8,128]{2,1,0:T(8,128)S(1)}, f32[31,8,128]{2,1,0:T(8,128)S(1)}, u32[]{:S(2)}, u32[]{:S(2)}) collective-permute-start(f32[31,8,128]{2,1,0:T(8,128)S(1)} %get-tuple-element.62.high.refs_9_), channel_id=1, source_target_pairs={{0,8},{8,16},{16,24},{24,32},{32,40},{40,48},{48,56},{56,64},{64,7... | collective-permute-start | bytes 380936 | tf_op jit(solution)/shard_map/ppermute | solution.py:633
  58.6 2.6 %collective-permute-done.6.rows_e.refs_12_ = f32[31,8,128]{2,1,0:T(8,128)S(1)} collective-permute-done((f32[31,8,128]{2,1,0:T(8,128)S(1)}, f32[31,8,128]{2,1,0:T(8,128)S(1)}, u32[]{:S(2)}, u32[]{:S(2)}) %collective-permute-start.6) | collective-permute-done | bytes 127008 | tf_op jit(solution)/shard_map/ppermute | solution.py:632
  61.2 0.0 collective-permute-done.7.rows_w.refs_13_
  61.2 0.2 collective-permute-start.8
  61.4 1.4 %collective-permute-start.9 = (f32[12,8,128]{2,1,0:T(8,128)S(1)}, f32[12,8,128]{2,1,0:T(8,128)S(1)}, u32[]{:S(2)}, u32[]{:S(2)}) collective-permute-start(f32[12,8,128]{2,1,0:T(8,128)S(1)} %get-tuple-element.66), channel_id=1, source_target_pairs={{0,1},{1,2},{2,3},{3,4},{4,5},{5,6},{6,7},{7,0},{8,9},{9,10},{10,1... | collective-permute-start | bytes 147464 | tf_op jit(solution)/shard_map/ppermute | solution.py:642
  62.8 1.8 %collective-permute-done.8.cols_n.refs_14_ = f32[12,8,128]{2,1,0:T(8,128)S(1)} collective-permute-done((f32[12,8,128]{2,1,0:T(8,128)S(1)}, f32[12,8,128]{2,1,0:T(8,128)S(1)}, u32[]{:S(2)}, u32[]{:S(2)}) %collective-permute-start.8) | collective-permute-done | bytes 49184 | tf_op jit(solution)/shard_map/ppermute | solution.py:641
  64.6 1.2 %collective-permute-done.9.cols_s.refs_15_ = f32[12,8,128]{2,1,0:T(8,128)S(1)} collective-permute-done((f32[12,8,128]{2,1,0:T(8,128)S(1)}, f32[12,8,128]{2,1,0:T(8,128)S(1)}, u32[]{:S(2)}, u32[]{:S(2)}) %collective-permute-start.9) | collective-permute-done | bytes 49184 | tf_op jit(solution)/shard_map/ppermute | solution.py:642
  65.8 0.7 next_surface.1
  66.5 24.5 %all_to_all.23 = f32[256,1,128]{2,1,0:T(1,128)S(1)} all-to-all(f32[256,1,128]{2,1,0:T(1,128)S(1)} %bitcast.11), channel_id=1, replica_groups=mesh['gx'=32,'gy'=8] {'gx','gy'}, dimensions={0} | all-to-all | bytes 262144 | tf_op jit(solution)/shard_map/all_to_all | solution.py:650
  90.9 5.2 %last_step.1 = (f32[48,16,128]{2,1,0:T(8,128)}, f32[48,16,128]{2,1,0:T(8,128)}, f32[16,128]{1,0:T(8,128)}) custom-call(f32[48,16,128]{2,1,0:T(8,128)S(1)} %get-tuple-element.59.temp, f32[48,16,128]{2,1,0:T(8,128)S(1)} %get-tuple-element.60.salt, f32[48,16,128]{2,1,0:T(8,128)S(1)} %get-tuple-element.38.temp_response, ...), custom_call_target="tpu_custom_call" | custom-call | tf_op jit(solution)/shard_map/last_step/pallas_call | solution.py:702
  (2 shorter events, 0.0 us)
Async XLA Ops:
  6.0 4.7 %collective-permute-start = (f32[15,8,128]{2,1,0:T(8,128)S(1)}, f32[15,8,128]{2,1,0:T(8,128)S(1)}, u32[]{:S(2)}, u32[]{:S(2)}) collective-permute-start(f32[15,8,128]{2,1,0:T(8,128)S(1)} %get-tuple-element.43.low), channel_id=1, source_target_pairs={{8,0},{16,8},{24,16},{32,24},{40,32},{48,40},{56,48},{64,56},{72,6... | collective-permute-start | bytes 184328 | tf_op jit(solution)/shard_map/ppermute | solution.py:632
  9.3 3.7 %collective-permute-start.1 = (f32[15,8,128]{2,1,0:T(8,128)S(1)}, f32[15,8,128]{2,1,0:T(8,128)S(1)}, u32[]{:S(2)}, u32[]{:S(2)}) collective-permute-start(f32[15,8,128]{2,1,0:T(8,128)S(1)} %get-tuple-element.44.high), channel_id=1, source_target_pairs={{0,8},{8,16},{16,24},{24,32},{32,40},{40,48},{48,56},{56,64},{64,7... | collective-permute-start | bytes 184328 | tf_op jit(solution)/shard_map/ppermute | solution.py:633
  13.0 7.4 %collective-permute-start.2 = (f32[26,8,128]{2,1,0:T(8,128)S(1)}, f32[26,8,128]{2,1,0:T(8,128)S(1)}, u32[]{:S(2)}, u32[]{:S(2)}) collective-permute-start(f32[26,8,128]{2,1,0:T(8,128)S(1)} %get-tuple-element.47), channel_id=1, source_target_pairs={{1,0},{2,1},{3,2},{4,3},{5,4},{6,5},{7,6},{0,7},{9,8},{10,9},{11,1... | collective-permute-start | bytes 319496 | tf_op jit(solution)/shard_map/ppermute | solution.py:641
  18.6 8.8 %collective-permute-start.3 = (f32[26,8,128]{2,1,0:T(8,128)S(1)}, f32[26,8,128]{2,1,0:T(8,128)S(1)}, u32[]{:S(2)}, u32[]{:S(2)}) collective-permute-start(f32[26,8,128]{2,1,0:T(8,128)S(1)} %get-tuple-element.48), channel_id=1, source_target_pairs={{0,1},{1,2},{2,3},{3,4},{4,5},{5,6},{6,7},{7,0},{8,9},{9,10},{10,1... | collective-permute-start | bytes 319496 | tf_op jit(solution)/shard_map/ppermute | solution.py:642
  20.4 30.7 %collective-permute-start.4 = (f32[72,8,128]{2,1,0:T(8,128)S(1)}, f32[72,8,128]{2,1,0:T(8,128)S(1)}, u32[]{:S(2)}, u32[]{:S(2)}) collective-permute-start(f32[72,8,128]{2,1,0:T(8,128)S(1)} %get-tuple-element.55.refs_1_.refs_0_), channel_id=1, source_target_pairs={{8,0},{16,8},{24,16},{32,24},{40,32},{48,40},{56,48},{64,56},{72,6... | collective-permute-start | bytes 884744 | tf_op jit(solution)/shard_map/ppermute | solution.py:647
  27.4 23.7 %collective-permute-start.5 = (f32[72,8,128]{2,1,0:T(8,128)S(1)}, f32[72,8,128]{2,1,0:T(8,128)S(1)}, u32[]{:S(2)}, u32[]{:S(2)}) collective-permute-start(f32[72,8,128]{2,1,0:T(8,128)S(1)} %get-tuple-element.56.refs_2_.refs_1_), channel_id=1, source_target_pairs={{0,8},{8,16},{16,24},{24,32},{32,40},{40,48},{48,56},{56,64},{64,7... | collective-permute-start | bytes 884744 | tf_op jit(solution)/shard_map/ppermute | solution.py:647
  56.8 4.4 %collective-permute-start.6 = (f32[31,8,128]{2,1,0:T(8,128)S(1)}, f32[31,8,128]{2,1,0:T(8,128)S(1)}, u32[]{:S(2)}, u32[]{:S(2)}) collective-permute-start(f32[31,8,128]{2,1,0:T(8,128)S(1)} %get-tuple-element.61.low.refs_8_), channel_id=1, source_target_pairs={{8,0},{16,8},{24,16},{32,24},{40,32},{48,40},{56,48},{64,56},{72,6... | collective-permute-start | bytes 380936 | tf_op jit(solution)/shard_map/ppermute | solution.py:632
  57.5 3.8 %collective-permute-start.7 = (f32[31,8,128]{2,1,0:T(8,128)S(1)}, f32[31,8,128]{2,1,0:T(8,128)S(1)}, u32[]{:S(2)}, u32[]{:S(2)}) collective-permute-start(f32[31,8,128]{2,1,0:T(8,128)S(1)} %get-tuple-element.62.high.refs_9_), channel_id=1, source_target_pairs={{0,8},{8,16},{16,24},{24,32},{32,40},{40,48},{48,56},{56,64},{64,7... | collective-permute-start | bytes 380936 | tf_op jit(solution)/shard_map/ppermute | solution.py:633
  61.2 3.3 %collective-permute-start.8 = (f32[12,8,128]{2,1,0:T(8,128)S(1)}, f32[12,8,128]{2,1,0:T(8,128)S(1)}, u32[]{:S(2)}, u32[]{:S(2)}) collective-permute-start(f32[12,8,128]{2,1,0:T(8,128)S(1)} %get-tuple-element.65), channel_id=1, source_target_pairs={{1,0},{2,1},{3,2},{4,3},{5,4},{6,5},{7,6},{0,7},{9,8},{10,9},{11,1... | collective-permute-start | bytes 147464 | tf_op jit(solution)/shard_map/ppermute | solution.py:641
  61.4 4.3 %collective-permute-start.9 = (f32[12,8,128]{2,1,0:T(8,128)S(1)}, f32[12,8,128]{2,1,0:T(8,128)S(1)}, u32[]{:S(2)}, u32[]{:S(2)}) collective-permute-start(f32[12,8,128]{2,1,0:T(8,128)S(1)} %get-tuple-element.66), channel_id=1, source_target_pairs={{0,1},{1,2},{2,3},{3,4},{4,5},{5,6},{6,7},{7,0},{8,9},{9,10},{10,1... | collective-permute-start | bytes 147464 | tf_op jit(solution)/shard_map/ppermute | solution.py:642

commit v6 on v5

--- a/solution.py
+++ b/solution.py
@@ -74,9 +74,10 @@
     return lax.broadcasted_iota(jnp.int32, shape, axis)
 
 
-A_CORNERS, T_CORNERS = 6, 3
+A_CORNERS, T_CORNERS = 1, 3
 A_SURFACE, T_SURFACE = 2 * A_CORNERS, 2 * T_CORNERS
 A_ROWS, T_ROWS = A_SURFACE + 3, T_SURFACE + 1
+STRIPS = 12
 
 
 def put_rows(low_ref, high_ref, first, field, group, j, cells):
@@ -108,7 +109,7 @@
 
 def put_cols(refs, n, low, high):
     row_low, row_high, col_low, col_high = refs
-    count = corners_of(row_low)
+    count = 0 if row_low is None else corners_of(row_low)
     for col, side, cells in ((col_low, 0, low), (col_high, count, high)):
         col[2 * n] = cells[:8]
         col[2 * n + 1] = cells[8:]
@@ -121,89 +122,138 @@
     return A_CORNERS if rows.shape[0] == A_ROWS else T_CORNERS
 
 
-def forward_kernel(own_low, own_high, rows_e, rows_w, to_south, to_north):
+def forward_kernel(own_low, own_high, rows_e, rows_w, *refs):
     count = rows_e.shape[0] // 2
     own = own_low.shape[0]
+    more, outs = refs[:-2], refs[-2:]
     place = lax.axis_index("gy")
     ends_at = 0, lax.axis_size("gy") - 1
-    for out, mine, side, end in zip((to_south, to_north), (own_low, own_high), (0, count), ends_at):
+    for n, (out, mine, end) in enumerate(zip(outs, (own_low, own_high), ends_at)):
         inner = place != end
+        side = n * count
         out[:own] = jnp.where(inner, mine[...], 0.0)
         out[own : own + count] = jnp.where(inner, rows_e[side : side + count], 0.0)
-        out[own + count :] = jnp.where(inner, rows_w[side : side + count], 0.0)
+        out[own + count : own + 2 * count] = jnp.where(inner, rows_w[side : side + count], 0.0)
+        if more:
+            out[own + 2 * count :] = jnp.where(inner, more[n][...], 0.0)
+
+
+def strip_corner_kernel(_low, _high, cols_n, cols_s, out_low, out_high):
+    for side, cols in enumerate((cols_n, cols_s)):
+        for n in range(5):
+            out_low[5 * side + n] = cols[4 + 2 * n]
+            out_high[5 * side + n] = cols[5 + 2 * n]
+    for out in (out_low, out_high):
+        out[10:] = jnp.zeros((STRIPS - 10, 8, COLS), F32)
 
 
 def wet_at(mask, last, level):
     return jnp.where(last > level, mask[jnp.minimum(level, LEVELS - 1)], 0).astype(F32)
 
 
-def prepare_kernel(
-    mix, thermal, haline, temp_in, salt_in, east_in, north_in, mask_in, bottom, surface, diag,
-    row_low, row_high, col_low, col_high, strip_low, strip_high, *rest,
+def combine_kernel(
+    mix, thermal, haline, temp_in, salt_in, mask_in, bottom, surface, diag,
+    row_low, row_high, col_low, col_high, temp, salt, wets, kept, mask, sems,
 ):
-    solved, rest = rest[:4], rest[4:]
-    inverses, ratios, east, north, wets, kept, temp, salt, mask, sems = rest
     last = bottom[...]
     zero = jnp.zeros((ROWS, COLS), F32)
-    pair = (zero, zero)
-    fields = list(
-        zip((mask_in, temp_in, salt_in, east_in, north_in), (mask, temp, salt, east, north))
-    )
+    fields = (mask_in, mask), (temp_in, temp), (salt_in, salt)
+    parts = LEVELS // CHUNK
 
     def copy(n, part):
         source, target = fields[n]
         levels = pl.ds(part * CHUNK, CHUNK)
         return pltpu.make_async_copy(source.at[levels], target.at[levels], sems.at[n, part])
 
-    parts = LEVELS // CHUNK
     for part in range(parts):
-        copy(0, part).start()
-    for part in range(parts):
-        for n in range(1, 5):
+        for n in range(3):
             copy(n, part).start()
 
-    def down_body(group, carry):
-        total, depth, up, ratio, values, wet, packs = carry
+    def body(group, carry):
+        total, depth = carry
         for j in range(4):
             level = group * 4 + j
-            below = wet_at(mask, last, level + 1)
-            down = mix[level] * (wet * below)
-            inverse = 1.0 / ((1.0 + up + down) - up * ratio)
-            t, s = temp[level], salt[level]
-            tw, hw = thermal[level] * wet, haline[level] * wet
-            total = total + (tw * t - hw * s)
-            depth = depth + wet
+            wet = jnp.where(last > level, mask[level], 0).astype(F32)
             wets[level] = wet
             for n, weight in enumerate((mix, thermal, haline)):
                 kept[n, level] = jnp.full((8, COLS), weight[level], F32)
-            values = tuple((r + up * v) * inverse for r, v in zip((t, s, tw, hw), values))
+            total = total + wet * (thermal[level] * temp[level] - haline[level] * salt[level])
+            depth = depth + wet
+        return total, depth
+
+    carry = zero, zero
+    step = CHUNK // 4
+    for part in range(parts):
+        for n in range(3):
+            copy(n, part).wait()
+        carry = lax.fori_loop(part * step, (part + 1) * step, body, carry)
+    total, depth = carry
+    refs = row_low, row_high, col_low, col_high
+    put_surface(refs, A_SURFACE, (surface[...] + total, depth / LEVELS, diag[...]))
+
+
+def weight_at(kept, n, level):
+    value = kept[n, level]
+    return jnp.concatenate([value, value], axis=0)
+
+
+def solve_kernel(
+    temp, salt, wets, kept, east_in, north_in,
+    col_low, col_high, strip_low, strip_high, *rest,
+):
+    solved, (inverses, ratios, east, north, sems) = rest[:4], rest[4:]
+    zero = jnp.zeros((ROWS, COLS), F32)
+    pair = (zero, zero)
+    copies = [
+        pltpu.make_async_copy(source, target, sems.at[n])
+        for n, (source, target) in enumerate(((east_in, east), (north_in, north)))
+    ]
+    for copy in copies:
+        copy.start()
+
+    def down_body(group, carry):
+        up, ratio, values, wet, pack = carry
+        for j in range(4):
+            level = group * 4 + j
+            below = jnp.where(
+                level < LEVELS - 1, wets[jnp.minimum(level + 1, LEVELS - 1)], 0.0
+            )
+            down = weight_at(kept, 0, level) * (wet * below)
+            inverse = 1.0 / ((1.0 + up + down) - up * ratio)
+            sources = (
+                temp[level],
+                salt[level],
+                weight_at(kept, 1, level) * wet,
+                weight_at(kept, 2, level) * wet,
+            )
+            values = tuple((r + up * v) * inverse for r, v in zip(sources, values))
             for ref, v in zip(solved, values):
                 ref[level] = v
             ratio = down * inverse
             inverses[level] = inverse
             ratios[level] = ratio
-            put_rows(strip_low, strip_high, 0, 2, group, j, wet)
-            put_rows(strip_low, strip_high, 0, 5, group, j, east[level])
-            packs = tuple(packed(acc, v, level) for acc, v in zip(packs, (wet, north[level])))
+            put_rows(strip_low, strip_high, STRIPS, 2, group, j, wet)
+            pack = packed(pack, wet, level)
             up = down
             wet = below
-        return total, depth, up, ratio, values, wet, packs
-
-    for part in range(parts):
-        copy(0, part).wait()
-    carry = (zero, zero, zero, zero, (zero,) * 4, wet_at(mask, last, 0), (pair, pair))
-    step = CHUNK // 4
-    for part in range(parts):
-        for n in range(1, 5):
-            copy(n, part).wait()
-        carry = lax.fori_loop(part * step, (part + 1) * step, down_body, carry)
-    total, depth, _, _, _, _, packs = carry
-    refs = row_low, row_high, col_low, col_high
-    put_surface(refs, A_SURFACE, (surface[...] + total, depth / LEVELS, diag[...]))
-    put_cols(refs, 3, *packs[0])
-    put_cols(refs, 6, *packs[1])
+        return up, ratio, values, wet, pack
+
+    carry = lax.fori_loop(0, GROUPS, down_body, (zero, zero, (zero,) * 4, wets[0], pair))
+    refs = None, None, col_low, col_high
+    put_cols(refs, 2, *carry[-1])
+    for copy in copies:
+        copy.wait()
+
+    def flow_body(group, pack):
+        for j in range(4):
+            level = group * 4 + j
+            put_rows(strip_low, strip_high, STRIPS, 5, group, j, east[level])
+            pack = packed(pack, north[level], level)
+        return pack
+
+    put_cols(refs, 5, *lax.fori_loop(0, GROUPS, flow_body, pair))
     strips = strip_low, strip_high
-    back_substitute(refs, strips, 0, solved, ratios, ((0, 1), (1, 2), (3, 4), (4, 5)))
+    back_substitute(refs, strips, STRIPS, solved, ratios, ((0, 0), (1, 1), (3, 3), (4, 4)))
 
 
 def back_substitute(refs, strips, first, solved, ratios, places):
@@ -344,9 +394,11 @@
 
 
 class Halo:
-    def __init__(self, refs, first, corners):
+    def __init__(self, refs, late):
         self.low, self.high, self.own_s, self.own_n, self.e, self.w, self.n, self.s = refs
-        self.first, self.corners = first, corners
+        self.late = late
+        self.first = STRIPS if late else T_ROWS
+        self.own_at, self.far_at = (-2, 2) if late else (0, 0)
         self.even_row = iota((8, COLS), 0) % 2 == 0
         self.even_lane = iota((8, COLS), 1) % 2 == 0
         self.sub = iota((8, COLS), 0)
@@ -365,28 +417,33 @@
         return jnp.where(self.even_row, self.e[at], self.w[at])
 
     def edge_columns(self, block):
+        at = self.far_at + 2 * block
         return jnp.concatenate(
-            [
-                jnp.where(self.even_lane, self.n[2 * block + h], self.s[2 * block + h])
-                for h in range(2)
-            ],
-            axis=0,
-        )
+            [jnp.where(self.even_lane, self.n[at + h], self.s[at + h]) for h in range(2)], axis=0
+        )
+
+    def corners(self, block):
+        if self.late:
+            at = block - 1
+            return self.e[at], self.e[at + 5], self.w[at], self.w[at + 5]
+        east = self.n.shape[0] - 2 * T_CORNERS + block
+        west = east + T_CORNERS
+        return self.n[east], self.s[east], self.n[west], self.s[west]
 
     def columns(self, block):
         inner, outer = [], []
         for h in range(2):
-            at = 2 * block + h
+            at = self.own_at + 2 * block + h
             inner.append(
                 jnp.where(self.even_lane, roll(self.own_n[at], -1, 1), roll(self.own_s[at], 1, 1))
             )
+            at = self.far_at + 2 * block + h
             outer.append(jnp.where(self.even_lane, roll(self.n[at], -1, 1), roll(self.s[at], 1, 1)))
-        east = self.n.shape[0] - 2 * self.corners + block
-        west = east + self.corners
+        ne, se, nw, sw = self.corners(block)
         corner = jnp.where(
             self.sub < 4,
-            jnp.where(self.even_lane, self.n[east], self.s[east]),
-            jnp.where(self.even_lane, self.n[west], self.s[west]),
+            jnp.where(self.even_lane, ne, se),
+            jnp.where(self.even_lane, nw, sw),
         )
         return (
             jnp.concatenate(inner, axis=0),
@@ -406,14 +463,10 @@
 ):
     if not final:
         kept, refs = refs[0], refs[1:]
-
-        def weight(n, level):
-            value = kept[n, level]
-            return jnp.concatenate([value, value], axis=0)
-
-    a_halo = Halo(refs[:8], 0, A_CORNERS)
+        weight = functools.partial(weight_at, kept)
+    a_halo = Halo(refs[:8], True)
     if final:
-        t_halo = Halo(refs[8:16], T_ROWS, T_CORNERS)
+        t_halo = Halo(refs[8:16], False)
         new_temp, new_salt, new_surface = refs[16:]
     else:
         t_halo = a_halo
@@ -597,8 +650,10 @@
     return pl.BlockSpec(block, lambda i: (0,) * len(block), memory_space=pltpu.VMEM)
 
 
-def call(kernel, outs, in_specs, out_specs=None, scratch=(), name=None, grid=None, room=40):
+def call(kernel, outs, in_specs, out_specs=None, scratch=(), name=None, grid=None, room=40, aliases=None):
     extra = {} if grid is None else {"grid": grid}
+    if aliases:
+        extra["input_output_aliases"] = aliases
     return pl.pallas_call(
         kernel,
         out_shape=outs,
@@ -627,24 +682,33 @@
     def back(pairs):
         return [(b, a) for a, b in pairs]
 
-    def exchange(messages, corners):
+    def exchange(messages, corners, behind=()):
         row_low, row_high, col_low, col_high = messages
         rows_e = lax.ppermute(row_low, "gx", back(eastward))
         rows_w = lax.ppermute(row_high, "gx", eastward)
         own = col_low.shape[0]
-        out = shape(own + 2 * corners, 8, COLS)
+        out = shape(own + 2 * corners + sum(b.shape[0] for b in behind[:1]), 8, COLS)
         to_south, to_north = call(
             forward_kernel, [out, out],
-            [head(own, 8, COLS)] * 2 + [head(2 * corners, 8, COLS)] * 2,
+            [head(own, 8, COLS)] * 2
+            + [head(2 * corners, 8, COLS)] * 2
+            + [head(*b.shape) for b in behind],
             [head(*out.shape)] * 2, name="corners", grid=(1,),
-        )(col_low, col_high, rows_e, rows_w)
+        )(col_low, col_high, rows_e, rows_w, *behind)
         cols_n = lax.ppermute(to_south, "gy", back(northward))
         cols_s = lax.ppermute(to_north, "gy", northward)
         return [rows_e, rows_w, cols_n, cols_s]
 
-    def exchange_strips(low, high, after):
-        low, high, _ = lax.optimization_barrier((low, high, after))
-        return [lax.ppermute(low, "gx", back(eastward)), lax.ppermute(high, "gx", eastward)]
+    def exchange_strips(low, high, cols_n, cols_s):
+        block = head(STRIPS, 8, COLS)
+        low, high = call(
+            strip_corner_kernel, [shape(*low.shape)] * 2,
+            [block] * 2 + [head(*cols_n.shape)] * 2, [block] * 2,
+            name="strip_corners", grid=(1,), aliases={0: 0, 1: 1},
+        )(low, high, cols_n, cols_s)
+        return [low, high], [
+            lax.ppermute(low, "gx", back(eastward)), lax.ppermute(high, "gx", eastward)
+        ]
 
     def all_sum(block):
         return lax.all_to_all(block, both, 0, 0, tiled=True)
@@ -664,33 +728,41 @@
         sens_temp, sens_salt, sens_surface, flow_east, flow_north, mix_profile,
         thermal_weight, haline_weight, surface_diag, land_mask, bottom_level,
     ):
-        *sent, strip_low, strip_high, temp, salt, temp_response, salt_response, inverses, ratios, east, north, wets, kept = call(
-            prepare_kernel,
-            message_shapes(3, 0, 6, 5)
-            + [shape(6 * GROUPS, 8, COLS)] * 2
-            + [field] * 9
-            + [shape(3, LEVELS, 8, COLS)],
-            [SMEM] * 3 + [HBM] * 5 + [VMEM] * 3,
-            scratch=[pltpu.VMEM((LEVELS, ROWS, COLS), F32)] * 2
-            + [pltpu.VMEM((LEVELS, ROWS, COLS), jnp.int32)]
-            + [pltpu.SemaphoreType.DMA((5, LEVELS // CHUNK))],
-            name="prepare",
+        def in_hbm(*xs):
+            return [pltpu.with_memory_space_constraint(x, pltpu.HBM) for x in xs]
+
+        *sent, temp, salt, wets, kept = call(
+            combine_kernel,
+            message_shapes(3, 0, 0, 0) + [field] * 3 + [shape(3, LEVELS, 8, COLS)],
+            [SMEM] * 3 + [HBM] * 3 + [VMEM] * 3,
+            scratch=[
+                pltpu.VMEM((LEVELS, ROWS, COLS), jnp.int32),
+                pltpu.SemaphoreType.DMA((3, LEVELS // CHUNK)),
+            ],
+            name="combine",
         )(
-            *(
-                pltpu.with_memory_space_constraint(x, pltpu.HBM)
-                for x in (
-                    mix_profile, thermal_weight, haline_weight, sens_temp, sens_salt, flow_east,
-                    flow_north, land_mask, bottom_level, sens_surface, surface_diag,
-                )
+            *in_hbm(
+                mix_profile, thermal_weight, haline_weight, sens_temp, sens_salt, land_mask,
+                bottom_level, sens_surface, surface_diag,
             )
         )
-        got = exchange(sent, A_CORNERS)
-        strips = exchange_strips(strip_low, strip_high, got[2])
-        halo = [strip_low, strip_high, *sent[2:], *strips, *got[2:]]
+        cols = shape(12, 8, COLS)
+        strip = shape(STRIPS + 6 * GROUPS, 8, COLS)
+        (col_low, col_high, strip_low, strip_high,
+         temp, salt, temp_response, salt_response, inverses, ratios, east, north) = call(
+            solve_kernel,
+            [cols, cols, strip, strip] + [field] * 8,
+            [VMEM] * 4 + [HBM] * 2,
+            scratch=[pltpu.SemaphoreType.DMA((2,))],
+            name="solve",
+        )(temp, salt, wets, kept, *in_hbm(flow_east, flow_north))
+        got = exchange(sent, A_CORNERS, (col_low, col_high))
+        strips, far_strips = exchange_strips(strip_low, strip_high, got[2], got[3])
+        halo = [*strips, col_low, col_high, *far_strips, *got[2:]]
         basis, gram, fixed = call(
             first_surface_kernel,
             [basis_shape, gram_shape, shape(2, 32, 2 * COLS)],
-            surface_specs(A_ROWS, 2 * 7 + 2 * A_CORNERS),
+            surface_specs(A_ROWS, 2 + 2 * A_CORNERS),
             [head(4, 32, 2 * COLS), head(devices, COLS), head(2, 32, 2 * COLS)],
             name="first_surface",
             grid=(1,),

time: 96.3 us -> 95.2 us (0.989)
  blocking collectives: 47.5 us -> 46.4 us
  waiting for transfers between devices: 11 us -> 9.92 us
    ppermute x2, waiting for transfers between devices: 1.22 us -> 4.21 us  [exchange(): cols_s = lax.ppermute(to_north, 'gy', northward)]
    ppermute x2, waiting for transfers between devices: 2.3 us -> 0.01 us  [exchange(): rows_w = lax.ppermute(row_high, 'gx', eastward)]
    ppermute x2, waiting for transfers between devices: 3.95 us -> 2.61 us  [exchange(): rows_e = lax.ppermute(row_low, 'gx', back(eastward))]
    all_to_all x2, blocking collectives: 47.5 us -> 46.4 us  [all_sum(): return lax.all_to_all(block, both, 0, 0, tiled=True)]
    pallas_call x1 -> x3, Pallas kernels: 5.35 us -> 6.27 us  [the longest x1 3.88 us: per_device(): call(solve_kernel, [cols, cols, strip, strip] + [field] * 8, [VMEM] * 4 +...]
  transfers between devices with their start and end apart: 10 -> 10, of which waited for: 6 -> 5; matrix products, arithmetic and copies ran while one was open for 0% -> 0% of each run, Pallas kernels for 1% -> 5%
where the time goes in v6:
time: 95.2 us; the launch traced here: 94.9 us
  blocking collectives  46.4 us (49%)
  starting transfers between devices  19.4 us (20%)
  Pallas kernels  18.5 us (19%)
  waiting for transfers between devices  9.92 us (10%)
    all_to_all x2, blocking collectives, all_sum(): return lax.all_to_all(block, both, 0, 0, tiled=True)  46.4 us
    pallas_call x2, Pallas kernels, step(): call(functools.partial(step_kernel, final), outs, [VMEM] * (18 + len(weig...  10.8 us
    ppermute x1, starting transfers between devices, exchange_strips(): lax.ppermute(low, 'gx', back(eastward))  7.35 us
    ppermute x2, starting transfers between devices, exchange(): cols_n = lax.ppermute(to_south, 'gy', back(northward))  5.52 us
    ppermute x2, waiting for transfers between devices, exchange(): cols_s = lax.ppermute(to_north, 'gy', northward)  4.21 us
    ppermute x2, starting transfers between devices, exchange(): rows_e = lax.ppermute(row_low, 'gx', back(eastward))  3.98 us
    pallas_call x1, Pallas kernels, per_device(): call(solve_kernel, [cols, cols, strip, strip] + [field] * 8, [VMEM] * 4 +...  3.88 us
    ppermute x2, waiting for transfers between devices, exchange(): cols_n = lax.ppermute(to_south, 'gy', back(northward))  3.1 us
  transfers between devices with their start and end apart: 10, of which 5 were waited for; matrix products, arithmetic and copies ran while one was open for 0% of the time, Pallas kernels for 5%

profile of v6, /device:TPU:1, one launch (start us, length us, event | category | flops | bytes accessed | tf_op | source)
XLA Modules:
  0.0 94.9 jit_solution(10416263896180466722)
XLA Ops:
  0.6 2.4 %combine.1 = (f32[5,8,128]{2,1,0:T(8,128)S(1)}, f32[5,8,128]{2,1,0:T(8,128)S(1)}, f32[2,8,128]{2,1,0:T(8,128)S(1)}, f32[2,8,128]{2,1,0:T(8,128)S(1)}, f32[48,16,...) custom-call(f32[48]{0:T(128)} %mix.1, f32[48]{0:T(128)} %thermal.1, ...), custom_call_target="tpu_custom_call" | custom-call | tf_op jit(solution)/shard_map/combine/pallas_call | solution.py:734
  3.0 3.3 %collective-permute-start = (f32[5,8,128]{2,1,0:T(8,128)S(1)}, f32[5,8,128]{2,1,0:T(8,128)S(1)}, u32[]{:S(2)}, u32[]{:S(2)}) collective-permute-start(f32[5,8,128]{2,1,0:T(8,128)S(1)} %get-tuple-element.50.low), channel_id=1, source_target_pairs={{8,0},{16,8},{24,16},{32,24},{40,32},{48,40},{56,48},{64,56},{72,6... | collective-permute-start | bytes 61448 | tf_op jit(solution)/shard_map/ppermute | solution.py:687
  6.3 0.0 collective-permute-start.1
  6.4 3.9 %solve.1 = (f32[12,8,128]{2,1,0:T(8,128)S(1)}, f32[12,8,128]{2,1,0:T(8,128)S(1)}, f32[84,8,128]{2,1,0:T(8,128)S(1)}, f32[84,8,128]{2,1,0:T(8,128)S(1)}, f32[48,1...) custom-call(f32[48,16,128]{2,1,0:T(8,128)S(1)} %get-tuple-element.40, ...), custom_call_target="tpu_custom_call" | custom-call | tf_op jit(solution)/shard_map/solve/pallas_call | solution.py:752
  10.2 0.0 collective-permute-done.rows_e
  10.2 0.0 collective-permute-done.1.rows_w
  10.3 5.3 %collective-permute-start.2 = (f32[16,8,128]{2,1,0:T(8,128)S(1)}, f32[16,8,128]{2,1,0:T(8,128)S(1)}, u32[]{:S(2)}, u32[]{:S(2)}) collective-permute-start(f32[16,8,128]{2,1,0:T(8,128)S(1)} %get-tuple-element.56), channel_id=1, source_target_pairs={{1,0},{2,1},{3,2},{4,3},{5,4},{6,5},{7,6},{0,7},{9,8},{10,9},{11,1... | collective-permute-start | bytes 196616 | tf_op jit(solution)/shard_map/ppermute | solution.py:698
  15.6 0.0 collective-permute-start.3
  15.6 1.3 %collective-permute-done.2.cols_n.refs_7_.refs_6_ = f32[16,8,128]{2,1,0:T(8,128)S(1)} collective-permute-done((f32[16,8,128]{2,1,0:T(8,128)S(1)}, f32[16,8,128]{2,1,0:T(8,128)S(1)}, u32[]{:S(2)}, u32[]{:S(2)}) %collective-permute-start.2) | collective-permute-done | bytes 65568 | tf_op jit(solution)/shard_map/ppermute | solution.py:698
  17.0 3.0 %collective-permute-done.3.cols_s.refs_8_.refs_7_ = f32[16,8,128]{2,1,0:T(8,128)S(1)} collective-permute-done((f32[16,8,128]{2,1,0:T(8,128)S(1)}, f32[16,8,128]{2,1,0:T(8,128)S(1)}, u32[]{:S(2)}, u32[]{:S(2)}) %collective-permute-start.3) | collective-permute-done | bytes 65568 | tf_op jit(solution)/shard_map/ppermute | solution.py:699
  20.0 7.4 %collective-permute-start.4 = (f32[84,8,128]{2,1,0:T(8,128)S(1)}, f32[84,8,128]{2,1,0:T(8,128)S(1)}, u32[]{:S(2)}, u32[]{:S(2)}) collective-permute-start(f32[84,8,128]{2,1,0:T(8,128)S(1)} %get-tuple-element.63.refs_1_.refs_0_), channel_id=1, source_target_pairs={{8,0},{16,8},{24,16},{32,24},{40,32},{48,40},{56,48},{64,56},{72,6... | collective-permute-start | bytes 1032200 | tf_op jit(solution)/shard_map/ppermute | solution.py:710
  27.3 0.0 collective-permute-start.5
  27.3 0.7 first_surface.1
  28.0 22.0 %all_to_all.22 = f32[256,1,128]{2,1,0:T(1,128)S(1)} all-to-all(f32[256,1,128]{2,1,0:T(1,128)S(1)} %bitcast.10), channel_id=1, replica_groups=mesh['gx'=32,'gy'=8] {'gx','gy'}, dimensions={0} | all-to-all | bytes 262144 | tf_op jit(solution)/shard_map/all_to_all | solution.py:714
  50.0 0.0 collective-permute-done.4.refs_5_.refs_4_
  50.0 0.0 collective-permute-done.5.refs_6_.refs_5_
  50.0 5.7 %first_step.1 = (f32[48,16,128]{2,1,0:T(8,128)S(1)}, f32[48,16,128]{2,1,0:T(8,128)S(1)}, f32[31,8,128]{2,1,0:T(8,128)S(1)}, f32[31,8,128]{2,1,0:T(8,128)S(1)}, f...) custom-call(f32[48,16,128]{2,1,0:T(8,128)S(1)} %get-tuple-element.44.temp, f32[48,16,128]{2,1,0:T(8,128)S(1)} %get-tuple-element.45.salt, ...), custom_call_target="tpu_custom_call" | custom-call | tf_op jit(solution)/shard_map/first_step/pallas_call | solution.py:774
  55.7 0.7 collective-permute-start.6
  56.3 1.2 %collective-permute-start.7 = (f32[31,8,128]{2,1,0:T(8,128)S(1)}, f32[31,8,128]{2,1,0:T(8,128)S(1)}, u32[]{:S(2)}, u32[]{:S(2)}) collective-permute-start(f32[31,8,128]{2,1,0:T(8,128)S(1)} %get-tuple-element.70.high.refs_9_), channel_id=1, source_target_pairs={{0,8},{8,16},{16,24},{24,32},{32,40},{40,48},{48,56},{56,64},{64,7... | collective-permute-start | bytes 380936 | tf_op jit(solution)/shard_map/ppermute | solution.py:688
  57.5 2.6 %collective-permute-done.6.rows_e.refs_12_ = f32[31,8,128]{2,1,0:T(8,128)S(1)} collective-permute-done((f32[31,8,128]{2,1,0:T(8,128)S(1)}, f32[31,8,128]{2,1,0:T(8,128)S(1)}, u32[]{:S(2)}, u32[]{:S(2)}) %collective-permute-start.6) | collective-permute-done | bytes 127008 | tf_op jit(solution)/shard_map/ppermute | solution.py:687
  60.1 0.0 collective-permute-done.7.rows_w.refs_13_
  60.1 0.2 collective-permute-start.8
  60.3 1.4 %collective-permute-start.9 = (f32[12,8,128]{2,1,0:T(8,128)S(1)}, f32[12,8,128]{2,1,0:T(8,128)S(1)}, u32[]{:S(2)}, u32[]{:S(2)}) collective-permute-start(f32[12,8,128]{2,1,0:T(8,128)S(1)} %get-tuple-element.74), channel_id=1, source_target_pairs={{0,1},{1,2},{2,3},{3,4},{4,5},{5,6},{6,7},{7,0},{8,9},{9,10},{10,1... | collective-permute-start | bytes 147464 | tf_op jit(solution)/shard_map/ppermute | solution.py:699
  61.6 1.8 %collective-permute-done.8.cols_n.refs_14_ = f32[12,8,128]{2,1,0:T(8,128)S(1)} collective-permute-done((f32[12,8,128]{2,1,0:T(8,128)S(1)}, f32[12,8,128]{2,1,0:T(8,128)S(1)}, u32[]{:S(2)}, u32[]{:S(2)}) %collective-permute-start.8) | collective-permute-done | bytes 49184 | tf_op jit(solution)/shard_map/ppermute | solution.py:698
  63.4 1.2 %collective-permute-done.9.cols_s.refs_15_ = f32[12,8,128]{2,1,0:T(8,128)S(1)} collective-permute-done((f32[12,8,128]{2,1,0:T(8,128)S(1)}, f32[12,8,128]{2,1,0:T(8,128)S(1)}, u32[]{:S(2)}, u32[]{:S(2)}) %collective-permute-start.9) | collective-permute-done | bytes 49184 | tf_op jit(solution)/shard_map/ppermute | solution.py:699
  64.6 0.7 next_surface.1
  65.3 24.5 %all_to_all.23 = f32[256,1,128]{2,1,0:T(1,128)S(1)} all-to-all(f32[256,1,128]{2,1,0:T(1,128)S(1)} %bitcast.11), channel_id=1, replica_groups=mesh['gx'=32,'gy'=8] {'gx','gy'}, dimensions={0} | all-to-all | bytes 262144 | tf_op jit(solution)/shard_map/all_to_all | solution.py:714
  89.8 5.1 %last_step.1 = (f32[48,16,128]{2,1,0:T(8,128)}, f32[48,16,128]{2,1,0:T(8,128)}, f32[16,128]{1,0:T(8,128)}) custom-call(f32[48,16,128]{2,1,0:T(8,128)S(1)} %get-tuple-element.67.temp, f32[48,16,128]{2,1,0:T(8,128)S(1)} %get-tuple-element.68.salt, f32[48,16,128]{2,1,0:T(8,128)S(1)} %get-tuple-element.46.temp_response, ...), custom_call_target="tpu_custom_call" | custom-call | tf_op jit(solution)/shard_map/last_step/pallas_call | solution.py:774
  (3 shorter events, 0.1 us)
Async XLA Ops:
  3.0 7.2 %collective-permute-start = (f32[5,8,128]{2,1,0:T(8,128)S(1)}, f32[5,8,128]{2,1,0:T(8,128)S(1)}, u32[]{:S(2)}, u32[]{:S(2)}) collective-permute-start(f32[5,8,128]{2,1,0:T(8,128)S(1)} %get-tuple-element.50.low), channel_id=1, source_target_pairs={{8,0},{16,8},{24,16},{32,24},{40,32},{48,40},{56,48},{64,56},{72,6... | collective-permute-start | bytes 61448 | tf_op jit(solution)/shard_map/ppermute | solution.py:687
  6.3 3.9 %collective-permute-start.1 = (f32[5,8,128]{2,1,0:T(8,128)S(1)}, f32[5,8,128]{2,1,0:T(8,128)S(1)}, u32[]{:S(2)}, u32[]{:S(2)}) collective-permute-start(f32[5,8,128]{2,1,0:T(8,128)S(1)} %get-tuple-element.51.high), channel_id=1, source_target_pairs={{0,8},{8,16},{16,24},{24,32},{32,40},{40,48},{48,56},{56,64},{64,7... | collective-permute-start | bytes 61448 | tf_op jit(solution)/shard_map/ppermute | solution.py:688
  10.3 6.7 %collective-permute-start.2 = (f32[16,8,128]{2,1,0:T(8,128)S(1)}, f32[16,8,128]{2,1,0:T(8,128)S(1)}, u32[]{:S(2)}, u32[]{:S(2)}) collective-permute-start(f32[16,8,128]{2,1,0:T(8,128)S(1)} %get-tuple-element.56), channel_id=1, source_target_pairs={{1,0},{2,1},{3,2},{4,3},{5,4},{6,5},{7,6},{0,7},{9,8},{10,9},{11,1... | collective-permute-start | bytes 196616 | tf_op jit(solution)/shard_map/ppermute | solution.py:698
  15.6 4.3 %collective-permute-start.3 = (f32[16,8,128]{2,1,0:T(8,128)S(1)}, f32[16,8,128]{2,1,0:T(8,128)S(1)}, u32[]{:S(2)}, u32[]{:S(2)}) collective-permute-start(f32[16,8,128]{2,1,0:T(8,128)S(1)} %get-tuple-element.57), channel_id=1, source_target_pairs={{0,1},{1,2},{2,3},{3,4},{4,5},{5,6},{6,7},{7,0},{8,9},{9,10},{10,1... | collective-permute-start | bytes 196616 | tf_op jit(solution)/shard_map/ppermute | solution.py:699
  20.0 30.0 %collective-permute-start.4 = (f32[84,8,128]{2,1,0:T(8,128)S(1)}, f32[84,8,128]{2,1,0:T(8,128)S(1)}, u32[]{:S(2)}, u32[]{:S(2)}) collective-permute-start(f32[84,8,128]{2,1,0:T(8,128)S(1)} %get-tuple-element.63.refs_1_.refs_0_), channel_id=1, source_target_pairs={{8,0},{16,8},{24,16},{32,24},{40,32},{48,40},{56,48},{64,56},{72,6... | collective-permute-start | bytes 1032200 | tf_op jit(solution)/shard_map/ppermute | solution.py:710
  27.3 22.7 %collective-permute-start.5 = (f32[84,8,128]{2,1,0:T(8,128)S(1)}, f32[84,8,128]{2,1,0:T(8,128)S(1)}, u32[]{:S(2)}, u32[]{:S(2)}) collective-permute-start(f32[84,8,128]{2,1,0:T(8,128)S(1)} %get-tuple-element.64.refs_2_.refs_1_), channel_id=1, source_target_pairs={{0,8},{8,16},{16,24},{24,32},{32,40},{40,48},{48,56},{56,64},{64,7... | collective-permute-start | bytes 1032200 | tf_op jit(solution)/shard_map/ppermute | solution.py:710
  55.7 4.4 %collective-permute-start.6 = (f32[31,8,128]{2,1,0:T(8,128)S(1)}, f32[31,8,128]{2,1,0:T(8,128)S(1)}, u32[]{:S(2)}, u32[]{:S(2)}) collective-permute-start(f32[31,8,128]{2,1,0:T(8,128)S(1)} %get-tuple-element.69.low.refs_8_), channel_id=1, source_target_pairs={{8,0},{16,8},{24,16},{32,24},{40,32},{48,40},{56,48},{64,56},{72,6... | collective-permute-start | bytes 380936 | tf_op jit(solution)/shard_map/ppermute | solution.py:687
  56.3 3.8 %collective-permute-start.7 = (f32[31,8,128]{2,1,0:T(8,128)S(1)}, f32[31,8,128]{2,1,0:T(8,128)S(1)}, u32[]{:S(2)}, u32[]{:S(2)}) collective-permute-start(f32[31,8,128]{2,1,0:T(8,128)S(1)} %get-tuple-element.70.high.refs_9_), channel_id=1, source_target_pairs={{0,8},{8,16},{16,24},{24,32},{32,40},{40,48},{48,56},{56,64},{64,7... | collective-permute-start | bytes 380936 | tf_op jit(solution)/shard_map/ppermute | solution.py:688
  60.1 3.3 %collective-permute-start.8 = (f32[12,8,128]{2,1,0:T(8,128)S(1)}, f32[12,8,128]{2,1,0:T(8,128)S(1)}, u32[]{:S(2)}, u32[]{:S(2)}) collective-permute-start(f32[12,8,128]{2,1,0:T(8,128)S(1)} %get-tuple-element.73), channel_id=1, source_target_pairs={{1,0},{2,1},{3,2},{4,3},{5,4},{6,5},{7,6},{0,7},{9,8},{10,9},{11,1... | collective-permute-start | bytes 147464 | tf_op jit(solution)/shard_map/ppermute | solution.py:698
  60.3 4.3 %collective-permute-start.9 = (f32[12,8,128]{2,1,0:T(8,128)S(1)}, f32[12,8,128]{2,1,0:T(8,128)S(1)}, u32[]{:S(2)}, u32[]{:S(2)}) collective-permute-start(f32[12,8,128]{2,1,0:T(8,128)S(1)} %get-tuple-element.74), channel_id=1, source_target_pairs={{0,1},{1,2},{2,3},{3,4},{4,5},{5,6},{6,7},{7,0},{8,9},{9,10},{10,1... | collective-permute-start | bytes 147464 | tf_op jit(solution)/shard_map/ppermute | solution.py:699

commit v7 on v6

--- a/solution.py
+++ b/solution.py
@@ -467,10 +467,11 @@
     a_halo = Halo(refs[:8], True)
     if final:
         t_halo = Halo(refs[8:16], False)
-        new_temp, new_salt, new_surface = refs[16:]
+        arounds, diagonals = refs[16:18]
+        temp_out, salt_out, new_surface, new_temp, new_salt, sems = refs[18:]
     else:
         t_halo = a_halo
-        inverses, ratios, new_temp, new_salt, *messages = refs[8:]
+        inverses, ratios, new_temp, new_salt, arounds, diagonals, *messages = refs[8:]
     tracers = ((temp, temp_response, 0, 3, 1.0), (salt, salt_response, 1, 4, -1.0))
 
     weights = coefficients(gathered[...])
@@ -592,9 +593,14 @@
 
             wet = wets[level]
             fe, fn = east[level], north[level]
-            we, ww, wn, ws = four(wet, wet, wet, wet, row_wet, column_wet)
-            around = wet * ((we + ww) + (wn + ws))
-            diagonal = around + wet * (fe * (ww - we) + fn * (ws - wn))
+            if final:
+                around, diagonal = arounds[level], diagonals[level]
+            else:
+                we, ww, wn, ws = four(wet, wet, wet, wet, row_wet, column_wet)
+                around = wet * ((we + ww) + (wn + ws))
+                diagonal = around + wet * (fe * (ww - we) + fn * (ws - wn))
+                arounds[level] = around
+                diagonals[level] = diagonal
             done = []
             for n, (field, response, _, _, sign) in enumerate(tracers):
                 g = field[level] + (sign * multiplier) * response[level]
@@ -628,7 +634,17 @@
 
     zero = jnp.zeros((ROWS, COLS), F32)
     if final:
-        lax.fori_loop(0, GROUPS, body, 0)
+        copies = []
+        for part in range(LEVELS // CHUNK):
+            lax.fori_loop(part * CHUNK // 4, (part + 1) * CHUNK // 4, body, 0)
+            levels = pl.ds(part * CHUNK, CHUNK)
+            for n, (source, target) in enumerate(((new_temp, temp_out), (new_salt, salt_out))):
+                copies.append(
+                    pltpu.make_async_copy(source.at[levels], target.at[levels], sems.at[n, part])
+                )
+                copies[-1].start()
+        for copy in copies:
+            copy.wait()
     else:
         _, total, _, _ = lax.fori_loop(0, GROUPS, body, (zero,) * 4)
         put_surface(messages, T_SURFACE, (surface + total,))
@@ -770,20 +786,29 @@
         gathered = all_sum(gram)
 
         def step(final, temp, salt, basis, gathered, more, outs):
+            if final:
+                places = {
+                    "out_specs": [HBM, HBM, VMEM],
+                    "scratch": [pltpu.VMEM((LEVELS, ROWS, COLS), F32)] * 2
+                    + [pltpu.SemaphoreType.DMA((2, LEVELS // CHUNK))],
+                }
+            else:
+                places = {}
             weights = [] if final else [kept]
             return call(
                 functools.partial(step_kernel, final),
                 outs,
                 [VMEM] * (18 + len(weights) + len(more)),
                 name="last_step" if final else "first_step",
+                **places,
             )(
                 temp, salt, temp_response, salt_response, east, north, wets, fixed,
                 basis, gathered, *weights, *halo, *more,
             )
 
-        temp, salt, *second = step(
+        temp, salt, arounds, diagonals, *second = step(
             False, temp, salt, basis, gathered, [inverses, ratios],
-            [field, field] + message_shapes(1, 2, 2, 2),
+            [field] * 4 + message_shapes(1, 2, 2, 2),
         )
         more = exchange(second, T_CORNERS)
         basis, gram = call(
@@ -796,7 +821,7 @@
         )(second[0], second[1], *more, fixed)
         gathered = all_sum(gram)
         return tuple(
-            step(True, temp, salt, basis, gathered, [*second, *more], [field, field, tile])
+            step(True, temp, salt, basis, gathered, [*second, *more, arounds, diagonals], [field, field, tile])
         )
 
     in_specs = (

time: 95.2 us -> 94.8 us (level)
  no operation moved by 1% of the time
where the time goes in v7:
time: 94.8 us; the launch traced here: 94.6 us
  blocking collectives  46.4 us (49%)
  starting transfers between devices  19.4 us (20%)
  Pallas kernels  18.2 us (19%)
  waiting for transfers between devices  9.92 us (10%)
    all_to_all x2, blocking collectives, all_sum(): return lax.all_to_all(block, both, 0, 0, tiled=True)  46.4 us
    pallas_call x2, Pallas kernels, step(): call(functools.partial(step_kernel, final), outs, [VMEM] * (18 + len(weig...  10.5 us
    ppermute x1, starting transfers between devices, exchange_strips(): lax.ppermute(low, 'gx', back(eastward))  7.35 us
    ppermute x2, starting transfers between devices, exchange(): cols_n = lax.ppermute(to_south, 'gy', back(northward))  5.52 us
    ppermute x2, waiting for transfers between devices, exchange(): cols_s = lax.ppermute(to_north, 'gy', northward)  4.21 us
    ppermute x2, starting transfers between devices, exchange(): rows_e = lax.ppermute(row_low, 'gx', back(eastward))  3.98 us
    pallas_call x1, Pallas kernels, per_device(): call(solve_kernel, [cols, cols, strip, strip] + [field] * 8, [VMEM] * 4 +...  3.88 us
    ppermute x2, waiting for transfers between devices, exchange(): cols_n = lax.ppermute(to_south, 'gy', back(northward))  3.1 us
  transfers between devices with their start and end apart: 10, of which 5 were waited for; matrix products, arithmetic and copies ran while one was open for 0% of the time, Pallas kernels for 5%

profile of v7, /device:TPU:1, one launch (start us, length us, event | category | flops | bytes accessed | tf_op | source)
XLA Modules:
  0.0 94.6 jit_solution(931145872951977250)
XLA Ops:
  0.6 2.4 %combine.1 = (f32[5,8,128]{2,1,0:T(8,128)S(1)}, f32[5,8,128]{2,1,0:T(8,128)S(1)}, f32[2,8,128]{2,1,0:T(8,128)S(1)}, f32[2,8,128]{2,1,0:T(8,128)S(1)}, f32[48,16,...) custom-call(f32[48]{0:T(128)} %mix.1, f32[48]{0:T(128)} %thermal.1, ...), custom_call_target="tpu_custom_call" | custom-call | tf_op jit(solution)/shard_map/combine/pallas_call | solution.py:750
  3.0 3.3 %collective-permute-start = (f32[5,8,128]{2,1,0:T(8,128)S(1)}, f32[5,8,128]{2,1,0:T(8,128)S(1)}, u32[]{:S(2)}, u32[]{:S(2)}) collective-permute-start(f32[5,8,128]{2,1,0:T(8,128)S(1)} %get-tuple-element.52.low), channel_id=1, source_target_pairs={{8,0},{16,8},{24,16},{32,24},{40,32},{48,40},{56,48},{64,56},{72,6... | collective-permute-start | bytes 61448 | tf_op jit(solution)/shard_map/ppermute | solution.py:703
  6.3 0.0 collective-permute-start.1
  6.4 3.9 %solve.1 = (f32[12,8,128]{2,1,0:T(8,128)S(1)}, f32[12,8,128]{2,1,0:T(8,128)S(1)}, f32[84,8,128]{2,1,0:T(8,128)S(1)}, f32[84,8,128]{2,1,0:T(8,128)S(1)}, f32[48,1...) custom-call(f32[48,16,128]{2,1,0:T(8,128)S(1)} %get-tuple-element.42, ...), custom_call_target="tpu_custom_call" | custom-call | tf_op jit(solution)/shard_map/solve/pallas_call | solution.py:768
  10.2 0.0 collective-permute-done.rows_e
  10.2 0.0 collective-permute-done.1.rows_w
  10.3 5.3 %collective-permute-start.2 = (f32[16,8,128]{2,1,0:T(8,128)S(1)}, f32[16,8,128]{2,1,0:T(8,128)S(1)}, u32[]{:S(2)}, u32[]{:S(2)}) collective-permute-start(f32[16,8,128]{2,1,0:T(8,128)S(1)} %get-tuple-element.58), channel_id=1, source_target_pairs={{1,0},{2,1},{3,2},{4,3},{5,4},{6,5},{7,6},{0,7},{9,8},{10,9},{11,1... | collective-permute-start | bytes 196616 | tf_op jit(solution)/shard_map/ppermute | solution.py:714
  15.6 0.0 collective-permute-start.3
  15.6 1.3 %collective-permute-done.2.cols_n.refs_7_.refs_6_ = f32[16,8,128]{2,1,0:T(8,128)S(1)} collective-permute-done((f32[16,8,128]{2,1,0:T(8,128)S(1)}, f32[16,8,128]{2,1,0:T(8,128)S(1)}, u32[]{:S(2)}, u32[]{:S(2)}) %collective-permute-start.2) | collective-permute-done | bytes 65568 | tf_op jit(solution)/shard_map/ppermute | solution.py:714
  17.0 3.0 %collective-permute-done.3.cols_s.refs_8_.refs_7_ = f32[16,8,128]{2,1,0:T(8,128)S(1)} collective-permute-done((f32[16,8,128]{2,1,0:T(8,128)S(1)}, f32[16,8,128]{2,1,0:T(8,128)S(1)}, u32[]{:S(2)}, u32[]{:S(2)}) %collective-permute-start.3) | collective-permute-done | bytes 65568 | tf_op jit(solution)/shard_map/ppermute | solution.py:715
  20.0 7.4 %collective-permute-start.4 = (f32[84,8,128]{2,1,0:T(8,128)S(1)}, f32[84,8,128]{2,1,0:T(8,128)S(1)}, u32[]{:S(2)}, u32[]{:S(2)}) collective-permute-start(f32[84,8,128]{2,1,0:T(8,128)S(1)} %get-tuple-element.65.refs_1_.refs_0_), channel_id=1, source_target_pairs={{8,0},{16,8},{24,16},{32,24},{40,32},{48,40},{56,48},{64,56},{72,6... | collective-permute-start | bytes 1032200 | tf_op jit(solution)/shard_map/ppermute | solution.py:726
  27.3 0.0 collective-permute-start.5
  27.3 0.7 first_surface.1
  28.0 22.0 %all_to_all.22 = f32[256,1,128]{2,1,0:T(1,128)S(1)} all-to-all(f32[256,1,128]{2,1,0:T(1,128)S(1)} %bitcast.10), channel_id=1, replica_groups=mesh['gx'=32,'gy'=8] {'gx','gy'}, dimensions={0} | all-to-all | bytes 262144 | tf_op jit(solution)/shard_map/all_to_all | solution.py:730
  50.0 0.0 collective-permute-done.4.refs_5_.refs_4_
  50.0 0.0 collective-permute-done.5.refs_6_.refs_5_
  50.0 5.7 %first_step.1 = (f32[48,16,128]{2,1,0:T(8,128)S(1)}, f32[48,16,128]{2,1,0:T(8,128)S(1)}, f32[48,16,128]{2,1,0:T(8,128)S(1)}, f32[48,16,128]{2,1,0:T(8,128)S(1)},...) custom-call(f32[48,16,128]{2,1,0:T(8,128)S(1)} %get-tuple-element.46, ...), custom_call_target="tpu_custom_call" | custom-call | tf_op jit(solution)/shard_map/first_step/pallas_call | solution.py:798
  55.7 0.7 collective-permute-start.6
  56.3 1.2 %collective-permute-start.7 = (f32[31,8,128]{2,1,0:T(8,128)S(1)}, f32[31,8,128]{2,1,0:T(8,128)S(1)}, u32[]{:S(2)}, u32[]{:S(2)}) collective-permute-start(f32[31,8,128]{2,1,0:T(8,128)S(1)} %get-tuple-element.72.high.refs_9_), channel_id=1, source_target_pairs={{0,8},{8,16},{16,24},{24,32},{32,40},{40,48},{48,56},{56,64},{64,7... | collective-permute-start | bytes 380936 | tf_op jit(solution)/shard_map/ppermute | solution.py:704
  57.5 2.6 %collective-permute-done.6.rows_e.refs_12_ = f32[31,8,128]{2,1,0:T(8,128)S(1)} collective-permute-done((f32[31,8,128]{2,1,0:T(8,128)S(1)}, f32[31,8,128]{2,1,0:T(8,128)S(1)}, u32[]{:S(2)}, u32[]{:S(2)}) %collective-permute-start.6) | collective-permute-done | bytes 127008 | tf_op jit(solution)/shard_map/ppermute | solution.py:703
  60.1 0.0 collective-permute-done.7.rows_w.refs_13_
  60.1 0.2 collective-permute-start.8
  60.3 1.4 %collective-permute-start.9 = (f32[12,8,128]{2,1,0:T(8,128)S(1)}, f32[12,8,128]{2,1,0:T(8,128)S(1)}, u32[]{:S(2)}, u32[]{:S(2)}) collective-permute-start(f32[12,8,128]{2,1,0:T(8,128)S(1)} %get-tuple-element.76), channel_id=1, source_target_pairs={{0,1},{1,2},{2,3},{3,4},{4,5},{5,6},{6,7},{7,0},{8,9},{9,10},{10,1... | collective-permute-start | bytes 147464 | tf_op jit(solution)/shard_map/ppermute | solution.py:715
  61.7 1.8 %collective-permute-done.8.cols_n.refs_14_ = f32[12,8,128]{2,1,0:T(8,128)S(1)} collective-permute-done((f32[12,8,128]{2,1,0:T(8,128)S(1)}, f32[12,8,128]{2,1,0:T(8,128)S(1)}, u32[]{:S(2)}, u32[]{:S(2)}) %collective-permute-start.8) | collective-permute-done | bytes 49184 | tf_op jit(solution)/shard_map/ppermute | solution.py:714
  63.4 1.2 %collective-permute-done.9.cols_s.refs_15_ = f32[12,8,128]{2,1,0:T(8,128)S(1)} collective-permute-done((f32[12,8,128]{2,1,0:T(8,128)S(1)}, f32[12,8,128]{2,1,0:T(8,128)S(1)}, u32[]{:S(2)}, u32[]{:S(2)}) %collective-permute-start.9) | collective-permute-done | bytes 49184 | tf_op jit(solution)/shard_map/ppermute | solution.py:715
  64.6 0.7 next_surface.1
  65.3 24.5 %all_to_all.23 = f32[256,1,128]{2,1,0:T(1,128)S(1)} all-to-all(f32[256,1,128]{2,1,0:T(1,128)S(1)} %bitcast.11), channel_id=1, replica_groups=mesh['gx'=32,'gy'=8] {'gx','gy'}, dimensions={0} | all-to-all | bytes 262144 | tf_op jit(solution)/shard_map/all_to_all | solution.py:730
  89.8 4.8 %last_step.1 = (f32[48,16,128]{2,1,0:T(8,128)}, f32[48,16,128]{2,1,0:T(8,128)}, f32[16,128]{1,0:T(8,128)}) custom-call(f32[48,16,128]{2,1,0:T(8,128)S(1)} %get-tuple-element.69.temp, f32[48,16,128]{2,1,0:T(8,128)S(1)} %get-tuple-element.70.salt, f32[48,16,128]{2,1,0:T(8,128)S(1)} %get-tuple-element.48.temp_response, ...), custom_call_target="tpu_custom_call" | custom-call | tf_op jit(solution)/shard_map/last_step/pallas_call | solution.py:798
  (3 shorter events, 0.1 us)
Async XLA Ops:
  3.0 7.2 %collective-permute-start = (f32[5,8,128]{2,1,0:T(8,128)S(1)}, f32[5,8,128]{2,1,0:T(8,128)S(1)}, u32[]{:S(2)}, u32[]{:S(2)}) collective-permute-start(f32[5,8,128]{2,1,0:T(8,128)S(1)} %get-tuple-element.52.low), channel_id=1, source_target_pairs={{8,0},{16,8},{24,16},{32,24},{40,32},{48,40},{56,48},{64,56},{72,6... | collective-permute-start | bytes 61448 | tf_op jit(solution)/shard_map/ppermute | solution.py:703
  6.3 3.9 %collective-permute-start.1 = (f32[5,8,128]{2,1,0:T(8,128)S(1)}, f32[5,8,128]{2,1,0:T(8,128)S(1)}, u32[]{:S(2)}, u32[]{:S(2)}) collective-permute-start(f32[5,8,128]{2,1,0:T(8,128)S(1)} %get-tuple-element.53.high), channel_id=1, source_target_pairs={{0,8},{8,16},{16,24},{24,32},{32,40},{40,48},{48,56},{56,64},{64,7... | collective-permute-start | bytes 61448 | tf_op jit(solution)/shard_map/ppermute | solution.py:704
  10.3 6.7 %collective-permute-start.2 = (f32[16,8,128]{2,1,0:T(8,128)S(1)}, f32[16,8,128]{2,1,0:T(8,128)S(1)}, u32[]{:S(2)}, u32[]{:S(2)}) collective-permute-start(f32[16,8,128]{2,1,0:T(8,128)S(1)} %get-tuple-element.58), channel_id=1, source_target_pairs={{1,0},{2,1},{3,2},{4,3},{5,4},{6,5},{7,6},{0,7},{9,8},{10,9},{11,1... | collective-permute-start | bytes 196616 | tf_op jit(solution)/shard_map/ppermute | solution.py:714
  15.6 4.3 %collective-permute-start.3 = (f32[16,8,128]{2,1,0:T(8,128)S(1)}, f32[16,8,128]{2,1,0:T(8,128)S(1)}, u32[]{:S(2)}, u32[]{:S(2)}) collective-permute-start(f32[16,8,128]{2,1,0:T(8,128)S(1)} %get-tuple-element.59), channel_id=1, source_target_pairs={{0,1},{1,2},{2,3},{3,4},{4,5},{5,6},{6,7},{7,0},{8,9},{9,10},{10,1... | collective-permute-start | bytes 196616 | tf_op jit(solution)/shard_map/ppermute | solution.py:715
  20.0 30.0 %collective-permute-start.4 = (f32[84,8,128]{2,1,0:T(8,128)S(1)}, f32[84,8,128]{2,1,0:T(8,128)S(1)}, u32[]{:S(2)}, u32[]{:S(2)}) collective-permute-start(f32[84,8,128]{2,1,0:T(8,128)S(1)} %get-tuple-element.65.refs_1_.refs_0_), channel_id=1, source_target_pairs={{8,0},{16,8},{24,16},{32,24},{40,32},{48,40},{56,48},{64,56},{72,6... | collective-permute-start | bytes 1032200 | tf_op jit(solution)/shard_map/ppermute | solution.py:726
  27.3 22.7 %collective-permute-start.5 = (f32[84,8,128]{2,1,0:T(8,128)S(1)}, f32[84,8,128]{2,1,0:T(8,128)S(1)}, u32[]{:S(2)}, u32[]{:S(2)}) collective-permute-start(f32[84,8,128]{2,1,0:T(8,128)S(1)} %get-tuple-element.66.refs_2_.refs_1_), channel_id=1, source_target_pairs={{0,8},{8,16},{16,24},{24,32},{32,40},{40,48},{48,56},{56,64},{64,7... | collective-permute-start | bytes 1032200 | tf_op jit(solution)/shard_map/ppermute | solution.py:726
  55.7 4.4 %collective-permute-start.6 = (f32[31,8,128]{2,1,0:T(8,128)S(1)}, f32[31,8,128]{2,1,0:T(8,128)S(1)}, u32[]{:S(2)}, u32[]{:S(2)}) collective-permute-start(f32[31,8,128]{2,1,0:T(8,128)S(1)} %get-tuple-element.71.low.refs_8_), channel_id=1, source_target_pairs={{8,0},{16,8},{24,16},{32,24},{40,32},{48,40},{56,48},{64,56},{72,6... | collective-permute-start | bytes 380936 | tf_op jit(solution)/shard_map/ppermute | solution.py:703
  56.3 3.8 %collective-permute-start.7 = (f32[31,8,128]{2,1,0:T(8,128)S(1)}, f32[31,8,128]{2,1,0:T(8,128)S(1)}, u32[]{:S(2)}, u32[]{:S(2)}) collective-permute-start(f32[31,8,128]{2,1,0:T(8,128)S(1)} %get-tuple-element.72.high.refs_9_), channel_id=1, source_target_pairs={{0,8},{8,16},{16,24},{24,32},{32,40},{40,48},{48,56},{56,64},{64,7... | collective-permute-start | bytes 380936 | tf_op jit(solution)/shard_map/ppermute | solution.py:704
  60.1 3.3 %collective-permute-start.8 = (f32[12,8,128]{2,1,0:T(8,128)S(1)}, f32[12,8,128]{2,1,0:T(8,128)S(1)}, u32[]{:S(2)}, u32[]{:S(2)}) collective-permute-start(f32[12,8,128]{2,1,0:T(8,128)S(1)} %get-tuple-element.75), channel_id=1, source_target_pairs={{1,0},{2,1},{3,2},{4,3},{5,4},{6,5},{7,6},{0,7},{9,8},{10,9},{11,1... | collective-permute-start | bytes 147464 | tf_op jit(solution)/shard_map/ppermute | solution.py:714
  60.3 4.3 %collective-permute-start.9 = (f32[12,8,128]{2,1,0:T(8,128)S(1)}, f32[12,8,128]{2,1,0:T(8,128)S(1)}, u32[]{:S(2)}, u32[]{:S(2)}) collective-permute-start(f32[12,8,128]{2,1,0:T(8,128)S(1)} %get-tuple-element.76), channel_id=1, source_target_pairs={{0,1},{1,2},{2,3},{3,4},{4,5},{5,6},{6,7},{7,0},{8,9},{9,10},{10,1... | collective-permute-start | bytes 147464 | tf_op jit(solution)/shard_map/ppermute | solution.py:715

commit v8 on v7

--- a/solution.py
+++ b/solution.py
@@ -186,7 +186,7 @@
     for part in range(parts):
         for n in range(3):
             copy(n, part).wait()
-        carry = lax.fori_loop(part * step, (part + 1) * step, body, carry)
+        carry = lax.fori_loop(part * step, (part + 1) * step, body, carry, unroll=True)
     total, depth = carry
     refs = row_low, row_high, col_low, col_high
     put_surface(refs, A_SURFACE, (surface[...] + total, depth / LEVELS, diag[...]))
@@ -273,7 +273,7 @@
         return values, packs
 
     n = len(places)
-    _, packs = lax.fori_loop(0, GROUPS, up_body, ((zero,) * n, ((zero, zero),) * n))
+    _, packs = lax.fori_loop(0, GROUPS, up_body, ((zero,) * n, ((zero, zero),) * n), unroll=2)
     for (_, block), acc in zip(places, packs):
         put_cols(refs, block, *acc)
 

time: 94.8 us -> 94.3 us (level)
  transfers between devices with their start and end apart: 10 -> 10, of which waited for: 5 -> 6; matrix products, arithmetic and copies ran while one was open for 0% -> 0% of each run, Pallas kernels for 5% -> 4%
where the time goes in v8:
time: 94.3 us; the launch traced here: 94 us
  blocking collectives  46.2 us (49%)
  starting transfers between devices  19.7 us (21%)
  Pallas kernels  17.3 us (18%)
  waiting for transfers between devices  10.1 us (11%)
    all_to_all x2, blocking collectives, all_sum(): return lax.all_to_all(block, both, 0, 0, tiled=True)  46.2 us
    pallas_call x2, Pallas kernels, step(): call(functools.partial(step_kernel, final), outs, [VMEM] * (18 + len(weig...  10 us
    ppermute x1, starting transfers between devices, exchange_strips(): lax.ppermute(low, 'gx', back(eastward))  7.35 us
    ppermute x2, starting transfers between devices, exchange(): cols_n = lax.ppermute(to_south, 'gy', back(northward))  5.84 us
    ppermute x2, waiting for transfers between devices, exchange(): cols_s = lax.ppermute(to_north, 'gy', northward)  4.21 us
    ppermute x2, starting transfers between devices, exchange(): rows_e = lax.ppermute(row_low, 'gx', back(eastward))  3.98 us
    pallas_call x1, Pallas kernels, per_device(): call(solve_kernel, [cols, cols, strip, strip] + [field] * 8, [VMEM] * 4 +...  3.44 us
    ppermute x2, waiting for transfers between devices, exchange(): cols_n = lax.ppermute(to_south, 'gy', back(northward))  3.1 us
  transfers between devices with their start and end apart: 10, of which 6 were waited for; matrix products, arithmetic and copies ran while one was open for 0% of the time, Pallas kernels for 4%

profile of v8, /device:TPU:1, one launch (start us, length us, event | category | flops | bytes accessed | tf_op | source)
XLA Modules:
  0.0 94.0 jit_solution(7196615807215985061)
XLA Ops:
  0.6 2.4 %combine.1 = (f32[5,8,128]{2,1,0:T(8,128)S(1)}, f32[5,8,128]{2,1,0:T(8,128)S(1)}, f32[2,8,128]{2,1,0:T(8,128)S(1)}, f32[2,8,128]{2,1,0:T(8,128)S(1)}, f32[48,16,...) custom-call(f32[48]{0:T(128)} %mix.1, f32[48]{0:T(128)} %thermal.1, ...), custom_call_target="tpu_custom_call" | custom-call | tf_op jit(solution)/shard_map/combine/pallas_call | solution.py:750
  3.0 3.3 %collective-permute-start = (f32[5,8,128]{2,1,0:T(8,128)S(1)}, f32[5,8,128]{2,1,0:T(8,128)S(1)}, u32[]{:S(2)}, u32[]{:S(2)}) collective-permute-start(f32[5,8,128]{2,1,0:T(8,128)S(1)} %get-tuple-element.52.low), channel_id=1, source_target_pairs={{8,0},{16,8},{24,16},{32,24},{40,32},{48,40},{56,48},{64,56},{72,6... | collective-permute-start | bytes 61448 | tf_op jit(solution)/shard_map/ppermute | solution.py:703
  6.3 0.0 collective-permute-start.1
  6.3 3.4 %solve.1 = (f32[12,8,128]{2,1,0:T(8,128)S(1)}, f32[12,8,128]{2,1,0:T(8,128)S(1)}, f32[84,8,128]{2,1,0:T(8,128)S(1)}, f32[84,8,128]{2,1,0:T(8,128)S(1)}, f32[48,1...) custom-call(f32[48,16,128]{2,1,0:T(8,128)S(1)} %get-tuple-element.42, ...), custom_call_target="tpu_custom_call" | custom-call | tf_op jit(solution)/shard_map/solve/pallas_call | solution.py:768
  9.8 0.0 collective-permute-done.rows_e
  9.8 0.1 collective-permute-done.1.rows_w
  9.9 5.7 %collective-permute-start.2 = (f32[16,8,128]{2,1,0:T(8,128)S(1)}, f32[16,8,128]{2,1,0:T(8,128)S(1)}, u32[]{:S(2)}, u32[]{:S(2)}) collective-permute-start(f32[16,8,128]{2,1,0:T(8,128)S(1)} %get-tuple-element.58), channel_id=1, source_target_pairs={{1,0},{2,1},{3,2},{4,3},{5,4},{6,5},{7,6},{0,7},{9,8},{10,9},{11,1... | collective-permute-start | bytes 196616 | tf_op jit(solution)/shard_map/ppermute | solution.py:714
  15.6 0.0 collective-permute-start.3
  15.6 1.3 %collective-permute-done.2.cols_n.refs_7_.refs_6_ = f32[16,8,128]{2,1,0:T(8,128)S(1)} collective-permute-done((f32[16,8,128]{2,1,0:T(8,128)S(1)}, f32[16,8,128]{2,1,0:T(8,128)S(1)}, u32[]{:S(2)}, u32[]{:S(2)}) %collective-permute-start.2) | collective-permute-done | bytes 65568 | tf_op jit(solution)/shard_map/ppermute | solution.py:714
  16.9 3.0 %collective-permute-done.3.cols_s.refs_8_.refs_7_ = f32[16,8,128]{2,1,0:T(8,128)S(1)} collective-permute-done((f32[16,8,128]{2,1,0:T(8,128)S(1)}, f32[16,8,128]{2,1,0:T(8,128)S(1)}, u32[]{:S(2)}, u32[]{:S(2)}) %collective-permute-start.3) | collective-permute-done | bytes 65568 | tf_op jit(solution)/shard_map/ppermute | solution.py:715
  19.9 7.4 %collective-permute-start.4 = (f32[84,8,128]{2,1,0:T(8,128)S(1)}, f32[84,8,128]{2,1,0:T(8,128)S(1)}, u32[]{:S(2)}, u32[]{:S(2)}) collective-permute-start(f32[84,8,128]{2,1,0:T(8,128)S(1)} %get-tuple-element.65.refs_1_.refs_0_), channel_id=1, source_target_pairs={{8,0},{16,8},{24,16},{32,24},{40,32},{48,40},{56,48},{64,56},{72,6... | collective-permute-start | bytes 1032200 | tf_op jit(solution)/shard_map/ppermute | solution.py:726
  27.3 0.0 collective-permute-start.5
  27.3 0.7 first_surface.1
  28.0 21.5 %all_to_all.22 = f32[256,1,128]{2,1,0:T(1,128)S(1)} all-to-all(f32[256,1,128]{2,1,0:T(1,128)S(1)} %bitcast.10), channel_id=1, replica_groups=mesh['gx'=32,'gy'=8] {'gx','gy'}, dimensions={0} | all-to-all | bytes 262144 | tf_op jit(solution)/shard_map/all_to_all | solution.py:730
  49.5 0.0 collective-permute-done.4.refs_5_.refs_4_
  49.5 0.0 collective-permute-done.5.refs_6_.refs_5_
  49.5 5.3 %first_step.1 = (f32[48,16,128]{2,1,0:T(8,128)S(1)}, f32[48,16,128]{2,1,0:T(8,128)S(1)}, f32[48,16,128]{2,1,0:T(8,128)S(1)}, f32[48,16,128]{2,1,0:T(8,128)S(1)},...) custom-call(f32[48,16,128]{2,1,0:T(8,128)S(1)} %get-tuple-element.46, ...), custom_call_target="tpu_custom_call" | custom-call | tf_op jit(solution)/shard_map/first_step/pallas_call | solution.py:798
  54.8 0.7 collective-permute-start.6
  55.4 1.2 %collective-permute-start.7 = (f32[31,8,128]{2,1,0:T(8,128)S(1)}, f32[31,8,128]{2,1,0:T(8,128)S(1)}, u32[]{:S(2)}, u32[]{:S(2)}) collective-permute-start(f32[31,8,128]{2,1,0:T(8,128)S(1)} %get-tuple-element.72.high.refs_9_), channel_id=1, source_target_pairs={{0,8},{8,16},{16,24},{24,32},{32,40},{40,48},{48,56},{56,64},{64,7... | collective-permute-start | bytes 380936 | tf_op jit(solution)/shard_map/ppermute | solution.py:704
  56.6 2.6 %collective-permute-done.6.rows_e.refs_12_ = f32[31,8,128]{2,1,0:T(8,128)S(1)} collective-permute-done((f32[31,8,128]{2,1,0:T(8,128)S(1)}, f32[31,8,128]{2,1,0:T(8,128)S(1)}, u32[]{:S(2)}, u32[]{:S(2)}) %collective-permute-start.6) | collective-permute-done | bytes 127008 | tf_op jit(solution)/shard_map/ppermute | solution.py:703
  59.2 0.0 collective-permute-done.7.rows_w.refs_13_
  59.2 0.2 collective-permute-start.8
  59.4 1.4 %collective-permute-start.9 = (f32[12,8,128]{2,1,0:T(8,128)S(1)}, f32[12,8,128]{2,1,0:T(8,128)S(1)}, u32[]{:S(2)}, u32[]{:S(2)}) collective-permute-start(f32[12,8,128]{2,1,0:T(8,128)S(1)} %get-tuple-element.76), channel_id=1, source_target_pairs={{0,1},{1,2},{2,3},{3,4},{4,5},{5,6},{6,7},{7,0},{8,9},{9,10},{10,1... | collective-permute-start | bytes 147464 | tf_op jit(solution)/shard_map/ppermute | solution.py:715
  60.8 1.8 %collective-permute-done.8.cols_n.refs_14_ = f32[12,8,128]{2,1,0:T(8,128)S(1)} collective-permute-done((f32[12,8,128]{2,1,0:T(8,128)S(1)}, f32[12,8,128]{2,1,0:T(8,128)S(1)}, u32[]{:S(2)}, u32[]{:S(2)}) %collective-permute-start.8) | collective-permute-done | bytes 49184 | tf_op jit(solution)/shard_map/ppermute | solution.py:714
  62.5 1.2 %collective-permute-done.9.cols_s.refs_15_ = f32[12,8,128]{2,1,0:T(8,128)S(1)} collective-permute-done((f32[12,8,128]{2,1,0:T(8,128)S(1)}, f32[12,8,128]{2,1,0:T(8,128)S(1)}, u32[]{:S(2)}, u32[]{:S(2)}) %collective-permute-start.9) | collective-permute-done | bytes 49184 | tf_op jit(solution)/shard_map/ppermute | solution.py:715
  63.7 0.7 next_surface.1
  64.4 24.7 %all_to_all.23 = f32[256,1,128]{2,1,0:T(1,128)S(1)} all-to-all(f32[256,1,128]{2,1,0:T(1,128)S(1)} %bitcast.11), channel_id=1, replica_groups=mesh['gx'=32,'gy'=8] {'gx','gy'}, dimensions={0} | all-to-all | bytes 262144 | tf_op jit(solution)/shard_map/all_to_all | solution.py:730
  89.1 4.8 %last_step.1 = (f32[48,16,128]{2,1,0:T(8,128)}, f32[48,16,128]{2,1,0:T(8,128)}, f32[16,128]{1,0:T(8,128)}) custom-call(f32[48,16,128]{2,1,0:T(8,128)S(1)} %get-tuple-element.69.temp, f32[48,16,128]{2,1,0:T(8,128)S(1)} %get-tuple-element.70.salt, f32[48,16,128]{2,1,0:T(8,128)S(1)} %get-tuple-element.48.temp_response, ...), custom_call_target="tpu_custom_call" | custom-call | tf_op jit(solution)/shard_map/last_step/pallas_call | solution.py:798
  (3 shorter events, 0.0 us)
Async XLA Ops:
  3.0 6.8 %collective-permute-start = (f32[5,8,128]{2,1,0:T(8,128)S(1)}, f32[5,8,128]{2,1,0:T(8,128)S(1)}, u32[]{:S(2)}, u32[]{:S(2)}) collective-permute-start(f32[5,8,128]{2,1,0:T(8,128)S(1)} %get-tuple-element.52.low), channel_id=1, source_target_pairs={{8,0},{16,8},{24,16},{32,24},{40,32},{48,40},{56,48},{64,56},{72,6... | collective-permute-start | bytes 61448 | tf_op jit(solution)/shard_map/ppermute | solution.py:703
  6.3 3.6 %collective-permute-start.1 = (f32[5,8,128]{2,1,0:T(8,128)S(1)}, f32[5,8,128]{2,1,0:T(8,128)S(1)}, u32[]{:S(2)}, u32[]{:S(2)}) collective-permute-start(f32[5,8,128]{2,1,0:T(8,128)S(1)} %get-tuple-element.53.high), channel_id=1, source_target_pairs={{0,8},{8,16},{16,24},{24,32},{32,40},{40,48},{48,56},{56,64},{64,7... | collective-permute-start | bytes 61448 | tf_op jit(solution)/shard_map/ppermute | solution.py:704
  9.9 7.0 %collective-permute-start.2 = (f32[16,8,128]{2,1,0:T(8,128)S(1)}, f32[16,8,128]{2,1,0:T(8,128)S(1)}, u32[]{:S(2)}, u32[]{:S(2)}) collective-permute-start(f32[16,8,128]{2,1,0:T(8,128)S(1)} %get-tuple-element.58), channel_id=1, source_target_pairs={{1,0},{2,1},{3,2},{4,3},{5,4},{6,5},{7,6},{0,7},{9,8},{10,9},{11,1... | collective-permute-start | bytes 196616 | tf_op jit(solution)/shard_map/ppermute | solution.py:714
  15.6 4.3 %collective-permute-start.3 = (f32[16,8,128]{2,1,0:T(8,128)S(1)}, f32[16,8,128]{2,1,0:T(8,128)S(1)}, u32[]{:S(2)}, u32[]{:S(2)}) collective-permute-start(f32[16,8,128]{2,1,0:T(8,128)S(1)} %get-tuple-element.59), channel_id=1, source_target_pairs={{0,1},{1,2},{2,3},{3,4},{4,5},{5,6},{6,7},{7,0},{8,9},{9,10},{10,1... | collective-permute-start | bytes 196616 | tf_op jit(solution)/shard_map/ppermute | solution.py:715
  19.9 29.6 %collective-permute-start.4 = (f32[84,8,128]{2,1,0:T(8,128)S(1)}, f32[84,8,128]{2,1,0:T(8,128)S(1)}, u32[]{:S(2)}, u32[]{:S(2)}) collective-permute-start(f32[84,8,128]{2,1,0:T(8,128)S(1)} %get-tuple-element.65.refs_1_.refs_0_), channel_id=1, source_target_pairs={{8,0},{16,8},{24,16},{32,24},{40,32},{48,40},{56,48},{64,56},{72,6... | collective-permute-start | bytes 1032200 | tf_op jit(solution)/shard_map/ppermute | solution.py:726
  27.3 22.2 %collective-permute-start.5 = (f32[84,8,128]{2,1,0:T(8,128)S(1)}, f32[84,8,128]{2,1,0:T(8,128)S(1)}, u32[]{:S(2)}, u32[]{:S(2)}) collective-permute-start(f32[84,8,128]{2,1,0:T(8,128)S(1)} %get-tuple-element.66.refs_2_.refs_1_), channel_id=1, source_target_pairs={{0,8},{8,16},{16,24},{24,32},{32,40},{40,48},{48,56},{56,64},{64,7... | collective-permute-start | bytes 1032200 | tf_op jit(solution)/shard_map/ppermute | solution.py:726
  54.8 4.4 %collective-permute-start.6 = (f32[31,8,128]{2,1,0:T(8,128)S(1)}, f32[31,8,128]{2,1,0:T(8,128)S(1)}, u32[]{:S(2)}, u32[]{:S(2)}) collective-permute-start(f32[31,8,128]{2,1,0:T(8,128)S(1)} %get-tuple-element.71.low.refs_8_), channel_id=1, source_target_pairs={{8,0},{16,8},{24,16},{32,24},{40,32},{48,40},{56,48},{64,56},{72,6... | collective-permute-start | bytes 380936 | tf_op jit(solution)/shard_map/ppermute | solution.py:703
  55.4 3.8 %collective-permute-start.7 = (f32[31,8,128]{2,1,0:T(8,128)S(1)}, f32[31,8,128]{2,1,0:T(8,128)S(1)}, u32[]{:S(2)}, u32[]{:S(2)}) collective-permute-start(f32[31,8,128]{2,1,0:T(8,128)S(1)} %get-tuple-element.72.high.refs_9_), channel_id=1, source_target_pairs={{0,8},{8,16},{16,24},{24,32},{32,40},{40,48},{48,56},{56,64},{64,7... | collective-permute-start | bytes 380936 | tf_op jit(solution)/shard_map/ppermute | solution.py:704
  59.2 3.3 %collective-permute-start.8 = (f32[12,8,128]{2,1,0:T(8,128)S(1)}, f32[12,8,128]{2,1,0:T(8,128)S(1)}, u32[]{:S(2)}, u32[]{:S(2)}) collective-permute-start(f32[12,8,128]{2,1,0:T(8,128)S(1)} %get-tuple-element.75), channel_id=1, source_target_pairs={{1,0},{2,1},{3,2},{4,3},{5,4},{6,5},{7,6},{0,7},{9,8},{10,9},{11,1... | collective-permute-start | bytes 147464 | tf_op jit(solution)/shard_map/ppermute | solution.py:714
  59.4 4.3 %collective-permute-start.9 = (f32[12,8,128]{2,1,0:T(8,128)S(1)}, f32[12,8,128]{2,1,0:T(8,128)S(1)}, u32[]{:S(2)}, u32[]{:S(2)}) collective-permute-start(f32[12,8,128]{2,1,0:T(8,128)S(1)} %get-tuple-element.76), channel_id=1, source_target_pairs={{0,1},{1,2},{2,3},{3,4},{4,5},{5,6},{6,7},{7,0},{8,9},{9,10},{10,1... | collective-permute-start | bytes 147464 | tf_op jit(solution)/shard_map/ppermute | solution.py:715
